TPU v7x, 1024 devices: a whole 4x8x16 slice. The times are simulated.
1024 devices in a mesh: node: 64 (over y, z_hi, x), local: 16 (over z_lo, core).
Axes of the slice: x: 4, y: 8, z: 16 (z_hi: 2, z_lo: 8; z = z_hi * 8 + z_lo), core: 2. Of those that a mesh axis runs over, the one named last changes fastest.
Arguments:
- activations: bfloat16 [131072, 4096], P(('node', 'local')), may hold values from -24 to 24
- codes: bfloat16 [16, 256, 128], P('local'), may hold values from -127 to 127, as said below
- scales: float32 [16, 128], P('local'), may hold values from 5e-05 to 0.0005
- cotangent: bfloat16 [131072, 128], P(('node', 'local')), may hold values from -6 to 6
Outputs:
- values_out: bfloat16 [131072, 128], P(('node', 'local'))
- weight_grad: float32 [4096, 128], P(('node', 'local'))
Inputs may be any that keep to these rules, and one draw needn't show every extreme that they name: codes are whole numbers.
All inputs are finite; a program needn't handle non-finite values.
Results may differ from a plain program's by a relative error of at most 0.0048.
Values may be sent and summed in bfloat16 or wider, within the bound.
No kernel may reach another device: no remote copies, remote signals or barrier semaphores. Data moves between devices by JAX's collectives and lax.ppermute only.
A program may use at most 32 MiB of HBM per device.

v0:
```python
import jax
import jax.numpy as jnp
from jax import lax
from jax.sharding import PartitionSpec as P


def on_device(activations, codes, scales, cotangent):
    head_width = codes.shape[2]
    stored = (
        (codes.astype(jnp.float32) * scales[:, None, :])
        .astype(jnp.bfloat16)
        .reshape(-1, head_width)
    )
    projected = jnp.dot(
        activations,
        lax.all_gather(stored, "local", axis=0, tiled=True),
        preferred_element_type=jnp.float32,
    )
    values_out = projected.astype(jnp.bfloat16)
    node_count = lax.axis_size("node")
    local_count = lax.axis_size("local")
    token_total = activations.shape[0] * node_count * local_count
    term = lax.dot_general(
        activations, cotangent, (((0,), (0,)), ((), ())), preferred_element_type=jnp.float32
    )
    term = term * float(token_total) ** (-0.5)
    width = term.shape[0]
    share = width // (node_count * local_count)
    shaped = term.reshape(node_count, local_count, share, head_width)
    partial_value = lax.psum_scatter(shaped, "local", scatter_dimension=1, tiled=True)
    finished = lax.psum_scatter(partial_value, "node", scatter_dimension=0, tiled=True)
    weight_grad = finished.reshape(share, head_width)
    return (values_out, weight_grad)


def solution(mesh):
    in_specs = (
        P(("node", "local"), None),
        P("local", None, None),
        P("local", None),
        P(("node", "local"), None),
    )
    out_specs = (P(("node", "local"), None), P(("node", "local"), None))
    return jax.shard_map(
        on_device, mesh=mesh, in_specs=in_specs, out_specs=out_specs, check_vma=False
    )
```

profile of v0, /device:TPU:1, one launch (start us, length us, event | category | flops | bytes accessed | tf_op | source)
XLA Modules:
  0.0 1281.0 jit_solution(290999029047898145)
XLA Ops:
  7.2 0.0 copy-start
  7.2 0.0 reduce-scatter.2.cloned.1.call-start
  7.2 1.2 copy-done
  8.4 1.2 convolution_multiply_fusion
  9.6 2.6 copy.7
  12.2 0.0 copy-start.1
  12.2 0.0 copy-start.2
  12.2 0.0 reduce-scatter.2.cloned.1.call-update
  12.2 0.0 all-gather.3.cloned.1.call-start
  12.3 0.8 copy-done.1
  13.0 0.0 copy-done.2
  13.0 0.6 multiply_convert_fusion
  13.7 0.0 all-gather.3.cloned.1.call-update
  13.7 0.0 all-reduce.3.cloned.1.call-start
  13.8 1.3 dynamic-slice
  15.1 111.7 %reduce-scatter.2.cloned.1.call-done = f32[64,1,4,128]{3,0,2,1:T(8,128)} async-done(((f32[64,16,4,128]{3,0,2,1:T(8,128)}), f32[64,1,4,128]{3,0,2,1:T(8,128)}) %reduce-scatter.2.cloned.1.call-update) | async-done | bytes 131088 | tf_op jit(solution)/shard_map/reduce_scatter | solution.py:30
  126.8 1.6 copy.8
  128.5 0.0 all-reduce.3.cloned.1.call-update
  128.5 104.0 %all-gather.3.cloned.1.call-done = bf16[1,4096,128]{2,1,0:T(8,128)(2,1)} async-done(((bf16[1,256,128]{2,1,0:T(8,128)(2,1)}), bf16[1,4096,128]{2,1,0:T(8,128)(2,1)}) %all-gather.3.cloned.1.call-update) | async-done | bytes 1048592 | tf_op jit(solution)/shard_map/all_gather | solution.py:16
  232.5 1.7 fusion
  234.2 0.7 copy.9
  234.9 1037.6 %all-reduce.3.cloned.1.call-done = f32[64,1,4,128]{3,2,1,0:T(4,128)} async-done(((f32[64,1,4,128]{3,2,1,0:T(4,128)}), f32[64,1,4,128]{3,2,1,0:T(4,128)}) %all-reduce.3.cloned.1.call-update) | async-done | bytes 131088
  1272.5 1.9 dynamic-slice_bitcast_fusion
Async XLA Ops:
  7.2 1.2 copy-start
  7.2 119.6 %reduce-scatter.2.cloned.1.call-start = ((), (), s32[]{:S(2)}) async-start(), calls=%async_computation.1 | async-start | bytes 2228224 | tf_op jit(solution)/shard_map/reduce_scatter | solution.py:30
  12.2 0.8 copy-start.1
  12.2 0.8 copy-start.2
  12.2 220.3 %all-gather.3.cloned.1.call-start = ((), (), s32[]{:S(2)}) async-start(), calls=%async_computation.2 | async-start | bytes 1114112 | tf_op jit(solution)/shard_map/all_gather | solution.py:16
  13.7 1258.8 %all-reduce.3.cloned.1.call-start = ((), (), s32[]{:S(2)}) async-start(), calls=%async_computation.3 | async-start | bytes 262144
Sparse Core Ops, SparseCore 0:
  12.4 114.4 reduce-scatter.1
  129.5 102.9 all-gather.2
  236.0 1036.4 all-reduce.2
where the time goes:
time: 1300 us; the launch traced here: 1280 us
  waiting for transfers between devices  1250 us (96%)
  between operations  13.8 us (1%)
    unnamed x4, waiting for transfers between devices  1040 us
    reduce_scatter x1, waiting for transfers between devices, on_device(): lax.psum_scatter(shaped, 'local', scatter_dimension=1, tiled=True)  112 us
    all_gather x1, waiting for transfers between devices, on_device(): lax.all_gather(stored, 'local', axis=0, tiled=True)  104 us
  transfers between devices with their start and end apart: 3, of which 3 were waited for; matrix products, arithmetic and copies ran while one was open for 0% of the time, Pallas kernels for 0%

commit v1 on v0

v1 whole, which is shorter than its diff:
```python
import jax
import jax.numpy as jnp
from jax import lax
from jax.experimental import pallas as pl
from jax.experimental.pallas import tpu as pltpu
from jax.sharding import Mesh, PartitionSpec as P

Y, ZH, X, ZL, CORE = 8, 2, 4, 8, 2
AXES = ("y", "zh", "x", "zl", "core")


def term_kernel(scale, core_ref, act_ref, cot_ref, keep_ref, send_ref):
    first = core_ref[0] == 0
    share = 4
    per = act_ref.shape[1] // (Y * ZH)
    sub = per // X
    half = sub // 2
    cot = cot_ref[...]
    low = lax.broadcasted_iota(jnp.int32, (sub // 16, 8, cot.shape[1]), 1) < share
    for outer in range(Y * ZH):
        part = lax.dot_general(
            act_ref[:, outer * per : (outer + 1) * per],
            cot,
            (((0,), (0,)), ((), ())),
            preferred_element_type=jnp.float32,
        )
        part = part * scale
        for x in range(X):
            tiles = part[x * sub : (x + 1) * sub].reshape(sub // 16, 2, 8, cot.shape[1])
            even, odd = tiles[:, 0], tiles[:, 1]
            zero = jnp.where(low, even, pltpu.roll(odd, share, 1))
            one = jnp.where(low, pltpu.roll(even, share, 1), odd)
            at = pl.ds((x * Y * ZH + outer) * half, half)
            keep_ref[at, :] = jnp.where(first, zero, one).reshape(half, -1)
            send_ref[at, :] = jnp.where(first, one, zero).reshape(half, -1)


def project_kernel(core_ref, act_ref, own_ref, other_ref, out_ref):
    core = core_ref[0]
    block = own_ref.shape[1]
    total = None
    for zl in range(ZL):
        for ref, which in ((own_ref, core), (other_ref, 1 - core)):
            at = pl.multiple_of((2 * zl + which) * block, block)
            piece = jnp.dot(
                act_ref[:, pl.ds(at, block)], ref[zl], preferred_element_type=jnp.float32
            )
            total = piece if total is None else total + piece
    out_ref[...] = total.astype(out_ref.dtype)


def on_device(activations, codes, scales, cotangent):
    width = activations.shape[1]
    head = cotangent.shape[1]
    tokens = activations.shape[0] * Y * ZH * X * ZL * CORE
    vmem = pl.BlockSpec(memory_space=pltpu.VMEM)
    smem = pl.BlockSpec(memory_space=pltpu.SMEM)
    params = pltpu.CompilerParams(vmem_limit_bytes=32 * 1024 * 1024)
    core = lax.axis_index("core").reshape(1).astype(jnp.int32)
    swap = [(0, 1), (1, 0)]

    stored = (codes.astype(jnp.float32) * scales[:, None, :]).astype(jnp.bfloat16)
    own = lax.all_gather(stored, "zl", axis=0, tiled=True)

    rows = width // CORE
    keep, send = pl.pallas_call(
        lambda *refs: term_kernel(float(tokens) ** (-0.5), *refs),
        out_shape=[jax.ShapeDtypeStruct((rows, head), jnp.float32)] * 2,
        in_specs=[smem, vmem, vmem],
        out_specs=[vmem, vmem],
        compiler_params=params,
        cost_estimate=pl.CostEstimate(flops=2 * 128 * width * head, bytes_accessed=3 << 20, transcendentals=0),
    )(core, activations, cotangent)
    chip = keep + lax.ppermute(send, "core", swap)
    got = lax.all_to_all(chip.astype(jnp.bfloat16), "x", 0, 0, tiled=True)
    line = got.reshape(X, rows // X, head).astype(jnp.float32).sum(0).astype(jnp.bfloat16)
    peers = Y * ZH * ZL
    got = lax.all_to_all(
        line.reshape(peers, rows // X // peers, head), ("y", "zh", "zl"), 0, 0, tiled=True
    )
    weight_grad = got.astype(jnp.float32).sum(0)

    other = lax.ppermute(own, "core", swap)
    values_out = pl.pallas_call(
        project_kernel,
        out_shape=jax.ShapeDtypeStruct(cotangent.shape, jnp.bfloat16),
        in_specs=[smem, vmem, vmem, vmem],
        out_specs=vmem,
        compiler_params=params,
        cost_estimate=pl.CostEstimate(flops=2 * 128 * width * head, bytes_accessed=2 << 20, transcendentals=0),
    )(core, activations, own, other)
    return values_out, weight_grad


def solution(mesh):
    fine = Mesh(mesh.devices.reshape(Y, ZH, X, ZL, CORE), AXES)
    tokens, local = P(AXES, None), ("zl", "core")
    return jax.shard_map(
        on_device,
        mesh=fine,
        in_specs=(tokens, P(local, None, None), P(local, None), tokens),
        out_specs=(tokens, tokens),
        check_vma=False,
    )
```

time: 1300 us -> 111 us (0.09); the launches traced: 1280 us -> 109 us
  waiting for transfers between devices: 1250 us -> 18.6 us
  starting transfers between devices: 0.12 us -> 42.6 us
  blocking collectives: 0 us -> 41.3 us
  between operations: 13.8 us -> 0.74 us
    unnamed x4 -> x0, waiting for transfers between devices: 1040 us -> none
    reduce_scatter x1 -> x0, waiting for transfers between devices: 112 us -> none  [on_device(): lax.psum_scatter(shaped, 'local', scatter_dimension=1, tiled=True)]
    all_gather x1 -> x0, waiting for transfers between devices: 104 us -> none  [on_device(): lax.all_gather(stored, 'local', axis=0, tiled=True)]
    all_gather x0 -> x1, blocking collectives: none -> 41.3 us  [on_device(): own = lax.all_gather(stored, 'zl', axis=0, tiled=True)]
    ppermute x0 -> x2, starting transfers between devices: none -> 25.3 us  [the longest x1 16.1 us: on_device(): chip = keep + lax.ppermute(send, 'core', swap)]
    all_to_all x0 -> x2, starting transfers between devices: none -> 17.3 us  [the longest x1 13.7 us: on_device(): lax.all_to_all(line.reshape(peers, rows // X // peers, head), ('y', 'zh',...]
    all_to_all x0 -> x2, waiting for transfers between devices: none -> 16.3 us  [the longest x1 16.3 us: on_device(): lax.all_to_all(line.reshape(peers, rows // X // peers, head), ('y', 'zh',...]
  transfers between devices with their start and end apart: 3 -> 4, of which waited for: 3 -> 2; matrix products, arithmetic and copies ran while one was open for 0% -> 1% of each run, Pallas kernels for 0% -> 1%
where the time goes in v1:
time: 111 us; the launch traced here: 109 us
  starting transfers between devices  42.6 us (38%)
  blocking collectives  41.3 us (37%)
  waiting for transfers between devices  18.6 us (17%)
  other arithmetic  2.26 us (2%)
  local copies, waits for them, and re-layouts  1.99 us (2%)
  Pallas kernels  1.56 us (1%)
    all_gather x1, blocking collectives, on_device(): own = lax.all_gather(stored, 'zl', axis=0, tiled=True)  41.3 us
    all_to_all x1, waiting for transfers between devices, on_device(): lax.all_to_all(line.reshape(peers, rows // X // peers, head), ('y', 'zh',...  16.3 us
    ppermute x1, starting transfers between devices, on_device(): chip = keep + lax.ppermute(send, 'core', swap)  16.1 us
    all_to_all x1, starting transfers between devices, on_device(): lax.all_to_all(line.reshape(peers, rows // X // peers, head), ('y', 'zh',...  13.7 us
    ppermute x1, starting transfers between devices, on_device(): other = lax.ppermute(own, 'core', swap)  9.23 us
    all_to_all x1, starting transfers between devices, on_device(): got = lax.all_to_all(chip.astype(jnp.bfloat16), 'x', 0, 0, tiled=True)  3.6 us
    ppermute x1, waiting for transfers between devices, on_device(): chip = keep + lax.ppermute(send, 'core', swap)  2.26 us
  transfers between devices with their start and end apart: 4, of which 2 were waited for; matrix products, arithmetic and copies ran while one was open for 1% of the time, Pallas kernels for 1%

profile of v1, /device:TPU:1, one launch (start us, length us, event | category | flops | bytes accessed | tf_op | source)
XLA Modules:
  0.0 109.1 jit_solution(14444201660772743012)
XLA Ops:
  0.6 0.0 copy-start
  0.6 1.2 %copy-done = bf16[128,4096]{1,0:T(8,128)(2,1)S(1)} copy-done((bf16[128,4096]{1,0:T(8,128)(2,1)S(1)}, bf16[128,4096]{1,0:T(8,128)(2,1)}, u32[]{:S(2)}) %copy-start) | copy-done | bytes 1048600
  1.9 0.0 copy-start.2
  1.9 0.8 copy-done.2
  2.6 0.5 shard_map.60
  3.1 16.1 %collective-permute-start.1 = (f32[2048,128]{1,0:T(8,128)S(1)}, f32[2048,128]{1,0:T(8,128)S(1)}, u32[]{:S(2)}, u32[]{:S(2)}) collective-permute-start(f32[2048,128]{1,0:T(8,128)S(1)} %get-tuple-element.5), channel_id=1, source_target_pairs={{0,1},{1,0},{2,3},{3,2},{4,5},{5,4},{6,7},{7,6},{8,9},{9,8},{10,11... | collective-permute-start | bytes 3145736 | tf_op jit(solution)/shard_map/ppermute | solution.py:74
  19.2 2.3 %collective-permute-done.1 = f32[2048,128]{1,0:T(8,128)S(1)} collective-permute-done((f32[2048,128]{1,0:T(8,128)S(1)}, f32[2048,128]{1,0:T(8,128)S(1)}, u32[]{:S(2)}, u32[]{:S(2)}) %collective-permute-start.1) | collective-permute-done | bytes 1048608 | tf_op jit(solution)/shard_map/ppermute | solution.py:74
  21.5 0.9 add_convert_fusion
  22.4 0.0 copy-start.3
  22.4 0.0 copy-start.4
  22.4 3.6 %all-to-all-start = ((bf16[4,512,128]{2,1,0:T(8,128)(2,1)}), bf16[4,512,128]{2,1,0:T(8,128)(2,1)S(1)}, u32[]{:S(2)}, u32[]{:S(2)}) async-start(bf16[4,512,128]{2,1,0:T(8,128)(2,1)} %bitcast.2), calls=%async_computation | async-start | bytes 1048576 | tf_op jit(solution)/shard_map/all_to_all | solution.py:75
  26.0 0.0 copy-start.1
  26.0 0.0 copy-done.3
  26.0 0.0 copy-done.4
  26.0 41.3 %all_gather.3.own_ref = bf16[8,256,128]{2,1,0:T(8,128)(2,1)S(1)} all-gather(bf16[1,256,128]{2,1,0:T(8,128)(2,1)S(1)} %multiply_convert_fusion), channel_id=1, replica_groups=mesh['y'=8,'zh'=2,'x'=4,'zl'=8,'core'=2] {'zl'}, dimensions={0}, use_global_device_ids=true | all-gather | bytes 589824 | tf_op jit(solution)/shard_map/all_gather | solution.py:63
  67.3 9.2 %collective-permute-start = (bf16[8,256,128]{2,1,0:T(8,128)(2,1)S(1)}, bf16[8,256,128]{2,1,0:T(8,128)(2,1)S(1)}, u32[]{:S(2)}, u32[]{:S(2)}) collective-permute-start(bf16[8,256,128]{2,1,0:T(8,128)(2,1)S(1)} %all_gather.3.own_ref), channel_id=1, source_target_pairs={{0,1},{1,0},{2,3},{3,2},{4,5},{5,4},{6,7},{7,6},{8,9},{9,8},{10,11... | collective-permute-start | bytes 1572872 | tf_op jit(solution)/shard_map/ppermute | solution.py:83
  76.6 0.0 all-to-all-done
  76.6 0.7 reduce_sum.21
  77.3 13.7 %all-to-all-start.1 = ((bf16[128,4,128]{2,1,0:T(4,128)(2,1)}), bf16[128,4,128]{2,1,0:T(4,128)(2,1)S(1)}, u32[]{:S(2)}, u32[]{:S(2)}) async-start(bf16[128,4,128]{2,1,0:T(4,128)(2,1)} %bitcast.3), calls=%async_computation.1 | async-start | bytes 262144 | tf_op jit(solution)/shard_map/all_to_all | solution.py:78
  91.1 0.0 collective-permute-done.other_ref
  91.1 0.0 copy-done.1
  91.1 1.1 shard_map.59
  92.2 16.3 %all-to-all-done.1 = bf16[128,4,128]{2,1,0:T(4,128)(2,1)S(1)} async-done(((bf16[128,4,128]{2,1,0:T(4,128)(2,1)}), bf16[128,4,128]{2,1,0:T(4,128)(2,1)S(1)}, u32[]{:S(2)}, u32[]{:S(2)}) %all-to-all-start.1) | async-done | bytes 131104 | tf_op jit(solution)/shard_map/all_to_all | solution.py:78
  108.5 0.6 convert_reduce_fusion
  (1 shorter events, 0.0 us)
Async XLA Ops:
  0.6 1.2 %copy-start = (bf16[128,4096]{1,0:T(8,128)(2,1)S(1)}, bf16[128,4096]{1,0:T(8,128)(2,1)}, u32[]{:S(2)}) copy-start(bf16[128,4096]{1,0:T(8,128)(2,1)} %refs_1_.1) | copy-start | bytes 3145732
  1.9 0.8 copy-start.2
  3.1 18.3 %collective-permute-start.1 = (f32[2048,128]{1,0:T(8,128)S(1)}, f32[2048,128]{1,0:T(8,128)S(1)}, u32[]{:S(2)}, u32[]{:S(2)}) collective-permute-start(f32[2048,128]{1,0:T(8,128)S(1)} %get-tuple-element.5), channel_id=1, source_target_pairs={{0,1},{1,0},{2,3},{3,2},{4,5},{5,4},{6,7},{7,6},{8,9},{9,8},{10,11... | collective-permute-start | bytes 3145736 | tf_op jit(solution)/shard_map/ppermute | solution.py:74
  22.4 3.6 %copy-start.3 = (bf16[1,256,128]{2,1,0:T(8,128)(2,1)S(1)}, bf16[1,256,128]{2,1,0:T(8,128)(2,1)}, u32[]{:S(2)}) copy-start(bf16[1,256,128]{2,1,0:T(8,128)(2,1)} %param.5) | copy-start | bytes 196612
  22.4 3.6 %copy-start.4 = (f32[1,128]{1,0:T(1,128)S(1)}, f32[1,128]{1,0:T(1,128)}, u32[]{:S(2)}) copy-start(f32[1,128]{1,0:T(1,128)} %param.6) | copy-start | bytes 1540
  22.4 54.2 %all-to-all-start = ((bf16[4,512,128]{2,1,0:T(8,128)(2,1)}), bf16[4,512,128]{2,1,0:T(8,128)(2,1)S(1)}, u32[]{:S(2)}, u32[]{:S(2)}) async-start(bf16[4,512,128]{2,1,0:T(8,128)(2,1)} %bitcast.2), calls=%async_computation | async-start | bytes 1048576 | tf_op jit(solution)/shard_map/all_to_all | solution.py:75
  26.0 65.1 %copy-start.1 = (bf16[128,4096]{1,0:T(8,128)(2,1)S(1)}, bf16[128,4096]{1,0:T(8,128)(2,1)}, u32[]{:S(2)}) copy-start(bf16[128,4096]{1,0:T(8,128)(2,1)} %refs_1_.1) | copy-start | bytes 3145732
  67.3 23.7 %collective-permute-start = (bf16[8,256,128]{2,1,0:T(8,128)(2,1)S(1)}, bf16[8,256,128]{2,1,0:T(8,128)(2,1)S(1)}, u32[]{:S(2)}, u32[]{:S(2)}) collective-permute-start(bf16[8,256,128]{2,1,0:T(8,128)(2,1)S(1)} %all_gather.3.own_ref), channel_id=1, source_target_pairs={{0,1},{1,0},{2,3},{3,2},{4,5},{5,4},{6,7},{7,6},{8,9},{9,8},{10,11... | collective-permute-start | bytes 1572872 | tf_op jit(solution)/shard_map/ppermute | solution.py:83
  77.3 31.1 %all-to-all-start.1 = ((bf16[128,4,128]{2,1,0:T(4,128)(2,1)}), bf16[128,4,128]{2,1,0:T(4,128)(2,1)S(1)}, u32[]{:S(2)}, u32[]{:S(2)}) async-start(bf16[128,4,128]{2,1,0:T(4,128)(2,1)} %bitcast.3), calls=%async_computation.1 | async-start | bytes 262144 | tf_op jit(solution)/shard_map/all_to_all | solution.py:78

commit v2 on v1

--- a/solution.py
+++ b/solution.py
@@ -30,23 +30,34 @@
             even, odd = tiles[:, 0], tiles[:, 1]
             zero = jnp.where(low, even, pltpu.roll(odd, share, 1))
             one = jnp.where(low, pltpu.roll(even, share, 1), odd)
-            at = pl.ds((x * Y * ZH + outer) * half, half)
+            at = pl.ds(((outer // ZH * X + x) * ZH + outer % ZH) * half, half)
             keep_ref[at, :] = jnp.where(first, zero, one).reshape(half, -1)
             send_ref[at, :] = jnp.where(first, one, zero).reshape(half, -1)
 
 
-def project_kernel(core_ref, act_ref, own_ref, other_ref, out_ref):
-    core = core_ref[0]
-    block = own_ref.shape[1]
+def project_kernel(place_ref, act_ref, own_ref, other_ref, out_ref):
+    zl, core = place_ref[0], place_ref[1]
+    sign = 1 - 2 * core
+    block = own_ref.shape[0] // ZL
     total = None
-    for zl in range(ZL):
-        for ref, which in ((own_ref, core), (other_ref, 1 - core)):
-            at = pl.multiple_of((2 * zl + which) * block, block)
+    for step in range(ZL):
+        at_rows = pl.ds(step * block, block)
+        for ref, line, which in ((own_ref, zl + step * sign, core), (other_ref, zl - step * sign, 1 - core)):
+            at = pl.multiple_of((2 * ((line + ZL) % ZL) + which) * block, block)
             piece = jnp.dot(
-                act_ref[:, pl.ds(at, block)], ref[zl], preferred_element_type=jnp.float32
+                act_ref[:, pl.ds(at, block)], ref[at_rows, :], preferred_element_type=jnp.float32
             )
             total = piece if total is None else total + piece
     out_ref[...] = total.astype(out_ref.dtype)
+
+
+def along_z(value, shift):
+    ring = ZH * ZL
+    pairs = []
+    for z in range(ring):
+        pairs.append(((z + shift) % ring * CORE, z * CORE))
+        pairs.append(((z - shift) % ring * CORE + 1, z * CORE + 1))
+    return lax.ppermute(value, ("zh", "zl", "core"), pairs)
 
 
 def on_device(activations, codes, scales, cotangent):
@@ -57,10 +68,13 @@
     smem = pl.BlockSpec(memory_space=pltpu.SMEM)
     params = pltpu.CompilerParams(vmem_limit_bytes=32 * 1024 * 1024)
     core = lax.axis_index("core").reshape(1).astype(jnp.int32)
+    place = jnp.concatenate([lax.axis_index("zl").reshape(1).astype(jnp.int32), core])
     swap = [(0, 1), (1, 0)]
 
     stored = (codes.astype(jnp.float32) * scales[:, None, :]).astype(jnp.bfloat16)
-    own = lax.all_gather(stored, "zl", axis=0, tiled=True)
+    own = stored.reshape(-1, head)
+    for shift in (1, 2, 4):
+        own = jnp.concatenate([own, along_z(own, shift)])
 
     rows = width // CORE
     keep, send = pl.pallas_call(
@@ -72,13 +86,10 @@
         cost_estimate=pl.CostEstimate(flops=2 * 128 * width * head, bytes_accessed=3 << 20, transcendentals=0),
     )(core, activations, cotangent)
     chip = keep + lax.ppermute(send, "core", swap)
-    got = lax.all_to_all(chip.astype(jnp.bfloat16), "x", 0, 0, tiled=True)
-    line = got.reshape(X, rows // X, head).astype(jnp.float32).sum(0).astype(jnp.bfloat16)
-    peers = Y * ZH * ZL
-    got = lax.all_to_all(
-        line.reshape(peers, rows // X // peers, head), ("y", "zh", "zl"), 0, 0, tiled=True
-    )
-    weight_grad = got.astype(jnp.float32).sum(0)
+    got = lax.all_to_all(chip.astype(jnp.bfloat16), ("y", "x"), 0, 0, tiled=True)
+    peers = ZH * ZL
+    line = got.reshape(Y * X, peers, rows // (Y * X * peers), head).astype(jnp.float32).sum(0)
+    weight_grad = lax.all_to_all(line, ("zh", "zl"), 0, 0, tiled=True).sum(0)
 
     other = lax.ppermute(own, "core", swap)
     values_out = pl.pallas_call(
@@ -88,7 +99,7 @@
         out_specs=vmem,
         compiler_params=params,
         cost_estimate=pl.CostEstimate(flops=2 * 128 * width * head, bytes_accessed=2 << 20, transcendentals=0),
-    )(core, activations, own, other)
+    )(place, activations, own, other)
     return values_out, weight_grad
 
 

time: 111 us -> 80.6 us (0.73); the launches traced: 109 us -> 80 us
  blocking collectives: 41.3 us -> 0 us
  waiting for transfers between devices: 18.6 us -> 27.5 us
  starting transfers between devices: 42.6 us -> 45.2 us
    all_gather x1 -> x0, blocking collectives: 41.3 us -> none  [on_device(): own = lax.all_gather(stored, 'zl', axis=0, tiled=True)]
    ppermute x0 -> x3, waiting for transfers between devices: none -> 17.6 us  [along_z(): return lax.ppermute(value, ('zh', 'zl', 'core'), pairs)]
    all_to_all x2, waiting for transfers between devices: 16.3 us -> 9.9 us  [the longest x1 9.9 us: on_device(): weight_grad = lax.all_to_all(line, ('zh', 'zl'), 0, 0, tiled=True).sum(0)]
    ppermute x0 -> x3, starting transfers between devices: none -> 5.89 us  [along_z(): return lax.ppermute(value, ('zh', 'zl', 'core'), pairs)]
    all_to_all x2, starting transfers between devices: 17.3 us -> 14 us  [the longest x1 9.67 us: on_device(): lax.all_to_all(chip.astype(jnp.bfloat16), ('y', 'x'), 0, 0, tiled=True)]
    ppermute x1, waiting for transfers between devices: 2.26 us -> 0.01 us  [on_device(): chip = keep + lax.ppermute(send, 'core', swap)]
  transfers between devices with their start and end apart: 4 -> 7, of which waited for: 2 -> 3; matrix products, arithmetic and copies ran while one was open for 1% -> 2% of each run, Pallas kernels for 1% -> 2%
where the time goes in v2:
time: 80.6 us; the launch traced here: 80 us
  starting transfers between devices  45.2 us (56%)
  waiting for transfers between devices  27.5 us (34%)
  other arithmetic  2.36 us (3%)
  Pallas kernels  2.1 us (3%)
  local copies, waits for them, and re-layouts  1.99 us (2%)
    ppermute x3, waiting for transfers between devices, along_z(): return lax.ppermute(value, ('zh', 'zl', 'core'), pairs)  17.6 us
    ppermute x1, starting transfers between devices, on_device(): chip = keep + lax.ppermute(send, 'core', swap)  16.1 us
    all_to_all x1, waiting for transfers between devices, on_device(): weight_grad = lax.all_to_all(line, ('zh', 'zl'), 0, 0, tiled=True).sum(0)  9.9 us
    all_to_all x1, starting transfers between devices, on_device(): lax.all_to_all(chip.astype(jnp.bfloat16), ('y', 'x'), 0, 0, tiled=True)  9.67 us
    ppermute x1, starting transfers between devices, on_device(): other = lax.ppermute(own, 'core', swap)  9.31 us
    ppermute x3, starting transfers between devices, along_z(): return lax.ppermute(value, ('zh', 'zl', 'core'), pairs)  5.89 us
    all_to_all x1, starting transfers between devices, on_device(): weight_grad = lax.all_to_all(line, ('zh', 'zl'), 0, 0, tiled=True).sum(0)  4.31 us
    unnamed x10, local copies, waits for them, and re-layouts  1.99 us
  transfers between devices with their start and end apart: 7, of which 3 were waited for; matrix products, arithmetic and copies ran while one was open for 2% of the time, Pallas kernels for 2%

profile of v2, /device:TPU:1, one launch (start us, length us, event | category | flops | bytes accessed | tf_op | source)
XLA Modules:
  0.0 80.0 jit_solution(2997979720006317641)
XLA Ops:
  0.6 0.0 copy-start
  0.6 1.2 %copy-done = bf16[128,4096]{1,0:T(8,128)(2,1)S(1)} copy-done((bf16[128,4096]{1,0:T(8,128)(2,1)S(1)}, bf16[128,4096]{1,0:T(8,128)(2,1)}, u32[]{:S(2)}) %copy-start) | copy-done | bytes 1048600
  1.9 0.0 copy-start.2
  1.9 0.8 copy-done.2
  2.6 0.0 copy-start.3
  2.6 0.5 shard_map.60
  3.1 0.0 copy-start.4
  3.2 16.1 %collective-permute-start.4 = (f32[2048,128]{1,0:T(8,128)S(1)}, f32[2048,128]{1,0:T(8,128)S(1)}, u32[]{:S(2)}, u32[]{:S(2)}) collective-permute-start(f32[2048,128]{1,0:T(8,128)S(1)} %get-tuple-element.5), channel_id=1, source_target_pairs={{0,1},{1,0},{2,3},{3,2},{4,5},{5,4},{6,7},{7,6},{8,9},{9,8},{10,11... | collective-permute-start | bytes 3145736 | tf_op jit(solution)/shard_map/ppermute | solution.py:88
  19.2 0.0 copy-done.3
  19.2 0.0 copy-done.4
  19.3 1.9 %collective-permute-start = (bf16[256,128]{1,0:T(8,128)(2,1)S(1)}, bf16[256,128]{1,0:T(8,128)(2,1)S(1)}, u32[]{:S(2)}, u32[]{:S(2)}) collective-permute-start(bf16[256,128]{1,0:T(8,128)(2,1)S(1)} %fusion), channel_id=1, source_target_pairs={{2,0},{79,1},{4,2},{1,3},{6,4},{3,5},{8,6},{5,7},{10,8},{7,9},{12,... | collective-permute-start | bytes 196616 | tf_op jit(solution)/shard_map/ppermute | solution.py:60
  21.2 5.0 %collective-permute-done = bf16[256,128]{1,0:T(8,128)(2,1)S(1)} collective-permute-done((bf16[256,128]{1,0:T(8,128)(2,1)S(1)}, bf16[256,128]{1,0:T(8,128)(2,1)S(1)}, u32[]{:S(2)}, u32[]{:S(2)}) %collective-permute-start) | collective-permute-done | bytes 65568 | tf_op jit(solution)/shard_map/ppermute | solution.py:60
  26.2 1.9 %collective-permute-start.1 = (bf16[512,128]{1,0:T(8,128)(2,1)S(1)}, bf16[512,128]{1,0:T(8,128)(2,1)S(1)}, u32[]{:S(2)}, u32[]{:S(2)}) collective-permute-start(bf16[512,128]{1,0:T(8,128)(2,1)S(1)} %pad_maximum_fusion.2), channel_id=1, source_target_pairs={{4,0},{77,1},{6,2},{79,3},{8,4},{1,5},{10,6},{3,7},{12,8},{5,9},{1... | collective-permute-start | bytes 393224 | tf_op jit(solution)/shard_map/ppermute | solution.py:60
  28.2 0.0 collective-permute-done.4
  28.2 0.9 %add_convert_fusion = bf16[2048,128]{1,0:T(8,128)(2,1)} fusion(f32[2048,128]{1,0:T(8,128)S(1)} %get-tuple-element.4, f32[2048,128]{1,0:T(8,128)S(1)} %collective-permute-done.4), kind=kLoop, calls=%fused_computation.1 | loop fusion | flops 524288 | bytes 2621440 | tf_op jit(solution)/shard_map/convert_element_type | solution.py:89
  29.1 9.7 %all-to-all-start = ((bf16[32,64,128]{2,1,0:T(8,128)(2,1)}), bf16[32,64,128]{2,1,0:T(8,128)(2,1)S(1)}, u32[]{:S(2)}, u32[]{:S(2)}) async-start(bf16[32,64,128]{2,1,0:T(8,128)(2,1)} %bitcast.4), calls=%async_computation | async-start | bytes 1048576 | tf_op jit(solution)/shard_map/all_to_all | solution.py:89
  38.7 0.0 copy-start.1
  38.8 0.0 collective-permute-done.1
  38.8 2.1 %collective-permute-start.2 = (bf16[1024,128]{1,0:T(8,128)(2,1)S(1)}, bf16[1024,128]{1,0:T(8,128)(2,1)S(1)}, u32[]{:S(2)}, u32[]{:S(2)}) collective-permute-start(bf16[1024,128]{1,0:T(8,128)(2,1)S(1)} %pad_maximum_fusion.1), channel_id=1, source_target_pairs={{8,0},{73,1},{10,2},{75,3},{12,4},{77,5},{14,6},{79,7},{64,8},{1,9... | collective-permute-start | bytes 786440 | tf_op jit(solution)/shard_map/ppermute | solution.py:60
  40.9 12.6 %collective-permute-done.2 = bf16[1024,128]{1,0:T(8,128)(2,1)S(1)} collective-permute-done((bf16[1024,128]{1,0:T(8,128)(2,1)S(1)}, bf16[1024,128]{1,0:T(8,128)(2,1)S(1)}, u32[]{:S(2)}, u32[]{:S(2)}) %collective-permute-start.2) | collective-permute-done | bytes 262176 | tf_op jit(solution)/shard_map/ppermute | solution.py:60
  53.5 9.3 %collective-permute-start.3 = (bf16[2048,128]{1,0:T(8,128)(2,1)S(1)}, bf16[2048,128]{1,0:T(8,128)(2,1)S(1)}, u32[]{:S(2)}, u32[]{:S(2)}) collective-permute-start(bf16[2048,128]{1,0:T(8,128)(2,1)S(1)} %pad_maximum_fusion.own_ref), channel_id=1, source_target_pairs={{0,1},{1,0},{2,3},{3,2},{4,5},{5,4},{6,7},{7,6},{8,9},{9,8},{10,11... | collective-permute-start | bytes 1572872 | tf_op jit(solution)/shard_map/ppermute | solution.py:94
  62.8 0.0 all-to-all-done
  62.8 0.7 convert_reduce_fusion
  63.5 4.3 %all-to-all-start.1 = ((f32[16,4,128]{2,1,0:T(4,128)}), f32[16,4,128]{2,1,0:T(4,128)S(1)}, u32[]{:S(2)}, u32[]{:S(2)}) async-start(f32[16,4,128]{2,1,0:T(4,128)} %bitcast.5), calls=%async_computation.1 | async-start | bytes 65536 | tf_op jit(solution)/shard_map/all_to_all | solution.py:92
  67.8 0.1 pad_add_fusion.place_ref
  67.9 0.0 collective-permute-done.3.other_ref
  67.9 0.0 copy-done.1
  67.9 1.6 %shard_map.59 = bf16[128,128]{1,0:T(8,128)(2,1)} custom-call(s32[2]{0:T(128)S(1)} %pad_add_fusion.place_ref, bf16[128,4096]{1,0:T(8,128)(2,1)S(1)} %copy-done.1, bf16[2048,128]{1,0:T(8,128)(2,1)S(1)} %pad_maximum_fusion.own_ref, bf16[2048,128]{1,0:T(8,128)(2,1)S(1)} %collective-permute-done.3.other_ref), custom_call_target="tpu_custom_call" | custom-call | flops 134217728 | bytes 2097152 | tf_op jit(solution)/shard_map/pallas_call | solution.py:95
  69.5 9.9 %all-to-all-done.1 = f32[16,4,128]{2,1,0:T(4,128)S(1)} async-done(((f32[16,4,128]{2,1,0:T(4,128)}), f32[16,4,128]{2,1,0:T(4,128)S(1)}, u32[]{:S(2)}, u32[]{:S(2)}) %all-to-all-start.1) | async-done | bytes 32800 | tf_op jit(solution)/shard_map/all_to_all | solution.py:92
  79.4 0.6 reduce_sum.22
  (4 shorter events, 0.1 us)
Async XLA Ops:
  0.6 1.2 %copy-start = (bf16[128,4096]{1,0:T(8,128)(2,1)S(1)}, bf16[128,4096]{1,0:T(8,128)(2,1)}, u32[]{:S(2)}) copy-start(bf16[128,4096]{1,0:T(8,128)(2,1)} %refs_1_.1) | copy-start | bytes 3145732
  1.9 0.8 copy-start.2
  2.6 16.6 %copy-start.3 = (bf16[1,256,128]{2,1,0:T(8,128)(2,1)S(1)}, bf16[1,256,128]{2,1,0:T(8,128)(2,1)}, u32[]{:S(2)}) copy-start(bf16[1,256,128]{2,1,0:T(8,128)(2,1)} %param.5) | copy-start | bytes 196612
  3.1 16.1 %copy-start.4 = (f32[1,128]{1,0:T(1,128)S(1)}, f32[1,128]{1,0:T(1,128)}, u32[]{:S(2)}) copy-start(f32[1,128]{1,0:T(1,128)} %param.6) | copy-start | bytes 1540
  3.2 25.0 %collective-permute-start.4 = (f32[2048,128]{1,0:T(8,128)S(1)}, f32[2048,128]{1,0:T(8,128)S(1)}, u32[]{:S(2)}, u32[]{:S(2)}) collective-permute-start(f32[2048,128]{1,0:T(8,128)S(1)} %get-tuple-element.5), channel_id=1, source_target_pairs={{0,1},{1,0},{2,3},{3,2},{4,5},{5,4},{6,7},{7,6},{8,9},{9,8},{10,11... | collective-permute-start | bytes 3145736 | tf_op jit(solution)/shard_map/ppermute | solution.py:88
  19.3 6.9 %collective-permute-start = (bf16[256,128]{1,0:T(8,128)(2,1)S(1)}, bf16[256,128]{1,0:T(8,128)(2,1)S(1)}, u32[]{:S(2)}, u32[]{:S(2)}) collective-permute-start(bf16[256,128]{1,0:T(8,128)(2,1)S(1)} %fusion), channel_id=1, source_target_pairs={{2,0},{79,1},{4,2},{1,3},{6,4},{3,5},{8,6},{5,7},{10,8},{7,9},{12,... | collective-permute-start | bytes 196616 | tf_op jit(solution)/shard_map/ppermute | solution.py:60
  26.2 12.5 %collective-permute-start.1 = (bf16[512,128]{1,0:T(8,128)(2,1)S(1)}, bf16[512,128]{1,0:T(8,128)(2,1)S(1)}, u32[]{:S(2)}, u32[]{:S(2)}) collective-permute-start(bf16[512,128]{1,0:T(8,128)(2,1)S(1)} %pad_maximum_fusion.2), channel_id=1, source_target_pairs={{4,0},{77,1},{6,2},{79,3},{8,4},{1,5},{10,6},{3,7},{12,8},{5,9},{1... | collective-permute-start | bytes 393224 | tf_op jit(solution)/shard_map/ppermute | solution.py:60
  29.1 33.7 %all-to-all-start = ((bf16[32,64,128]{2,1,0:T(8,128)(2,1)}), bf16[32,64,128]{2,1,0:T(8,128)(2,1)S(1)}, u32[]{:S(2)}, u32[]{:S(2)}) async-start(bf16[32,64,128]{2,1,0:T(8,128)(2,1)} %bitcast.4), calls=%async_computation | async-start | bytes 1048576 | tf_op jit(solution)/shard_map/all_to_all | solution.py:89
  38.7 29.1 %copy-start.1 = (bf16[128,4096]{1,0:T(8,128)(2,1)S(1)}, bf16[128,4096]{1,0:T(8,128)(2,1)}, u32[]{:S(2)}) copy-start(bf16[128,4096]{1,0:T(8,128)(2,1)} %refs_1_.1) | copy-start | bytes 3145732
  38.8 14.6 %collective-permute-start.2 = (bf16[1024,128]{1,0:T(8,128)(2,1)S(1)}, bf16[1024,128]{1,0:T(8,128)(2,1)S(1)}, u32[]{:S(2)}, u32[]{:S(2)}) collective-permute-start(bf16[1024,128]{1,0:T(8,128)(2,1)S(1)} %pad_maximum_fusion.1), channel_id=1, source_target_pairs={{8,0},{73,1},{10,2},{75,3},{12,4},{77,5},{14,6},{79,7},{64,8},{1,9... | collective-permute-start | bytes 786440 | tf_op jit(solution)/shard_map/ppermute | solution.py:60
  53.5 14.4 %collective-permute-start.3 = (bf16[2048,128]{1,0:T(8,128)(2,1)S(1)}, bf16[2048,128]{1,0:T(8,128)(2,1)S(1)}, u32[]{:S(2)}, u32[]{:S(2)}) collective-permute-start(bf16[2048,128]{1,0:T(8,128)(2,1)S(1)} %pad_maximum_fusion.own_ref), channel_id=1, source_target_pairs={{0,1},{1,0},{2,3},{3,2},{4,5},{5,4},{6,7},{7,6},{8,9},{9,8},{10,11... | collective-permute-start | bytes 1572872 | tf_op jit(solution)/shard_map/ppermute | solution.py:94
  63.5 15.9 %all-to-all-start.1 = ((f32[16,4,128]{2,1,0:T(4,128)}), f32[16,4,128]{2,1,0:T(4,128)S(1)}, u32[]{:S(2)}, u32[]{:S(2)}) async-start(f32[16,4,128]{2,1,0:T(4,128)} %bitcast.5), calls=%async_computation.1 | async-start | bytes 65536 | tf_op jit(solution)/shard_map/all_to_all | solution.py:92

commit v3 on v2

--- a/solution.py
+++ b/solution.py
@@ -7,6 +7,7 @@
 
 Y, ZH, X, ZL, CORE = 8, 2, 4, 8, 2
 AXES = ("y", "zh", "x", "zl", "core")
+SHIFTS = (4, 2, 1)
 
 
 def term_kernel(scale, core_ref, act_ref, cot_ref, keep_ref, send_ref):
@@ -35,13 +36,20 @@
             send_ref[at, :] = jnp.where(first, one, zero).reshape(half, -1)
 
 
+def gather_order():
+    held = [0]
+    for shift in SHIFTS:
+        held = held + [step + shift for step in held]
+    return held
+
+
 def project_kernel(place_ref, act_ref, own_ref, other_ref, out_ref):
     zl, core = place_ref[0], place_ref[1]
     sign = 1 - 2 * core
     block = own_ref.shape[0] // ZL
     total = None
-    for step in range(ZL):
-        at_rows = pl.ds(step * block, block)
+    for place, step in enumerate(gather_order()):
+        at_rows = pl.ds(place * block, block)
         for ref, line, which in ((own_ref, zl + step * sign, core), (other_ref, zl - step * sign, 1 - core)):
             at = pl.multiple_of((2 * ((line + ZL) % ZL) + which) * block, block)
             piece = jnp.dot(
@@ -73,7 +81,7 @@
 
     stored = (codes.astype(jnp.float32) * scales[:, None, :]).astype(jnp.bfloat16)
     own = stored.reshape(-1, head)
-    for shift in (1, 2, 4):
+    for shift in SHIFTS:
         own = jnp.concatenate([own, along_z(own, shift)])
 
     rows = width // CORE

time: 80.6 us -> 80.3 us (level)
  waiting for transfers between devices: 27.5 us -> 23.2 us
  starting transfers between devices: 45.2 us -> 49.2 us
    all_to_all x1, starting transfers between devices: 4.31 us -> 10.7 us  [on_device(): weight_grad = lax.all_to_all(line, ('zh', 'zl'), 0, 0, tiled=True).sum(0)]
    ppermute x1, starting transfers between devices: 9.31 us -> 3.84 us  [on_device(): other = lax.ppermute(own, 'core', swap)]
    ppermute x3, waiting for transfers between devices: 17.6 us -> 13.4 us  [along_z(): return lax.ppermute(value, ('zh', 'zl', 'core'), pairs)]
    ppermute x3, starting transfers between devices: 5.89 us -> 8.25 us  [along_z(): return lax.ppermute(value, ('zh', 'zl', 'core'), pairs)]
where the time goes in v3:
time: 80.3 us; the launch traced here: 79.7 us
  starting transfers between devices  49.2 us (61%)
  waiting for transfers between devices  23.2 us (29%)
  other arithmetic  2.36 us (3%)
  Pallas kernels  2.11 us (3%)
  local copies, waits for them, and re-layouts  1.99 us (2%)
    ppermute x1, starting transfers between devices, on_device(): chip = keep + lax.ppermute(send, 'core', swap)  16.1 us
    ppermute x3, waiting for transfers between devices, along_z(): return lax.ppermute(value, ('zh', 'zl', 'core'), pairs)  13.4 us
    all_to_all x1, starting transfers between devices, on_device(): weight_grad = lax.all_to_all(line, ('zh', 'zl'), 0, 0, tiled=True).sum(0)  10.7 us
    all_to_all x1, starting transfers between devices, on_device(): lax.all_to_all(chip.astype(jnp.bfloat16), ('y', 'x'), 0, 0, tiled=True)  10.4 us
    all_to_all x1, waiting for transfers between devices, on_device(): weight_grad = lax.all_to_all(line, ('zh', 'zl'), 0, 0, tiled=True).sum(0)  9.79 us
    ppermute x3, starting transfers between devices, along_z(): return lax.ppermute(value, ('zh', 'zl', 'core'), pairs)  8.25 us
    ppermute x1, starting transfers between devices, on_device(): other = lax.ppermute(own, 'core', swap)  3.84 us
    unnamed x10, local copies, waits for them, and re-layouts  1.99 us
  transfers between devices with their start and end apart: 7, of which 3 were waited for; matrix products, arithmetic and copies ran while one was open for 2% of the time, Pallas kernels for 2%

profile of v3, /device:TPU:1, one launch (start us, length us, event | category | flops | bytes accessed | tf_op | source)
XLA Modules:
  0.0 79.7 jit_solution(11304422269901833842)
XLA Ops:
  0.6 0.0 copy-start
  0.6 1.2 %copy-done = bf16[128,4096]{1,0:T(8,128)(2,1)S(1)} copy-done((bf16[128,4096]{1,0:T(8,128)(2,1)S(1)}, bf16[128,4096]{1,0:T(8,128)(2,1)}, u32[]{:S(2)}) %copy-start) | copy-done | bytes 1048600
  1.9 0.0 copy-start.2
  1.9 0.8 copy-done.2
  2.6 0.0 copy-start.3
  2.6 0.5 shard_map.60
  3.1 0.0 copy-start.4
  3.2 16.1 %collective-permute-start.4 = (f32[2048,128]{1,0:T(8,128)S(1)}, f32[2048,128]{1,0:T(8,128)S(1)}, u32[]{:S(2)}, u32[]{:S(2)}) collective-permute-start(f32[2048,128]{1,0:T(8,128)S(1)} %get-tuple-element.5), channel_id=1, source_target_pairs={{0,1},{1,0},{2,3},{3,2},{4,5},{5,4},{6,7},{7,6},{8,9},{9,8},{10,11... | collective-permute-start | bytes 3145736 | tf_op jit(solution)/shard_map/ppermute | solution.py:96
  19.2 0.0 copy-done.3
  19.2 0.0 copy-done.4
  19.3 1.9 %collective-permute-start = (bf16[256,128]{1,0:T(8,128)(2,1)S(1)}, bf16[256,128]{1,0:T(8,128)(2,1)S(1)}, u32[]{:S(2)}, u32[]{:S(2)}) collective-permute-start(bf16[256,128]{1,0:T(8,128)(2,1)S(1)} %fusion), channel_id=1, source_target_pairs={{8,0},{73,1},{10,2},{75,3},{12,4},{77,5},{14,6},{79,7},{64,8},{1,9... | collective-permute-start | bytes 196616 | tf_op jit(solution)/shard_map/ppermute | solution.py:68
  21.2 7.3 %collective-permute-done = bf16[256,128]{1,0:T(8,128)(2,1)S(1)} collective-permute-done((bf16[256,128]{1,0:T(8,128)(2,1)S(1)}, bf16[256,128]{1,0:T(8,128)(2,1)S(1)}, u32[]{:S(2)}, u32[]{:S(2)}) %collective-permute-start) | collective-permute-done | bytes 65568 | tf_op jit(solution)/shard_map/ppermute | solution.py:68
  28.5 2.5 %collective-permute-start.1 = (bf16[512,128]{1,0:T(8,128)(2,1)S(1)}, bf16[512,128]{1,0:T(8,128)(2,1)S(1)}, u32[]{:S(2)}, u32[]{:S(2)}) collective-permute-start(bf16[512,128]{1,0:T(8,128)(2,1)S(1)} %pad_maximum_fusion.2), channel_id=1, source_target_pairs={{4,0},{77,1},{6,2},{79,3},{8,4},{1,5},{10,6},{3,7},{12,8},{5,9},{1... | collective-permute-start | bytes 393224 | tf_op jit(solution)/shard_map/ppermute | solution.py:68
  31.0 0.0 collective-permute-done.4
  31.0 0.9 %add_convert_fusion = bf16[2048,128]{1,0:T(8,128)(2,1)} fusion(f32[2048,128]{1,0:T(8,128)S(1)} %get-tuple-element.4, f32[2048,128]{1,0:T(8,128)S(1)} %collective-permute-done.4), kind=kLoop, calls=%fused_computation.1 | loop fusion | flops 524288 | bytes 2621440 | tf_op jit(solution)/shard_map/convert_element_type | solution.py:97
  31.9 10.4 %all-to-all-start = ((bf16[32,64,128]{2,1,0:T(8,128)(2,1)}), bf16[32,64,128]{2,1,0:T(8,128)(2,1)S(1)}, u32[]{:S(2)}, u32[]{:S(2)}) async-start(bf16[32,64,128]{2,1,0:T(8,128)(2,1)} %bitcast.4), calls=%async_computation | async-start | bytes 1048576 | tf_op jit(solution)/shard_map/all_to_all | solution.py:97
  42.3 0.0 copy-start.1
  42.3 0.0 collective-permute-done.1
  42.3 3.8 %collective-permute-start.2 = (bf16[1024,128]{1,0:T(8,128)(2,1)S(1)}, bf16[1024,128]{1,0:T(8,128)(2,1)S(1)}, u32[]{:S(2)}, u32[]{:S(2)}) collective-permute-start(bf16[1024,128]{1,0:T(8,128)(2,1)S(1)} %pad_maximum_fusion.1), channel_id=1, source_target_pairs={{2,0},{79,1},{4,2},{1,3},{6,4},{3,5},{8,6},{5,7},{10,8},{7,9},{12,... | collective-permute-start | bytes 786440 | tf_op jit(solution)/shard_map/ppermute | solution.py:68
  46.2 6.2 %collective-permute-done.2 = bf16[1024,128]{1,0:T(8,128)(2,1)S(1)} collective-permute-done((bf16[1024,128]{1,0:T(8,128)(2,1)S(1)}, bf16[1024,128]{1,0:T(8,128)(2,1)S(1)}, u32[]{:S(2)}, u32[]{:S(2)}) %collective-permute-start.2) | collective-permute-done | bytes 262176 | tf_op jit(solution)/shard_map/ppermute | solution.py:68
  52.4 3.8 %collective-permute-start.3 = (bf16[2048,128]{1,0:T(8,128)(2,1)S(1)}, bf16[2048,128]{1,0:T(8,128)(2,1)S(1)}, u32[]{:S(2)}, u32[]{:S(2)}) collective-permute-start(bf16[2048,128]{1,0:T(8,128)(2,1)S(1)} %pad_maximum_fusion.own_ref), channel_id=1, source_target_pairs={{0,1},{1,0},{2,3},{3,2},{4,5},{5,4},{6,7},{7,6},{8,9},{9,8},{10,11... | collective-permute-start | bytes 1572872 | tf_op jit(solution)/shard_map/ppermute | solution.py:102
  56.2 0.0 all-to-all-done
  56.2 0.7 convert_reduce_fusion
  56.9 10.7 %all-to-all-start.1 = ((f32[16,4,128]{2,1,0:T(4,128)}), f32[16,4,128]{2,1,0:T(4,128)S(1)}, u32[]{:S(2)}, u32[]{:S(2)}) async-start(f32[16,4,128]{2,1,0:T(4,128)} %bitcast.5), calls=%async_computation.1 | async-start | bytes 65536 | tf_op jit(solution)/shard_map/all_to_all | solution.py:100
  67.6 0.1 pad_add_fusion.place_ref
  67.7 0.0 collective-permute-done.3.other_ref
  67.7 0.0 copy-done.1
  67.7 1.6 %shard_map.59 = bf16[128,128]{1,0:T(8,128)(2,1)} custom-call(s32[2]{0:T(128)S(1)} %pad_add_fusion.place_ref, bf16[128,4096]{1,0:T(8,128)(2,1)S(1)} %copy-done.1, bf16[2048,128]{1,0:T(8,128)(2,1)S(1)} %pad_maximum_fusion.own_ref, bf16[2048,128]{1,0:T(8,128)(2,1)S(1)} %collective-permute-done.3.other_ref), custom_call_target="tpu_custom_call" | custom-call | flops 134217728 | bytes 2097152 | tf_op jit(solution)/shard_map/pallas_call | solution.py:103
  69.3 9.8 %all-to-all-done.1 = f32[16,4,128]{2,1,0:T(4,128)S(1)} async-done(((f32[16,4,128]{2,1,0:T(4,128)}), f32[16,4,128]{2,1,0:T(4,128)S(1)}, u32[]{:S(2)}, u32[]{:S(2)}) %all-to-all-start.1) | async-done | bytes 32800 | tf_op jit(solution)/shard_map/all_to_all | solution.py:100
  79.1 0.6 reduce_sum.22
  (4 shorter events, 0.1 us)
Async XLA Ops:
  0.6 1.2 %copy-start = (bf16[128,4096]{1,0:T(8,128)(2,1)S(1)}, bf16[128,4096]{1,0:T(8,128)(2,1)}, u32[]{:S(2)}) copy-start(bf16[128,4096]{1,0:T(8,128)(2,1)} %refs_1_.1) | copy-start | bytes 3145732
  1.9 0.8 copy-start.2
  2.6 16.6 %copy-start.3 = (bf16[1,256,128]{2,1,0:T(8,128)(2,1)S(1)}, bf16[1,256,128]{2,1,0:T(8,128)(2,1)}, u32[]{:S(2)}) copy-start(bf16[1,256,128]{2,1,0:T(8,128)(2,1)} %param.5) | copy-start | bytes 196612
  3.1 16.1 %copy-start.4 = (f32[1,128]{1,0:T(1,128)S(1)}, f32[1,128]{1,0:T(1,128)}, u32[]{:S(2)}) copy-start(f32[1,128]{1,0:T(1,128)} %param.6) | copy-start | bytes 1540
  3.2 27.9 %collective-permute-start.4 = (f32[2048,128]{1,0:T(8,128)S(1)}, f32[2048,128]{1,0:T(8,128)S(1)}, u32[]{:S(2)}, u32[]{:S(2)}) collective-permute-start(f32[2048,128]{1,0:T(8,128)S(1)} %get-tuple-element.5), channel_id=1, source_target_pairs={{0,1},{1,0},{2,3},{3,2},{4,5},{5,4},{6,7},{7,6},{8,9},{9,8},{10,11... | collective-permute-start | bytes 3145736 | tf_op jit(solution)/shard_map/ppermute | solution.py:96
  19.3 9.2 %collective-permute-start = (bf16[256,128]{1,0:T(8,128)(2,1)S(1)}, bf16[256,128]{1,0:T(8,128)(2,1)S(1)}, u32[]{:S(2)}, u32[]{:S(2)}) collective-permute-start(bf16[256,128]{1,0:T(8,128)(2,1)S(1)} %fusion), channel_id=1, source_target_pairs={{8,0},{73,1},{10,2},{75,3},{12,4},{77,5},{14,6},{79,7},{64,8},{1,9... | collective-permute-start | bytes 196616 | tf_op jit(solution)/shard_map/ppermute | solution.py:68
  28.5 13.8 %collective-permute-start.1 = (bf16[512,128]{1,0:T(8,128)(2,1)S(1)}, bf16[512,128]{1,0:T(8,128)(2,1)S(1)}, u32[]{:S(2)}, u32[]{:S(2)}) collective-permute-start(bf16[512,128]{1,0:T(8,128)(2,1)S(1)} %pad_maximum_fusion.2), channel_id=1, source_target_pairs={{4,0},{77,1},{6,2},{79,3},{8,4},{1,5},{10,6},{3,7},{12,8},{5,9},{1... | collective-permute-start | bytes 393224 | tf_op jit(solution)/shard_map/ppermute | solution.py:68
  31.9 24.3 %all-to-all-start = ((bf16[32,64,128]{2,1,0:T(8,128)(2,1)}), bf16[32,64,128]{2,1,0:T(8,128)(2,1)S(1)}, u32[]{:S(2)}, u32[]{:S(2)}) async-start(bf16[32,64,128]{2,1,0:T(8,128)(2,1)} %bitcast.4), calls=%async_computation | async-start | bytes 1048576 | tf_op jit(solution)/shard_map/all_to_all | solution.py:97
  42.3 25.4 %copy-start.1 = (bf16[128,4096]{1,0:T(8,128)(2,1)S(1)}, bf16[128,4096]{1,0:T(8,128)(2,1)}, u32[]{:S(2)}) copy-start(bf16[128,4096]{1,0:T(8,128)(2,1)} %refs_1_.1) | copy-start | bytes 3145732
  42.3 10.0 %collective-permute-start.2 = (bf16[1024,128]{1,0:T(8,128)(2,1)S(1)}, bf16[1024,128]{1,0:T(8,128)(2,1)S(1)}, u32[]{:S(2)}, u32[]{:S(2)}) collective-permute-start(bf16[1024,128]{1,0:T(8,128)(2,1)S(1)} %pad_maximum_fusion.1), channel_id=1, source_target_pairs={{2,0},{79,1},{4,2},{1,3},{6,4},{3,5},{8,6},{5,7},{10,8},{7,9},{12,... | collective-permute-start | bytes 786440 | tf_op jit(solution)/shard_map/ppermute | solution.py:68
  52.4 15.3 %collective-permute-start.3 = (bf16[2048,128]{1,0:T(8,128)(2,1)S(1)}, bf16[2048,128]{1,0:T(8,128)(2,1)S(1)}, u32[]{:S(2)}, u32[]{:S(2)}) collective-permute-start(bf16[2048,128]{1,0:T(8,128)(2,1)S(1)} %pad_maximum_fusion.own_ref), channel_id=1, source_target_pairs={{0,1},{1,0},{2,3},{3,2},{4,5},{5,4},{6,7},{7,6},{8,9},{9,8},{10,11... | collective-permute-start | bytes 1572872 | tf_op jit(solution)/shard_map/ppermute | solution.py:102
  56.9 22.2 %all-to-all-start.1 = ((f32[16,4,128]{2,1,0:T(4,128)}), f32[16,4,128]{2,1,0:T(4,128)S(1)}, u32[]{:S(2)}, u32[]{:S(2)}) async-start(f32[16,4,128]{2,1,0:T(4,128)} %bitcast.5), calls=%async_computation.1 | async-start | bytes 65536 | tf_op jit(solution)/shard_map/all_to_all | solution.py:100

commit v4 on v2

--- a/solution.py
+++ b/solution.py
@@ -7,6 +7,7 @@
 
 Y, ZH, X, ZL, CORE = 8, 2, 4, 8, 2
 AXES = ("y", "zh", "x", "zl", "core")
+FIRST, SECOND = 3, 1
 
 
 def term_kernel(scale, core_ref, act_ref, cot_ref, keep_ref, send_ref):
@@ -35,17 +36,23 @@
             send_ref[at, :] = jnp.where(first, one, zero).reshape(half, -1)
 
 
+def gather_order():
+    held = [0, FIRST, -FIRST]
+    return held + [step + SECOND for step in held] + [step - SECOND for step in held[:2]]
+
+
 def project_kernel(place_ref, act_ref, own_ref, other_ref, out_ref):
     zl, core = place_ref[0], place_ref[1]
-    sign = 1 - 2 * core
-    block = own_ref.shape[0] // ZL
+    steps = gather_order()
+    block = own_ref.shape[0] // len(steps)
     total = None
-    for step in range(ZL):
-        at_rows = pl.ds(step * block, block)
-        for ref, line, which in ((own_ref, zl + step * sign, core), (other_ref, zl - step * sign, 1 - core)):
-            at = pl.multiple_of((2 * ((line + ZL) % ZL) + which) * block, block)
+    for place, step in enumerate(steps):
+        line = 2 * ((zl + step + ZL) % ZL)
+        rows = pl.ds(place * block, block)
+        for ref, which in ((own_ref, core), (other_ref, 1 - core)):
+            at = pl.multiple_of((line + which) * block, block)
             piece = jnp.dot(
-                act_ref[:, pl.ds(at, block)], ref[at_rows, :], preferred_element_type=jnp.float32
+                act_ref[:, pl.ds(at, block)], ref[rows, :], preferred_element_type=jnp.float32
             )
             total = piece if total is None else total + piece
     out_ref[...] = total.astype(out_ref.dtype)
@@ -53,11 +60,8 @@
 
 def along_z(value, shift):
     ring = ZH * ZL
-    pairs = []
-    for z in range(ring):
-        pairs.append(((z + shift) % ring * CORE, z * CORE))
-        pairs.append(((z - shift) % ring * CORE + 1, z * CORE + 1))
-    return lax.ppermute(value, ("zh", "zl", "core"), pairs)
+    pairs = [((z + shift) % ring, z) for z in range(ring)]
+    return lax.ppermute(value, ("zh", "zl"), pairs)
 
 
 def on_device(activations, codes, scales, cotangent):
@@ -73,8 +77,6 @@
 
     stored = (codes.astype(jnp.float32) * scales[:, None, :]).astype(jnp.bfloat16)
     own = stored.reshape(-1, head)
-    for shift in (1, 2, 4):
-        own = jnp.concatenate([own, along_z(own, shift)])
 
     rows = width // CORE
     keep, send = pl.pallas_call(
@@ -85,8 +87,12 @@
         compiler_params=params,
         cost_estimate=pl.CostEstimate(flops=2 * 128 * width * head, bytes_accessed=3 << 20, transcendentals=0),
     )(core, activations, cotangent)
+    held = jnp.concatenate([own, along_z(own, FIRST), along_z(own, -FIRST)])
     chip = keep + lax.ppermute(send, "core", swap)
-    got = lax.all_to_all(chip.astype(jnp.bfloat16), ("y", "x"), 0, 0, tiled=True)
+    chip = chip.astype(jnp.bfloat16)
+    two = 2 * own.shape[0]
+    own = jnp.concatenate([held, along_z(held, SECOND), along_z(held[:two], -SECOND)])
+    got = lax.all_to_all(chip, ("y", "x"), 0, 0, tiled=True)
     peers = ZH * ZL
     line = got.reshape(Y * X, peers, rows // (Y * X * peers), head).astype(jnp.float32).sum(0)
     weight_grad = lax.all_to_all(line, ("zh", "zl"), 0, 0, tiled=True).sum(0)

time: 80.6 us -> 74.8 us (0.928)
  waiting for transfers between devices: 27.5 us -> 21.5 us
    ppermute x3 -> x4, starting transfers between devices: 5.89 us -> 12.4 us  [along_z(): return lax.ppermute(value, ('zh', 'zl'), pairs)]
    ppermute x1, starting transfers between devices: 9.31 us -> 3.09 us  [on_device(): other = lax.ppermute(own, 'core', swap)]
    ppermute x3 -> x4, waiting for transfers between devices: 17.6 us -> 11.7 us  [along_z(): return lax.ppermute(value, ('zh', 'zl'), pairs)]
    unnamed x10 -> x13, local copies, waits for them, and re-layouts: 1.99 us -> 2.05 us
  transfers between devices with their start and end apart: 7 -> 8, of which waited for: 3 -> 3; matrix products, arithmetic and copies ran while one was open for 2% -> 2% of each run, Pallas kernels for 2% -> 2%
where the time goes in v4:
time: 74.8 us; the launch traced here: 74.2 us
  starting transfers between devices  45.4 us (61%)
  waiting for transfers between devices  21.5 us (29%)
  other arithmetic  2.31 us (3%)
  Pallas kernels  2.1 us (3%)
  local copies, waits for them, and re-layouts  2.07 us (3%)
  between operations  0.83 us (1%)
    ppermute x1, starting transfers between devices, on_device(): chip = keep + lax.ppermute(send, 'core', swap)  16.1 us
    ppermute x4, starting transfers between devices, along_z(): return lax.ppermute(value, ('zh', 'zl'), pairs)  12.4 us
    ppermute x4, waiting for transfers between devices, along_z(): return lax.ppermute(value, ('zh', 'zl'), pairs)  11.7 us
    all_to_all x1, waiting for transfers between devices, on_device(): weight_grad = lax.all_to_all(line, ('zh', 'zl'), 0, 0, tiled=True).sum(0)  9.8 us
    all_to_all x1, starting transfers between devices, on_device(): got = lax.all_to_all(chip, ('y', 'x'), 0, 0, tiled=True)  9.66 us
    all_to_all x1, starting transfers between devices, on_device(): weight_grad = lax.all_to_all(line, ('zh', 'zl'), 0, 0, tiled=True).sum(0)  4.26 us
    ppermute x1, starting transfers between devices, on_device(): other = lax.ppermute(own, 'core', swap)  3.09 us
    unnamed x13, local copies, waits for them, and re-layouts  2.05 us
  transfers between devices with their start and end apart: 8, of which 3 were waited for; matrix products, arithmetic and copies ran while one was open for 2% of the time, Pallas kernels for 2%

profile of v4, /device:TPU:1, one launch (start us, length us, event | category | flops | bytes accessed | tf_op | source)
XLA Modules:
  0.0 74.2 jit_solution(16547764171453105645)
XLA Ops:
  0.6 0.0 copy-start
  0.6 1.2 %copy-done = bf16[128,4096]{1,0:T(8,128)(2,1)S(1)} copy-done((bf16[128,4096]{1,0:T(8,128)(2,1)S(1)}, bf16[128,4096]{1,0:T(8,128)(2,1)}, u32[]{:S(2)}) %copy-start) | copy-done | bytes 1048600
  1.9 0.0 copy-start.2
  1.9 0.8 %copy-done.2 = bf16[128,128]{1,0:T(8,128)(2,1)S(1)} copy-done((bf16[128,128]{1,0:T(8,128)(2,1)S(1)}, bf16[128,128]{1,0:T(8,128)(2,1)}, u32[]{:S(2)}) %copy-start.2) | copy-done | bytes 32792
  2.6 0.0 copy-start.3
  2.6 0.5 shard_map.60
  3.1 0.0 copy-start.4
  3.2 16.1 %collective-permute-start.5 = (f32[2048,128]{1,0:T(8,128)S(1)}, f32[2048,128]{1,0:T(8,128)S(1)}, u32[]{:S(2)}, u32[]{:S(2)}) collective-permute-start(f32[2048,128]{1,0:T(8,128)S(1)} %get-tuple-element.5), channel_id=1, source_target_pairs={{0,1},{1,0},{2,3},{3,2},{4,5},{5,4},{6,7},{7,6},{8,9},{9,8},{10,11... | collective-permute-start | bytes 3145736 | tf_op jit(solution)/shard_map/ppermute | solution.py:91
  19.2 0.0 copy-done.3
  19.2 0.0 copy-done.4
  19.3 5.3 %collective-permute-start = (bf16[256,128]{1,0:T(8,128)(2,1)S(1)}, bf16[256,128]{1,0:T(8,128)(2,1)S(1)}, u32[]{:S(2)}, u32[]{:S(2)}) collective-permute-start(bf16[256,128]{1,0:T(8,128)(2,1)S(1)} %get-tuple-element.7), channel_id=1, source_target_pairs={{6,0},{8,2},{10,4},{12,6},{14,8},{64,10},{66,12},{68,14},{70,64},{... | collective-permute-start | bytes 196616 | tf_op jit(solution)/shard_map/ppermute | solution.py:64
  24.6 0.0 collective-permute-done.5
  24.6 0.9 %add_convert_fusion = bf16[2048,128]{1,0:T(8,128)(2,1)} fusion(f32[2048,128]{1,0:T(8,128)S(1)} %get-tuple-element.4, f32[2048,128]{1,0:T(8,128)S(1)} %collective-permute-done.5), kind=kLoop, calls=%fused_computation.1 | loop fusion | flops 524288 | bytes 2621440 | tf_op jit(solution)/shard_map/convert_element_type | solution.py:92
  25.5 9.7 %all-to-all-start = ((bf16[32,64,128]{2,1,0:T(8,128)(2,1)}), bf16[32,64,128]{2,1,0:T(8,128)(2,1)S(1)}, u32[]{:S(2)}, u32[]{:S(2)}) async-start(bf16[32,64,128]{2,1,0:T(8,128)(2,1)} %bitcast.4), calls=%async_computation | async-start | bytes 1048576 | tf_op jit(solution)/shard_map/all_to_all | solution.py:95
  35.1 0.0 copy-start.1
  35.1 2.1 %collective-permute-start.1 = (bf16[256,128]{1,0:T(8,128)(2,1)S(1)}, bf16[256,128]{1,0:T(8,128)(2,1)S(1)}, u32[]{:S(2)}, u32[]{:S(2)}) collective-permute-start(bf16[256,128]{1,0:T(8,128)(2,1)S(1)} %get-tuple-element.7), channel_id=1, source_target_pairs={{74,0},{76,2},{78,4},{0,6},{2,8},{4,10},{6,12},{8,14},{10,64},{12,... | collective-permute-start | bytes 196616 | tf_op jit(solution)/shard_map/ppermute | solution.py:64
  37.2 0.0 collective-permute-done
  37.2 3.1 %collective-permute-start.3 = (bf16[512,128]{1,0:T(8,128)(2,1)S(1)}, bf16[512,128]{1,0:T(8,128)(2,1)S(1)}, u32[]{:S(2)}, u32[]{:S(2)}) collective-permute-start(bf16[512,128]{1,0:T(8,128)(2,1)S(1)} %pad_maximum_fusion.1), channel_id=1, source_target_pairs={{78,0},{0,2},{2,4},{4,6},{6,8},{8,10},{10,12},{12,14},{14,64},{64,... | collective-permute-start | bytes 393224 | tf_op jit(solution)/shard_map/ppermute | solution.py:64
  40.3 4.3 %collective-permute-done.1 = bf16[256,128]{1,0:T(8,128)(2,1)S(1)} collective-permute-done((bf16[256,128]{1,0:T(8,128)(2,1)S(1)}, bf16[256,128]{1,0:T(8,128)(2,1)S(1)}, u32[]{:S(2)}, u32[]{:S(2)}) %collective-permute-start.1) | collective-permute-done | bytes 65568 | tf_op jit(solution)/shard_map/ppermute | solution.py:64
  44.7 1.9 %collective-permute-start.2 = (bf16[768,128]{1,0:T(8,128)(2,1)S(1)}, bf16[768,128]{1,0:T(8,128)(2,1)S(1)}, u32[]{:S(2)}, u32[]{:S(2)}) collective-permute-start(bf16[768,128]{1,0:T(8,128)(2,1)S(1)} %pad_maximum_fusion), channel_id=1, source_target_pairs={{2,0},{4,2},{6,4},{8,6},{10,8},{12,10},{14,12},{64,14},{66,64},{68... | collective-permute-start | bytes 589832 | tf_op jit(solution)/shard_map/ppermute | solution.py:64
  46.6 7.4 %collective-permute-done.2 = bf16[768,128]{1,0:T(8,128)(2,1)S(1)} collective-permute-done((bf16[768,128]{1,0:T(8,128)(2,1)S(1)}, bf16[768,128]{1,0:T(8,128)(2,1)S(1)}, u32[]{:S(2)}, u32[]{:S(2)}) %collective-permute-start.2) | collective-permute-done | bytes 196640 | tf_op jit(solution)/shard_map/ppermute | solution.py:64
  54.0 0.0 collective-permute-done.3
  54.1 3.1 %collective-permute-start.4 = (bf16[2048,128]{1,0:T(8,128)(2,1)S(1)}, bf16[2048,128]{1,0:T(8,128)(2,1)S(1)}, u32[]{:S(2)}, u32[]{:S(2)}) collective-permute-start(bf16[2048,128]{1,0:T(8,128)(2,1)S(1)} %constant_dynamic-update-slice_fusion.own_ref), channel_id=1, source_target_pairs={{0,1},{1,0},{2,3},{3,2},{4,5},{5,4},{6,7},{7,6},{8,9},{9,8},{10,11... | collective-permute-start | bytes 1572872 | tf_op jit(solution)/shard_map/ppermute | solution.py:100
  57.2 0.0 all-to-all-done
  57.2 0.7 convert_reduce_fusion
  57.9 4.3 %all-to-all-start.1 = ((f32[16,4,128]{2,1,0:T(4,128)}), f32[16,4,128]{2,1,0:T(4,128)S(1)}, u32[]{:S(2)}, u32[]{:S(2)}) async-start(f32[16,4,128]{2,1,0:T(4,128)} %bitcast.5), calls=%async_computation.1 | async-start | bytes 65536 | tf_op jit(solution)/shard_map/all_to_all | solution.py:98
  62.1 0.1 pad_add_fusion.place_ref
  62.2 0.0 collective-permute-done.4.other_ref
  62.2 0.0 copy-done.1
  62.2 1.6 %shard_map.59 = bf16[128,128]{1,0:T(8,128)(2,1)} custom-call(s32[2]{0:T(128)S(1)} %pad_add_fusion.place_ref, bf16[128,4096]{1,0:T(8,128)(2,1)S(1)} %copy-done.1, bf16[2048,128]{1,0:T(8,128)(2,1)S(1)} %constant_dynamic-update-slice_fusion.own_ref, bf16[2048,128]{1,0:T(8,128)(2,1)S(1)} %collective-permute-done.4.other_ref), custom_call_target="tpu_custom_call" | custom-call | flops 134217728 | bytes 2097152 | tf_op jit(solution)/shard_map/pallas_call | solution.py:101
  63.8 9.8 %all-to-all-done.1 = f32[16,4,128]{2,1,0:T(4,128)S(1)} async-done(((f32[16,4,128]{2,1,0:T(4,128)}), f32[16,4,128]{2,1,0:T(4,128)S(1)}, u32[]{:S(2)}, u32[]{:S(2)}) %all-to-all-start.1) | async-done | bytes 32800 | tf_op jit(solution)/shard_map/all_to_all | solution.py:98
  73.6 0.6 reduce_sum.22
  (7 shorter events, 0.1 us)
Async XLA Ops:
  0.6 1.2 %copy-start = (bf16[128,4096]{1,0:T(8,128)(2,1)S(1)}, bf16[128,4096]{1,0:T(8,128)(2,1)}, u32[]{:S(2)}) copy-start(bf16[128,4096]{1,0:T(8,128)(2,1)} %refs_1_.1) | copy-start | bytes 3145732
  1.9 0.8 %copy-start.2 = (bf16[128,128]{1,0:T(8,128)(2,1)S(1)}, bf16[128,128]{1,0:T(8,128)(2,1)}, u32[]{:S(2)}) copy-start(bf16[128,128]{1,0:T(8,128)(2,1)} %refs_2_.1) | copy-start | bytes 98308
  2.6 16.6 %copy-start.3 = (bf16[1,256,128]{2,1,0:T(8,128)(2,1)S(1)}, bf16[1,256,128]{2,1,0:T(8,128)(2,1)}, u32[]{:S(2)}) copy-start(bf16[1,256,128]{2,1,0:T(8,128)(2,1)} %param.5) | copy-start | bytes 196612
  3.1 16.1 %copy-start.4 = (f32[1,128]{1,0:T(1,128)S(1)}, f32[1,128]{1,0:T(1,128)}, u32[]{:S(2)}) copy-start(f32[1,128]{1,0:T(1,128)} %param.6) | copy-start | bytes 1540
  3.2 21.4 %collective-permute-start.5 = (f32[2048,128]{1,0:T(8,128)S(1)}, f32[2048,128]{1,0:T(8,128)S(1)}, u32[]{:S(2)}, u32[]{:S(2)}) collective-permute-start(f32[2048,128]{1,0:T(8,128)S(1)} %get-tuple-element.5), channel_id=1, source_target_pairs={{0,1},{1,0},{2,3},{3,2},{4,5},{5,4},{6,7},{7,6},{8,9},{9,8},{10,11... | collective-permute-start | bytes 3145736 | tf_op jit(solution)/shard_map/ppermute | solution.py:91
  19.3 17.9 %collective-permute-start = (bf16[256,128]{1,0:T(8,128)(2,1)S(1)}, bf16[256,128]{1,0:T(8,128)(2,1)S(1)}, u32[]{:S(2)}, u32[]{:S(2)}) collective-permute-start(bf16[256,128]{1,0:T(8,128)(2,1)S(1)} %get-tuple-element.7), channel_id=1, source_target_pairs={{6,0},{8,2},{10,4},{12,6},{14,8},{64,10},{66,12},{68,14},{70,64},{... | collective-permute-start | bytes 196616 | tf_op jit(solution)/shard_map/ppermute | solution.py:64
  25.5 31.7 %all-to-all-start = ((bf16[32,64,128]{2,1,0:T(8,128)(2,1)}), bf16[32,64,128]{2,1,0:T(8,128)(2,1)S(1)}, u32[]{:S(2)}, u32[]{:S(2)}) async-start(bf16[32,64,128]{2,1,0:T(8,128)(2,1)} %bitcast.4), calls=%async_computation | async-start | bytes 1048576 | tf_op jit(solution)/shard_map/all_to_all | solution.py:95
  35.1 27.1 %copy-start.1 = (bf16[128,4096]{1,0:T(8,128)(2,1)S(1)}, bf16[128,4096]{1,0:T(8,128)(2,1)}, u32[]{:S(2)}) copy-start(bf16[128,4096]{1,0:T(8,128)(2,1)} %refs_1_.1) | copy-start | bytes 3145732
  35.1 9.5 %collective-permute-start.1 = (bf16[256,128]{1,0:T(8,128)(2,1)S(1)}, bf16[256,128]{1,0:T(8,128)(2,1)S(1)}, u32[]{:S(2)}, u32[]{:S(2)}) collective-permute-start(bf16[256,128]{1,0:T(8,128)(2,1)S(1)} %get-tuple-element.7), channel_id=1, source_target_pairs={{74,0},{76,2},{78,4},{0,6},{2,8},{4,10},{6,12},{8,14},{10,64},{12,... | collective-permute-start | bytes 196616 | tf_op jit(solution)/shard_map/ppermute | solution.py:64
  37.2 16.8 %collective-permute-start.3 = (bf16[512,128]{1,0:T(8,128)(2,1)S(1)}, bf16[512,128]{1,0:T(8,128)(2,1)S(1)}, u32[]{:S(2)}, u32[]{:S(2)}) collective-permute-start(bf16[512,128]{1,0:T(8,128)(2,1)S(1)} %pad_maximum_fusion.1), channel_id=1, source_target_pairs={{78,0},{0,2},{2,4},{4,6},{6,8},{8,10},{10,12},{12,14},{14,64},{64,... | collective-permute-start | bytes 393224 | tf_op jit(solution)/shard_map/ppermute | solution.py:64
  44.7 9.4 %collective-permute-start.2 = (bf16[768,128]{1,0:T(8,128)(2,1)S(1)}, bf16[768,128]{1,0:T(8,128)(2,1)S(1)}, u32[]{:S(2)}, u32[]{:S(2)}) collective-permute-start(bf16[768,128]{1,0:T(8,128)(2,1)S(1)} %pad_maximum_fusion), channel_id=1, source_target_pairs={{2,0},{4,2},{6,4},{8,6},{10,8},{12,10},{14,12},{64,14},{66,64},{68... | collective-permute-start | bytes 589832 | tf_op jit(solution)/shard_map/ppermute | solution.py:64
  54.1 8.1 %collective-permute-start.4 = (bf16[2048,128]{1,0:T(8,128)(2,1)S(1)}, bf16[2048,128]{1,0:T(8,128)(2,1)S(1)}, u32[]{:S(2)}, u32[]{:S(2)}) collective-permute-start(bf16[2048,128]{1,0:T(8,128)(2,1)S(1)} %constant_dynamic-update-slice_fusion.own_ref), channel_id=1, source_target_pairs={{0,1},{1,0},{2,3},{3,2},{4,5},{5,4},{6,7},{7,6},{8,9},{9,8},{10,11... | collective-permute-start | bytes 1572872 | tf_op jit(solution)/shard_map/ppermute | solution.py:100
  57.9 15.7 %all-to-all-start.1 = ((f32[16,4,128]{2,1,0:T(4,128)}), f32[16,4,128]{2,1,0:T(4,128)S(1)}, u32[]{:S(2)}, u32[]{:S(2)}) async-start(f32[16,4,128]{2,1,0:T(4,128)} %bitcast.5), calls=%async_computation.1 | async-start | bytes 65536 | tf_op jit(solution)/shard_map/all_to_all | solution.py:98

commit v5 on v4

--- a/solution.py
+++ b/solution.py
@@ -41,20 +41,28 @@
     return held + [step + SECOND for step in held] + [step - SECOND for step in held[:2]]
 
 
-def project_kernel(place_ref, act_ref, own_ref, other_ref, out_ref):
-    zl, core = place_ref[0], place_ref[1]
+def project(place_ref, act_ref, shards_ref, which):
+    zl = place_ref[0]
     steps = gather_order()
-    block = own_ref.shape[0] // len(steps)
+    block = shards_ref.shape[0] // len(steps)
     total = None
     for place, step in enumerate(steps):
-        line = 2 * ((zl + step + ZL) % ZL)
-        rows = pl.ds(place * block, block)
-        for ref, which in ((own_ref, core), (other_ref, 1 - core)):
-            at = pl.multiple_of((line + which) * block, block)
-            piece = jnp.dot(
-                act_ref[:, pl.ds(at, block)], ref[rows, :], preferred_element_type=jnp.float32
-            )
-            total = piece if total is None else total + piece
+        at = pl.multiple_of((2 * ((zl + step + ZL) % ZL) + which) * block, block)
+        piece = jnp.dot(
+            act_ref[:, pl.ds(at, block)],
+            shards_ref[pl.ds(place * block, block), :],
+            preferred_element_type=jnp.float32,
+        )
+        total = piece if total is None else total + piece
+    return total
+
+
+def own_kernel(place_ref, act_ref, own_ref, out_ref):
+    out_ref[...] = project(place_ref, act_ref, own_ref, place_ref[1])
+
+
+def other_kernel(place_ref, act_ref, other_ref, part_ref, out_ref):
+    total = part_ref[...] + project(place_ref, act_ref, other_ref, 1 - place_ref[1])
     out_ref[...] = total.astype(out_ref.dtype)
 
 
@@ -88,24 +96,34 @@
         cost_estimate=pl.CostEstimate(flops=2 * 128 * width * head, bytes_accessed=3 << 20, transcendentals=0),
     )(core, activations, cotangent)
     held = jnp.concatenate([own, along_z(own, FIRST), along_z(own, -FIRST)])
+    keep, _ = lax.optimization_barrier((keep, own))
     chip = keep + lax.ppermute(send, "core", swap)
     chip = chip.astype(jnp.bfloat16)
-    two = 2 * own.shape[0]
-    own = jnp.concatenate([held, along_z(held, SECOND), along_z(held[:two], -SECOND)])
+    ahead, back = along_z(held, SECOND), along_z(held[: 2 * own.shape[0]], -SECOND)
     got = lax.all_to_all(chip, ("y", "x"), 0, 0, tiled=True)
     peers = ZH * ZL
     line = got.reshape(Y * X, peers, rows // (Y * X * peers), head).astype(jnp.float32).sum(0)
+    ahead, back, _ = lax.optimization_barrier((ahead, back, line))
+    own = jnp.concatenate([held, ahead, back])
     weight_grad = lax.all_to_all(line, ("zh", "zl"), 0, 0, tiled=True).sum(0)
 
+    part = pl.pallas_call(
+        own_kernel,
+        out_shape=jax.ShapeDtypeStruct(cotangent.shape, jnp.float32),
+        in_specs=[smem, vmem, vmem],
+        out_specs=vmem,
+        compiler_params=params,
+        cost_estimate=pl.CostEstimate(flops=10**11, bytes_accessed=1 << 20, transcendentals=0),
+    )(place, activations, own)
     other = lax.ppermute(own, "core", swap)
     values_out = pl.pallas_call(
-        project_kernel,
+        other_kernel,
         out_shape=jax.ShapeDtypeStruct(cotangent.shape, jnp.bfloat16),
         in_specs=[smem, vmem, vmem, vmem],
         out_specs=vmem,
         compiler_params=params,
-        cost_estimate=pl.CostEstimate(flops=2 * 128 * width * head, bytes_accessed=2 << 20, transcendentals=0),
-    )(place, activations, own, other)
+        cost_estimate=pl.CostEstimate(flops=128 * width * head, bytes_accessed=1 << 20, transcendentals=0),
+    )(place, activations, other, part)
     return values_out, weight_grad
 
 

time: 74.8 us -> 75.8 us (1.013)
  the two profiles are of different devices: /device:TPU:1 before, /device:TPU:2 now
where the time goes in v5:
time: 75.8 us; the launch traced here: 75.2 us
  starting transfers between devices  50.8 us (67%)
  waiting for transfers between devices  16.4 us (22%)
  Pallas kernels  2.79 us (4%)
  other arithmetic  2.32 us (3%)
  local copies, waits for them, and re-layouts  2.07 us (3%)
  between operations  0.84 us (1%)
    ppermute x4, starting transfers between devices, along_z(): return lax.ppermute(value, ('zh', 'zl'), pairs)  20.7 us
    all_to_all x1, starting transfers between devices, on_device(): got = lax.all_to_all(chip, ('y', 'x'), 0, 0, tiled=True)  16.7 us
    all_to_all x1, waiting for transfers between devices, on_device(): weight_grad = lax.all_to_all(line, ('zh', 'zl'), 0, 0, tiled=True).sum(0)  9.76 us
    all_to_all x1, starting transfers between devices, on_device(): weight_grad = lax.all_to_all(line, ('zh', 'zl'), 0, 0, tiled=True).sum(0)  9.57 us
    ppermute x4, waiting for transfers between devices, along_z(): return lax.ppermute(value, ('zh', 'zl'), pairs)  4.05 us
    ppermute x1, waiting for transfers between devices, on_device(): chip = keep + lax.ppermute(send, 'core', swap)  2.58 us
    unnamed x13, local copies, waits for them, and re-layouts  2.05 us
    ppermute x1, starting transfers between devices, on_device(): chip = keep + lax.ppermute(send, 'core', swap)  1.92 us
  transfers between devices with their start and end apart: 8, of which 3 were waited for; matrix products, arithmetic and copies ran while one was open for 2% of the time, Pallas kernels for 1%

profile of v5, /device:TPU:2, one launch (start us, length us, event | category | flops | bytes accessed | tf_op | source)
XLA Modules:
  0.0 75.2 jit_solution(15676463197299074738)
XLA Ops:
  0.6 0.0 copy-start
  0.6 1.2 %copy-done = bf16[128,4096]{1,0:T(8,128)(2,1)S(1)} copy-done((bf16[128,4096]{1,0:T(8,128)(2,1)S(1)}, bf16[128,4096]{1,0:T(8,128)(2,1)}, u32[]{:S(2)}) %copy-start) | copy-done | bytes 1048600
  1.9 0.0 copy-start.2
  1.9 0.8 %copy-done.2 = bf16[128,128]{1,0:T(8,128)(2,1)S(1)} copy-done((bf16[128,128]{1,0:T(8,128)(2,1)S(1)}, bf16[128,128]{1,0:T(8,128)(2,1)}, u32[]{:S(2)}) %copy-start.2) | copy-done | bytes 32792
  2.6 0.0 copy-start.3
  2.6 0.5 shard_map.59
  3.1 0.0 copy-start.4
  3.2 1.9 %collective-permute-start.4 = (f32[2048,128]{1,0:T(8,128)S(1)}, f32[2048,128]{1,0:T(8,128)S(1)}, u32[]{:S(2)}, u32[]{:S(2)}) collective-permute-start(f32[2048,128]{1,0:T(8,128)S(1)} %get-tuple-element.9), channel_id=1, source_target_pairs={{0,1},{1,0},{2,3},{3,2},{4,5},{5,4},{6,7},{7,6},{8,9},{9,8},{10,11... | collective-permute-start | bytes 3145736 | tf_op jit(solution)/shard_map/ppermute | solution.py:100
  5.1 0.0 copy-done.3
  5.1 0.0 copy-done.4
  5.1 2.6 %collective-permute-done.4 = f32[2048,128]{1,0:T(8,128)S(1)} collective-permute-done((f32[2048,128]{1,0:T(8,128)S(1)}, f32[2048,128]{1,0:T(8,128)S(1)}, u32[]{:S(2)}, u32[]{:S(2)}) %collective-permute-start.4) | collective-permute-done | bytes 1048608 | tf_op jit(solution)/shard_map/ppermute | solution.py:100
  7.7 0.9 %add_convert_fusion = bf16[2048,128]{1,0:T(8,128)(2,1)} fusion(f32[2048,128]{1,0:T(8,128)S(1)} %get-tuple-element.8, f32[2048,128]{1,0:T(8,128)S(1)} %collective-permute-done.4), kind=kLoop, calls=%fused_computation.1 | loop fusion | flops 524288 | bytes 2621440 | tf_op jit(solution)/shard_map/convert_element_type | solution.py:101
  8.6 16.7 %all-to-all-start = ((bf16[32,64,128]{2,1,0:T(8,128)(2,1)}), bf16[32,64,128]{2,1,0:T(8,128)(2,1)S(1)}, u32[]{:S(2)}, u32[]{:S(2)}) async-start(bf16[32,64,128]{2,1,0:T(8,128)(2,1)} %bitcast.4), calls=%async_computation | async-start | bytes 1048576 | tf_op jit(solution)/shard_map/all_to_all | solution.py:103
  25.3 1.9 %collective-permute-start.1 = (bf16[256,128]{1,0:T(8,128)(2,1)S(1)}, bf16[256,128]{1,0:T(8,128)(2,1)S(1)}, u32[]{:S(2)}, u32[]{:S(2)}) collective-permute-start(bf16[256,128]{1,0:T(8,128)(2,1)S(1)} %get-tuple-element.13), channel_id=1, source_target_pairs={{74,0},{76,2},{78,4},{0,6},{2,8},{4,10},{6,12},{8,14},{10,64},{12,... | collective-permute-start | bytes 196616 | tf_op jit(solution)/shard_map/ppermute | solution.py:72
  27.3 11.7 %collective-permute-start = (bf16[256,128]{1,0:T(8,128)(2,1)S(1)}, bf16[256,128]{1,0:T(8,128)(2,1)S(1)}, u32[]{:S(2)}, u32[]{:S(2)}) collective-permute-start(bf16[256,128]{1,0:T(8,128)(2,1)S(1)} %get-tuple-element.13), channel_id=1, source_target_pairs={{6,0},{8,2},{10,4},{12,6},{14,8},{64,10},{66,12},{68,14},{70,64},{... | collective-permute-start | bytes 196616 | tf_op jit(solution)/shard_map/ppermute | solution.py:72
  39.0 0.1 pad_add_fusion.place_ref
  39.1 4.0 %collective-permute-done = bf16[256,128]{1,0:T(8,128)(2,1)S(1)} collective-permute-done((bf16[256,128]{1,0:T(8,128)(2,1)S(1)}, bf16[256,128]{1,0:T(8,128)(2,1)S(1)}, u32[]{:S(2)}, u32[]{:S(2)}) %collective-permute-start) | collective-permute-done | bytes 65568 | tf_op jit(solution)/shard_map/ppermute | solution.py:72
  43.1 1.9 %collective-permute-start.3 = (bf16[512,128]{1,0:T(8,128)(2,1)S(1)}, bf16[512,128]{1,0:T(8,128)(2,1)S(1)}, u32[]{:S(2)}, u32[]{:S(2)}) collective-permute-start(bf16[512,128]{1,0:T(8,128)(2,1)S(1)} %pad_maximum_fusion.1), channel_id=1, source_target_pairs={{78,0},{0,2},{2,4},{4,6},{6,8},{8,10},{10,12},{12,14},{14,64},{64,... | collective-permute-start | bytes 393224 | tf_op jit(solution)/shard_map/ppermute | solution.py:72
  45.1 0.0 collective-permute-done.1
  45.1 5.1 %collective-permute-start.2 = (bf16[768,128]{1,0:T(8,128)(2,1)S(1)}, bf16[768,128]{1,0:T(8,128)(2,1)S(1)}, u32[]{:S(2)}, u32[]{:S(2)}) collective-permute-start(bf16[768,128]{1,0:T(8,128)(2,1)S(1)} %pad_maximum_fusion), channel_id=1, source_target_pairs={{2,0},{4,2},{6,4},{8,6},{10,8},{12,10},{14,12},{64,14},{66,64},{68... | collective-permute-start | bytes 589832 | tf_op jit(solution)/shard_map/ppermute | solution.py:72
  50.3 0.0 all-to-all-done
  50.3 0.7 convert_reduce_fusion
  51.0 9.6 %all-to-all-start.1 = ((f32[16,4,128]{2,1,0:T(4,128)}), f32[16,4,128]{2,1,0:T(4,128)S(1)}, u32[]{:S(2)}, u32[]{:S(2)}) async-start(f32[16,4,128]{2,1,0:T(4,128)} %bitcast.5), calls=%async_computation.1 | async-start | bytes 65536 | tf_op jit(solution)/shard_map/all_to_all | solution.py:108
  60.6 0.0 collective-permute-done.3
  60.6 0.0 collective-permute-done.2
  60.6 1.9 %collective-permute-start.5 = (bf16[2048,128]{1,0:T(8,128)(2,1)S(1)}, bf16[2048,128]{1,0:T(8,128)(2,1)S(1)}, u32[]{:S(2)}, u32[]{:S(2)}) collective-permute-start(bf16[2048,128]{1,0:T(8,128)(2,1)S(1)} %constant_dynamic-update-slice_fusion.own_ref), channel_id=1, source_target_pairs={{0,1},{1,0},{2,3},{3,2},{4,5},{5,4},{6,7},{7,6},{8,9},{9,8},{10,11... | collective-permute-start | bytes 1572872 | tf_op jit(solution)/shard_map/ppermute | solution.py:118
  62.6 0.0 copy-done.1
  62.6 0.8 %shard_map.60.part_ref = f32[128,128]{1,0:T(8,128)S(1)} custom-call(s32[2]{0:T(128)S(1)} %pad_add_fusion.place_ref, bf16[128,4096]{1,0:T(8,128)(2,1)S(1)} %copy-done.1, bf16[2048,128]{1,0:T(8,128)(2,1)S(1)} %constant_dynamic-update-slice_fusion.own_ref), custom_call_target="tpu_custom_call" | custom-call | flops 99999997952 | bytes 1048576 | tf_op jit(solution)/shard_map/pallas_call | solution.py:110
  63.4 9.8 %all-to-all-done.1 = f32[16,4,128]{2,1,0:T(4,128)S(1)} async-done(((f32[16,4,128]{2,1,0:T(4,128)}), f32[16,4,128]{2,1,0:T(4,128)S(1)}, u32[]{:S(2)}, u32[]{:S(2)}) %all-to-all-start.1) | async-done | bytes 32800 | tf_op jit(solution)/shard_map/all_to_all | solution.py:108
  73.2 0.6 reduce_sum.22
  73.8 0.0 collective-permute-done.5.other_ref
  73.8 1.5 %shard_map.61 = bf16[128,128]{1,0:T(8,128)(2,1)} custom-call(s32[2]{0:T(128)S(1)} %pad_add_fusion.place_ref, bf16[128,4096]{1,0:T(8,128)(2,1)S(1)} %copy-done.1, bf16[2048,128]{1,0:T(8,128)(2,1)S(1)} %collective-permute-done.5.other_ref, f32[128,128]{1,0:T(8,128)S(1)} %shard_map.60.part_ref), custom_call_target="tpu_custom_call" | custom-call | flops 67108864 | bytes 1048576 | tf_op jit(solution)/shard_map/pallas_call | solution.py:119
  (8 shorter events, 0.1 us)
Async XLA Ops:
  0.6 1.2 %copy-start = (bf16[128,4096]{1,0:T(8,128)(2,1)S(1)}, bf16[128,4096]{1,0:T(8,128)(2,1)}, u32[]{:S(2)}) copy-start(bf16[128,4096]{1,0:T(8,128)(2,1)} %act_ref.3) | copy-start | bytes 3145732
  1.9 0.8 %copy-start.2 = (bf16[128,128]{1,0:T(8,128)(2,1)S(1)}, bf16[128,128]{1,0:T(8,128)(2,1)}, u32[]{:S(2)}) copy-start(bf16[128,128]{1,0:T(8,128)(2,1)} %refs_2_.1) | copy-start | bytes 98308
  2.6 2.5 %copy-start.3 = (bf16[1,256,128]{2,1,0:T(8,128)(2,1)S(1)}, bf16[1,256,128]{2,1,0:T(8,128)(2,1)}, u32[]{:S(2)}) copy-start(bf16[1,256,128]{2,1,0:T(8,128)(2,1)} %param.5) | copy-start | bytes 196612
  3.1 2.0 %copy-start.4 = (f32[1,128]{1,0:T(1,128)S(1)}, f32[1,128]{1,0:T(1,128)}, u32[]{:S(2)}) copy-start(f32[1,128]{1,0:T(1,128)} %param.6) | copy-start | bytes 1540
  3.2 4.6 %collective-permute-start.4 = (f32[2048,128]{1,0:T(8,128)S(1)}, f32[2048,128]{1,0:T(8,128)S(1)}, u32[]{:S(2)}, u32[]{:S(2)}) collective-permute-start(f32[2048,128]{1,0:T(8,128)S(1)} %get-tuple-element.9), channel_id=1, source_target_pairs={{0,1},{1,0},{2,3},{3,2},{4,5},{5,4},{6,7},{7,6},{8,9},{9,8},{10,11... | collective-permute-start | bytes 3145736 | tf_op jit(solution)/shard_map/ppermute | solution.py:100
  8.6 41.7 %all-to-all-start = ((bf16[32,64,128]{2,1,0:T(8,128)(2,1)}), bf16[32,64,128]{2,1,0:T(8,128)(2,1)S(1)}, u32[]{:S(2)}, u32[]{:S(2)}) async-start(bf16[32,64,128]{2,1,0:T(8,128)(2,1)} %bitcast.4), calls=%async_computation | async-start | bytes 1048576 | tf_op jit(solution)/shard_map/all_to_all | solution.py:103
  25.3 19.7 %collective-permute-start.1 = (bf16[256,128]{1,0:T(8,128)(2,1)S(1)}, bf16[256,128]{1,0:T(8,128)(2,1)S(1)}, u32[]{:S(2)}, u32[]{:S(2)}) collective-permute-start(bf16[256,128]{1,0:T(8,128)(2,1)S(1)} %get-tuple-element.13), channel_id=1, source_target_pairs={{74,0},{76,2},{78,4},{0,6},{2,8},{4,10},{6,12},{8,14},{10,64},{12,... | collective-permute-start | bytes 196616 | tf_op jit(solution)/shard_map/ppermute | solution.py:72
  27.3 15.9 %collective-permute-start = (bf16[256,128]{1,0:T(8,128)(2,1)S(1)}, bf16[256,128]{1,0:T(8,128)(2,1)S(1)}, u32[]{:S(2)}, u32[]{:S(2)}) collective-permute-start(bf16[256,128]{1,0:T(8,128)(2,1)S(1)} %get-tuple-element.13), channel_id=1, source_target_pairs={{6,0},{8,2},{10,4},{12,6},{14,8},{64,10},{66,12},{68,14},{70,64},{... | collective-permute-start | bytes 196616 | tf_op jit(solution)/shard_map/ppermute | solution.py:72
  39.1 23.5 %copy-start.1 = (bf16[128,4096]{1,0:T(8,128)(2,1)S(1)}, bf16[128,4096]{1,0:T(8,128)(2,1)}, u32[]{:S(2)}) copy-start(bf16[128,4096]{1,0:T(8,128)(2,1)} %act_ref.3) | copy-start | bytes 3145732
  43.1 17.4 %collective-permute-start.3 = (bf16[512,128]{1,0:T(8,128)(2,1)S(1)}, bf16[512,128]{1,0:T(8,128)(2,1)S(1)}, u32[]{:S(2)}, u32[]{:S(2)}) collective-permute-start(bf16[512,128]{1,0:T(8,128)(2,1)S(1)} %pad_maximum_fusion.1), channel_id=1, source_target_pairs={{78,0},{0,2},{2,4},{4,6},{6,8},{8,10},{10,12},{12,14},{14,64},{64,... | collective-permute-start | bytes 393224 | tf_op jit(solution)/shard_map/ppermute | solution.py:72
  45.1 15.5 %collective-permute-start.2 = (bf16[768,128]{1,0:T(8,128)(2,1)S(1)}, bf16[768,128]{1,0:T(8,128)(2,1)S(1)}, u32[]{:S(2)}, u32[]{:S(2)}) collective-permute-start(bf16[768,128]{1,0:T(8,128)(2,1)S(1)} %pad_maximum_fusion), channel_id=1, source_target_pairs={{2,0},{4,2},{6,4},{8,6},{10,8},{12,10},{14,12},{64,14},{66,64},{68... | collective-permute-start | bytes 589832 | tf_op jit(solution)/shard_map/ppermute | solution.py:72
  51.0 22.2 %all-to-all-start.1 = ((f32[16,4,128]{2,1,0:T(4,128)}), f32[16,4,128]{2,1,0:T(4,128)S(1)}, u32[]{:S(2)}, u32[]{:S(2)}) async-start(f32[16,4,128]{2,1,0:T(4,128)} %bitcast.5), calls=%async_computation.1 | async-start | bytes 65536 | tf_op jit(solution)/shard_map/all_to_all | solution.py:108
  60.6 13.1 %collective-permute-start.5 = (bf16[2048,128]{1,0:T(8,128)(2,1)S(1)}, bf16[2048,128]{1,0:T(8,128)(2,1)S(1)}, u32[]{:S(2)}, u32[]{:S(2)}) collective-permute-start(bf16[2048,128]{1,0:T(8,128)(2,1)S(1)} %constant_dynamic-update-slice_fusion.own_ref), channel_id=1, source_target_pairs={{0,1},{1,0},{2,3},{3,2},{4,5},{5,4},{6,7},{7,6},{8,9},{9,8},{10,11... | collective-permute-start | bytes 1572872 | tf_op jit(solution)/shard_map/ppermute | solution.py:118

commit v6 on v5

--- a/solution.py
+++ b/solution.py
@@ -31,7 +31,7 @@
             even, odd = tiles[:, 0], tiles[:, 1]
             zero = jnp.where(low, even, pltpu.roll(odd, share, 1))
             one = jnp.where(low, pltpu.roll(even, share, 1), odd)
-            at = pl.ds(((outer // ZH * X + x) * ZH + outer % ZH) * half, half)
+            at = pl.ds((x * Y * ZH + outer) * half, half)
             keep_ref[at, :] = jnp.where(first, zero, one).reshape(half, -1)
             send_ref[at, :] = jnp.where(first, one, zero).reshape(half, -1)
 
@@ -95,14 +95,17 @@
         compiler_params=params,
         cost_estimate=pl.CostEstimate(flops=2 * 128 * width * head, bytes_accessed=3 << 20, transcendentals=0),
     )(core, activations, cotangent)
-    held = jnp.concatenate([own, along_z(own, FIRST), along_z(own, -FIRST)])
+    far = along_z(own, FIRST), along_z(own, -FIRST)
     keep, _ = lax.optimization_barrier((keep, own))
-    chip = keep + lax.ppermute(send, "core", swap)
-    chip = chip.astype(jnp.bfloat16)
+    chip = (keep + lax.ppermute(send, "core", swap)).astype(jnp.bfloat16)
+    got = lax.all_to_all(chip, "x", 0, 0, tiled=True)
+    line = got.reshape(X, rows // X, head).astype(jnp.float32).sum(0).astype(jnp.bfloat16)
+    *far, _ = lax.optimization_barrier((*far, line))
+    held = jnp.concatenate([own, *far])
     ahead, back = along_z(held, SECOND), along_z(held[: 2 * own.shape[0]], -SECOND)
-    got = lax.all_to_all(chip, ("y", "x"), 0, 0, tiled=True)
+    got = lax.all_to_all(line, "y", 0, 0, tiled=True)
     peers = ZH * ZL
-    line = got.reshape(Y * X, peers, rows // (Y * X * peers), head).astype(jnp.float32).sum(0)
+    line = got.reshape(Y, peers, rows // (X * Y * peers), head).astype(jnp.float32).sum(0)
     ahead, back, _ = lax.optimization_barrier((ahead, back, line))
     own = jnp.concatenate([held, ahead, back])
     weight_grad = lax.all_to_all(line, ("zh", "zl"), 0, 0, tiled=True).sum(0)

time: 75.8 us -> 78.5 us (1.036)
  waiting for transfers between devices: 16.4 us -> 22 us
  starting transfers between devices: 50.8 us -> 47.2 us
    all_to_all x1 -> x2, starting transfers between devices: 16.7 us -> 24.4 us  [the longest x1 16.6 us: on_device(): got = lax.all_to_all(chip, 'x', 0, 0, tiled=True)]
    ppermute x4, starting transfers between devices: 20.7 us -> 14.2 us  [along_z(): return lax.ppermute(value, ('zh', 'zl'), pairs)]
    all_to_all x1, starting transfers between devices: 9.57 us -> 4.82 us  [on_device(): weight_grad = lax.all_to_all(line, ('zh', 'zl'), 0, 0, tiled=True).sum(0)]
    all_to_all x1 -> x2, waiting for transfers between devices: 0.01 us -> 3.34 us  [the longest x1 3.15 us: on_device(): got = lax.all_to_all(line, 'y', 0, 0, tiled=True)]
    ppermute x4, waiting for transfers between devices: 4.05 us -> 6.35 us  [along_z(): return lax.ppermute(value, ('zh', 'zl'), pairs)]
  transfers between devices with their start and end apart: 8 -> 9, of which waited for: 3 -> 6; matrix products, arithmetic and copies ran while one was open for 2% -> 3% of each run, Pallas kernels for 1% -> 1%
where the time goes in v6:
time: 78.5 us; the launch traced here: 77.9 us
  starting transfers between devices  47.2 us (60%)
  waiting for transfers between devices  22 us (28%)
  other arithmetic  2.99 us (4%)
  Pallas kernels  2.79 us (4%)
  local copies, waits for them, and re-layouts  2.07 us (3%)
  between operations  0.82 us (1%)
    all_to_all x1, starting transfers between devices, on_device(): got = lax.all_to_all(chip, 'x', 0, 0, tiled=True)  16.6 us
    ppermute x4, starting transfers between devices, along_z(): return lax.ppermute(value, ('zh', 'zl'), pairs)  14.2 us
    all_to_all x1, waiting for transfers between devices, on_device(): weight_grad = lax.all_to_all(line, ('zh', 'zl'), 0, 0, tiled=True).sum(0)  9.77 us
    all_to_all x1, starting transfers between devices, on_device(): got = lax.all_to_all(line, 'y', 0, 0, tiled=True)  7.75 us
    ppermute x4, waiting for transfers between devices, along_z(): return lax.ppermute(value, ('zh', 'zl'), pairs)  6.35 us
    all_to_all x1, starting transfers between devices, on_device(): weight_grad = lax.all_to_all(line, ('zh', 'zl'), 0, 0, tiled=True).sum(0)  4.82 us
    all_to_all x1, waiting for transfers between devices, on_device(): got = lax.all_to_all(line, 'y', 0, 0, tiled=True)  3.15 us
    ppermute x1, waiting for transfers between devices, on_device(): chip = (keep + lax.ppermute(send, 'core', swap)).astype(jnp.bfloat16)  2.58 us
  transfers between devices with their start and end apart: 9, of which 6 were waited for; matrix products, arithmetic and copies ran while one was open for 3% of the time, Pallas kernels for 1%

profile of v6, /device:TPU:2, one launch (start us, length us, event | category | flops | bytes accessed | tf_op | source)
XLA Modules:
  0.0 77.9 jit_solution(2905335634489413526)
XLA Ops:
  0.6 0.0 copy-start
  0.6 1.2 %copy-done = bf16[128,4096]{1,0:T(8,128)(2,1)S(1)} copy-done((bf16[128,4096]{1,0:T(8,128)(2,1)S(1)}, bf16[128,4096]{1,0:T(8,128)(2,1)}, u32[]{:S(2)}) %copy-start) | copy-done | bytes 1048600
  1.9 0.8 copy-done.2
  2.6 0.5 shard_map.59
  3.1 0.0 copy-start.4
  3.2 1.9 %collective-permute-start.2 = (f32[2048,128]{1,0:T(8,128)S(1)}, f32[2048,128]{1,0:T(8,128)S(1)}, u32[]{:S(2)}, u32[]{:S(2)}) collective-permute-start(f32[2048,128]{1,0:T(8,128)S(1)} %get-tuple-element.11), channel_id=1, source_target_pairs={{0,1},{1,0},{2,3},{3,2},{4,5},{5,4},{6,7},{7,6},{8,9},{9,8},{10,11... | collective-permute-start | bytes 3145736 | tf_op jit(solution)/shard_map/ppermute | solution.py:100
  5.1 0.0 copy-done.3
  5.1 2.6 %collective-permute-done.2 = f32[2048,128]{1,0:T(8,128)S(1)} collective-permute-done((f32[2048,128]{1,0:T(8,128)S(1)}, f32[2048,128]{1,0:T(8,128)S(1)}, u32[]{:S(2)}, u32[]{:S(2)}) %collective-permute-start.2) | collective-permute-done | bytes 1048608 | tf_op jit(solution)/shard_map/ppermute | solution.py:100
  7.7 0.9 %add_convert_fusion = bf16[2048,128]{1,0:T(8,128)(2,1)} fusion(f32[2048,128]{1,0:T(8,128)S(1)} %get-tuple-element.10, f32[2048,128]{1,0:T(8,128)S(1)} %collective-permute-done.2), kind=kLoop, calls=%fused_computation | loop fusion | flops 524288 | bytes 2621440 | tf_op jit(solution)/shard_map/convert_element_type | solution.py:100
  8.6 16.6 %all-to-all-start = ((bf16[4,512,128]{2,1,0:T(8,128)(2,1)}), bf16[4,512,128]{2,1,0:T(8,128)(2,1)S(1)}, u32[]{:S(2)}, u32[]{:S(2)}) async-start(bf16[4,512,128]{2,1,0:T(8,128)(2,1)} %bitcast.4), calls=%async_computation | async-start | bytes 1048576 | tf_op jit(solution)/shard_map/all_to_all | solution.py:101
  25.2 6.4 %collective-permute-start = (bf16[256,128]{1,0:T(8,128)(2,1)S(1)}, bf16[256,128]{1,0:T(8,128)(2,1)S(1)}, u32[]{:S(2)}, u32[]{:S(2)}) collective-permute-start(bf16[256,128]{1,0:T(8,128)(2,1)S(1)} %get-tuple-element.17), channel_id=1, source_target_pairs={{6,0},{8,2},{10,4},{12,6},{14,8},{64,10},{66,12},{68,14},{70,64},{... | collective-permute-start | bytes 196616 | tf_op jit(solution)/shard_map/ppermute | solution.py:72
  31.6 1.9 %collective-permute-start.1 = (bf16[256,128]{1,0:T(8,128)(2,1)S(1)}, bf16[256,128]{1,0:T(8,128)(2,1)S(1)}, u32[]{:S(2)}, u32[]{:S(2)}) collective-permute-start(bf16[256,128]{1,0:T(8,128)(2,1)S(1)} %get-tuple-element.17), channel_id=1, source_target_pairs={{74,0},{76,2},{78,4},{0,6},{2,8},{4,10},{6,12},{8,14},{10,64},{12,... | collective-permute-start | bytes 196616 | tf_op jit(solution)/shard_map/ppermute | solution.py:72
  33.6 0.1 pad_add_fusion.place_ref
  33.6 0.2 all-to-all-done
  33.8 0.7 reduce_sum.32
  34.6 1.2 %collective-permute-done = bf16[256,128]{1,0:T(8,128)(2,1)S(1)} collective-permute-done((bf16[256,128]{1,0:T(8,128)(2,1)S(1)}, bf16[256,128]{1,0:T(8,128)(2,1)S(1)}, u32[]{:S(2)}, u32[]{:S(2)}) %collective-permute-start) | collective-permute-done | bytes 65568 | tf_op jit(solution)/shard_map/ppermute | solution.py:72
  35.7 5.2 %collective-permute-done.1 = bf16[256,128]{1,0:T(8,128)(2,1)S(1)} collective-permute-done((bf16[256,128]{1,0:T(8,128)(2,1)S(1)}, bf16[256,128]{1,0:T(8,128)(2,1)S(1)}, u32[]{:S(2)}, u32[]{:S(2)}) %collective-permute-start.1) | collective-permute-done | bytes 65568 | tf_op jit(solution)/shard_map/ppermute | solution.py:72
  40.9 7.7 %all-to-all-start.1 = ((bf16[8,64,128]{2,1,0:T(8,128)(2,1)}), bf16[8,64,128]{2,1,0:T(8,128)(2,1)S(1)}, u32[]{:S(2)}, u32[]{:S(2)}) async-start(bf16[8,64,128]{2,1,0:T(8,128)(2,1)} %bitcast.5), calls=%async_computation.1 | async-start | bytes 262144 | tf_op jit(solution)/shard_map/all_to_all | solution.py:106
  48.7 2.6 %collective-permute-start.3 = (bf16[768,128]{1,0:T(8,128)(2,1)S(1)}, bf16[768,128]{1,0:T(8,128)(2,1)S(1)}, u32[]{:S(2)}, u32[]{:S(2)}) collective-permute-start(bf16[768,128]{1,0:T(8,128)(2,1)S(1)} %pad_maximum_fusion), channel_id=1, source_target_pairs={{2,0},{4,2},{6,4},{8,6},{10,8},{12,10},{14,12},{64,14},{66,64},{68... | collective-permute-start | bytes 589832 | tf_op jit(solution)/shard_map/ppermute | solution.py:72
  51.3 3.3 %collective-permute-start.4 = (bf16[512,128]{1,0:T(8,128)(2,1)S(1)}, bf16[512,128]{1,0:T(8,128)(2,1)S(1)}, u32[]{:S(2)}, u32[]{:S(2)}) collective-permute-start(bf16[512,128]{1,0:T(8,128)(2,1)S(1)} %pad_maximum_fusion.1), channel_id=1, source_target_pairs={{78,0},{0,2},{2,4},{4,6},{6,8},{8,10},{10,12},{12,14},{14,64},{64,... | collective-permute-start | bytes 393224 | tf_op jit(solution)/shard_map/ppermute | solution.py:72
  54.6 3.1 %all-to-all-done.1 = bf16[8,64,128]{2,1,0:T(8,128)(2,1)S(1)} async-done(((bf16[8,64,128]{2,1,0:T(8,128)(2,1)}), bf16[8,64,128]{2,1,0:T(8,128)(2,1)S(1)}, u32[]{:S(2)}, u32[]{:S(2)}) %all-to-all-start.1) | async-done | bytes 131104 | tf_op jit(solution)/shard_map/all_to_all | solution.py:106
  57.7 0.6 convert_reduce_fusion
  58.4 4.8 %all-to-all-start.2 = ((f32[16,4,128]{2,1,0:T(4,128)}), f32[16,4,128]{2,1,0:T(4,128)S(1)}, u32[]{:S(2)}, u32[]{:S(2)}) async-start(f32[16,4,128]{2,1,0:T(4,128)} %bitcast.6), calls=%async_computation.2 | async-start | bytes 65536 | tf_op jit(solution)/shard_map/all_to_all | solution.py:111
  63.2 0.0 collective-permute-done.4
  63.2 0.0 collective-permute-done.3
  63.3 1.9 %collective-permute-start.5 = (bf16[2048,128]{1,0:T(8,128)(2,1)S(1)}, bf16[2048,128]{1,0:T(8,128)(2,1)S(1)}, u32[]{:S(2)}, u32[]{:S(2)}) collective-permute-start(bf16[2048,128]{1,0:T(8,128)(2,1)S(1)} %constant_dynamic-update-slice_fusion.own_ref), channel_id=1, source_target_pairs={{0,1},{1,0},{2,3},{3,2},{4,5},{5,4},{6,7},{7,6},{8,9},{9,8},{10,11... | collective-permute-start | bytes 1572872 | tf_op jit(solution)/shard_map/ppermute | solution.py:121
  65.2 0.0 copy-done.1
  65.2 0.8 %shard_map.60.part_ref = f32[128,128]{1,0:T(8,128)S(1)} custom-call(s32[2]{0:T(128)S(1)} %pad_add_fusion.place_ref, bf16[128,4096]{1,0:T(8,128)(2,1)S(1)} %copy-done.1, bf16[2048,128]{1,0:T(8,128)(2,1)S(1)} %constant_dynamic-update-slice_fusion.own_ref), custom_call_target="tpu_custom_call" | custom-call | flops 99999997952 | bytes 1048576 | tf_op jit(solution)/shard_map/pallas_call | solution.py:113
  66.1 9.8 %all-to-all-done.2 = f32[16,4,128]{2,1,0:T(4,128)S(1)} async-done(((f32[16,4,128]{2,1,0:T(4,128)}), f32[16,4,128]{2,1,0:T(4,128)S(1)}, u32[]{:S(2)}, u32[]{:S(2)}) %all-to-all-start.2) | async-done | bytes 32800 | tf_op jit(solution)/shard_map/all_to_all | solution.py:111
  75.8 0.6 reduce_sum.35
  76.4 0.0 collective-permute-done.5.other_ref
  76.4 1.5 %shard_map.61 = bf16[128,128]{1,0:T(8,128)(2,1)} custom-call(s32[2]{0:T(128)S(1)} %pad_add_fusion.place_ref, bf16[128,4096]{1,0:T(8,128)(2,1)S(1)} %copy-done.1, bf16[2048,128]{1,0:T(8,128)(2,1)S(1)} %collective-permute-done.5.other_ref, f32[128,128]{1,0:T(8,128)S(1)} %shard_map.60.part_ref), custom_call_target="tpu_custom_call" | custom-call | flops 67108864 | bytes 1048576 | tf_op jit(solution)/shard_map/pallas_call | solution.py:122
  (11 shorter events, 0.1 us)
Async XLA Ops:
  0.6 1.2 %copy-start = (bf16[128,4096]{1,0:T(8,128)(2,1)S(1)}, bf16[128,4096]{1,0:T(8,128)(2,1)}, u32[]{:S(2)}) copy-start(bf16[128,4096]{1,0:T(8,128)(2,1)} %act_ref.3) | copy-start | bytes 3145732
  1.9 0.8 copy-start.2
  2.6 2.5 %copy-start.3 = (bf16[1,256,128]{2,1,0:T(8,128)(2,1)S(1)}, bf16[1,256,128]{2,1,0:T(8,128)(2,1)}, u32[]{:S(2)}) copy-start(bf16[1,256,128]{2,1,0:T(8,128)(2,1)} %param.5) | copy-start | bytes 196612
  3.1 2.0 %copy-start.4 = (f32[1,128]{1,0:T(1,128)S(1)}, f32[1,128]{1,0:T(1,128)}, u32[]{:S(2)}) copy-start(f32[1,128]{1,0:T(1,128)} %param.6) | copy-start | bytes 1540
  3.2 4.6 %collective-permute-start.2 = (f32[2048,128]{1,0:T(8,128)S(1)}, f32[2048,128]{1,0:T(8,128)S(1)}, u32[]{:S(2)}, u32[]{:S(2)}) collective-permute-start(f32[2048,128]{1,0:T(8,128)S(1)} %get-tuple-element.11), channel_id=1, source_target_pairs={{0,1},{1,0},{2,3},{3,2},{4,5},{5,4},{6,7},{7,6},{8,9},{9,8},{10,11... | collective-permute-start | bytes 3145736 | tf_op jit(solution)/shard_map/ppermute | solution.py:100
  8.6 25.2 %all-to-all-start = ((bf16[4,512,128]{2,1,0:T(8,128)(2,1)}), bf16[4,512,128]{2,1,0:T(8,128)(2,1)S(1)}, u32[]{:S(2)}, u32[]{:S(2)}) async-start(bf16[4,512,128]{2,1,0:T(8,128)(2,1)} %bitcast.4), calls=%async_computation | async-start | bytes 1048576 | tf_op jit(solution)/shard_map/all_to_all | solution.py:101
  25.2 10.5 %collective-permute-start = (bf16[256,128]{1,0:T(8,128)(2,1)S(1)}, bf16[256,128]{1,0:T(8,128)(2,1)S(1)}, u32[]{:S(2)}, u32[]{:S(2)}) collective-permute-start(bf16[256,128]{1,0:T(8,128)(2,1)S(1)} %get-tuple-element.17), channel_id=1, source_target_pairs={{6,0},{8,2},{10,4},{12,6},{14,8},{64,10},{66,12},{68,14},{70,64},{... | collective-permute-start | bytes 196616 | tf_op jit(solution)/shard_map/ppermute | solution.py:72
  31.6 9.3 %collective-permute-start.1 = (bf16[256,128]{1,0:T(8,128)(2,1)S(1)}, bf16[256,128]{1,0:T(8,128)(2,1)S(1)}, u32[]{:S(2)}, u32[]{:S(2)}) collective-permute-start(bf16[256,128]{1,0:T(8,128)(2,1)S(1)} %get-tuple-element.17), channel_id=1, source_target_pairs={{74,0},{76,2},{78,4},{0,6},{2,8},{4,10},{6,12},{8,14},{10,64},{12,... | collective-permute-start | bytes 196616 | tf_op jit(solution)/shard_map/ppermute | solution.py:72
  34.6 30.6 %copy-start.1 = (bf16[128,4096]{1,0:T(8,128)(2,1)S(1)}, bf16[128,4096]{1,0:T(8,128)(2,1)}, u32[]{:S(2)}) copy-start(bf16[128,4096]{1,0:T(8,128)(2,1)} %act_ref.3) | copy-start | bytes 3145732
  40.9 16.8 %all-to-all-start.1 = ((bf16[8,64,128]{2,1,0:T(8,128)(2,1)}), bf16[8,64,128]{2,1,0:T(8,128)(2,1)S(1)}, u32[]{:S(2)}, u32[]{:S(2)}) async-start(bf16[8,64,128]{2,1,0:T(8,128)(2,1)} %bitcast.5), calls=%async_computation.1 | async-start | bytes 262144 | tf_op jit(solution)/shard_map/all_to_all | solution.py:106
  48.7 14.5 %collective-permute-start.3 = (bf16[768,128]{1,0:T(8,128)(2,1)S(1)}, bf16[768,128]{1,0:T(8,128)(2,1)S(1)}, u32[]{:S(2)}, u32[]{:S(2)}) collective-permute-start(bf16[768,128]{1,0:T(8,128)(2,1)S(1)} %pad_maximum_fusion), channel_id=1, source_target_pairs={{2,0},{4,2},{6,4},{8,6},{10,8},{12,10},{14,12},{64,14},{66,64},{68... | collective-permute-start | bytes 589832 | tf_op jit(solution)/shard_map/ppermute | solution.py:72
  51.3 11.9 %collective-permute-start.4 = (bf16[512,128]{1,0:T(8,128)(2,1)S(1)}, bf16[512,128]{1,0:T(8,128)(2,1)S(1)}, u32[]{:S(2)}, u32[]{:S(2)}) collective-permute-start(bf16[512,128]{1,0:T(8,128)(2,1)S(1)} %pad_maximum_fusion.1), channel_id=1, source_target_pairs={{78,0},{0,2},{2,4},{4,6},{6,8},{8,10},{10,12},{12,14},{14,64},{64,... | collective-permute-start | bytes 393224 | tf_op jit(solution)/shard_map/ppermute | solution.py:72
  58.4 17.5 %all-to-all-start.2 = ((f32[16,4,128]{2,1,0:T(4,128)}), f32[16,4,128]{2,1,0:T(4,128)S(1)}, u32[]{:S(2)}, u32[]{:S(2)}) async-start(f32[16,4,128]{2,1,0:T(4,128)} %bitcast.6), calls=%async_computation.2 | async-start | bytes 65536 | tf_op jit(solution)/shard_map/all_to_all | solution.py:111
  63.3 13.2 %collective-permute-start.5 = (bf16[2048,128]{1,0:T(8,128)(2,1)S(1)}, bf16[2048,128]{1,0:T(8,128)(2,1)S(1)}, u32[]{:S(2)}, u32[]{:S(2)}) collective-permute-start(bf16[2048,128]{1,0:T(8,128)(2,1)S(1)} %constant_dynamic-update-slice_fusion.own_ref), channel_id=1, source_target_pairs={{0,1},{1,0},{2,3},{3,2},{4,5},{5,4},{6,7},{7,6},{8,9},{9,8},{10,11... | collective-permute-start | bytes 1572872 | tf_op jit(solution)/shard_map/ppermute | solution.py:121

commit v7 on v4

--- a/solution.py
+++ b/solution.py
@@ -33,7 +33,7 @@
             one = jnp.where(low, pltpu.roll(even, share, 1), odd)
             at = pl.ds(((outer // ZH * X + x) * ZH + outer % ZH) * half, half)
             keep_ref[at, :] = jnp.where(first, zero, one).reshape(half, -1)
-            send_ref[at, :] = jnp.where(first, one, zero).reshape(half, -1)
+            send_ref[at, :] = jnp.where(first, one, zero).reshape(half, -1).astype(send_ref.dtype)
 
 
 def gather_order():
@@ -81,14 +81,17 @@
     rows = width // CORE
     keep, send = pl.pallas_call(
         lambda *refs: term_kernel(float(tokens) ** (-0.5), *refs),
-        out_shape=[jax.ShapeDtypeStruct((rows, head), jnp.float32)] * 2,
+        out_shape=[
+            jax.ShapeDtypeStruct((rows, head), jnp.float32),
+            jax.ShapeDtypeStruct((rows, head), jnp.bfloat16),
+        ],
         in_specs=[smem, vmem, vmem],
         out_specs=[vmem, vmem],
         compiler_params=params,
         cost_estimate=pl.CostEstimate(flops=2 * 128 * width * head, bytes_accessed=3 << 20, transcendentals=0),
     )(core, activations, cotangent)
     held = jnp.concatenate([own, along_z(own, FIRST), along_z(own, -FIRST)])
-    chip = keep + lax.ppermute(send, "core", swap)
+    chip = keep + lax.ppermute(send, "core", swap).astype(jnp.float32)
     chip = chip.astype(jnp.bfloat16)
     two = 2 * own.shape[0]
     own = jnp.concatenate([held, along_z(held, SECOND), along_z(held[:two], -SECOND)])

time: 74.8 us -> 74.8 us (level)
  starting transfers between devices: 45.4 us -> 46.9 us
  waiting for transfers between devices: 21.5 us -> 20 us
    ppermute x4, waiting for transfers between devices: 11.7 us -> 10.2 us  [along_z(): return lax.ppermute(value, ('zh', 'zl'), pairs)]
    ppermute x4, starting transfers between devices: 12.4 us -> 13.7 us  [along_z(): return lax.ppermute(value, ('zh', 'zl'), pairs)]
where the time goes in v7:
time: 74.8 us; the launch traced here: 74.3 us
  starting transfers between devices  46.9 us (63%)
  waiting for transfers between devices  20 us (27%)
  other arithmetic  2.34 us (3%)
  Pallas kernels  2.12 us (3%)
  local copies, waits for them, and re-layouts  2.07 us (3%)
  between operations  0.83 us (1%)
    ppermute x1, starting transfers between devices, on_device(): chip = keep + lax.ppermute(send, 'core', swap).astype(jnp.float32)  16.1 us
    ppermute x4, starting transfers between devices, along_z(): return lax.ppermute(value, ('zh', 'zl'), pairs)  13.7 us
    ppermute x4, waiting for transfers between devices, along_z(): return lax.ppermute(value, ('zh', 'zl'), pairs)  10.2 us
    all_to_all x1, waiting for transfers between devices, on_device(): weight_grad = lax.all_to_all(line, ('zh', 'zl'), 0, 0, tiled=True).sum(0)  9.8 us
    all_to_all x1, starting transfers between devices, on_device(): got = lax.all_to_all(chip, ('y', 'x'), 0, 0, tiled=True)  9.66 us
    all_to_all x1, starting transfers between devices, on_device(): weight_grad = lax.all_to_all(line, ('zh', 'zl'), 0, 0, tiled=True).sum(0)  4.37 us
    ppermute x1, starting transfers between devices, on_device(): other = lax.ppermute(own, 'core', swap)  3.1 us
    unnamed x13, local copies, waits for them, and re-layouts  2.05 us
  transfers between devices with their start and end apart: 8, of which 3 were waited for; matrix products, arithmetic and copies ran while one was open for 2% of the time, Pallas kernels for 2%

profile of v7, /device:TPU:1, one launch (start us, length us, event | category | flops | bytes accessed | tf_op | source)
XLA Modules:
  0.0 74.3 jit_solution(5229602082437294255)
XLA Ops:
  0.6 0.0 copy-start
  0.6 1.2 %copy-done = bf16[128,4096]{1,0:T(8,128)(2,1)S(1)} copy-done((bf16[128,4096]{1,0:T(8,128)(2,1)S(1)}, bf16[128,4096]{1,0:T(8,128)(2,1)}, u32[]{:S(2)}) %copy-start) | copy-done | bytes 1048600
  1.9 0.0 copy-start.2
  1.9 0.8 %copy-done.2 = bf16[128,128]{1,0:T(8,128)(2,1)S(1)} copy-done((bf16[128,128]{1,0:T(8,128)(2,1)S(1)}, bf16[128,128]{1,0:T(8,128)(2,1)}, u32[]{:S(2)}) %copy-start.2) | copy-done | bytes 32792
  2.6 0.0 copy-start.3
  2.6 0.5 shard_map.60
  3.2 0.0 copy-start.4
  3.2 16.1 %collective-permute-start.5 = (bf16[2048,128]{1,0:T(8,128)(2,1)S(1)}, bf16[2048,128]{1,0:T(8,128)(2,1)S(1)}, u32[]{:S(2)}, u32[]{:S(2)}) collective-permute-start(bf16[2048,128]{1,0:T(8,128)(2,1)S(1)} %get-tuple-element.5), channel_id=1, source_target_pairs={{0,1},{1,0},{2,3},{3,2},{4,5},{5,4},{6,7},{7,6},{8,9},{9,8},{10,11... | collective-permute-start | bytes 1572872 | tf_op jit(solution)/shard_map/ppermute | solution.py:94
  19.2 0.0 copy-done.3
  19.3 0.0 copy-done.4
  19.3 5.3 %collective-permute-start = (bf16[256,128]{1,0:T(8,128)(2,1)S(1)}, bf16[256,128]{1,0:T(8,128)(2,1)S(1)}, u32[]{:S(2)}, u32[]{:S(2)}) collective-permute-start(bf16[256,128]{1,0:T(8,128)(2,1)S(1)} %get-tuple-element.7), channel_id=1, source_target_pairs={{6,0},{8,2},{10,4},{12,6},{14,8},{64,10},{66,12},{68,14},{70,64},{... | collective-permute-start | bytes 196616 | tf_op jit(solution)/shard_map/ppermute | solution.py:64
  24.6 0.0 collective-permute-done.5
  24.6 0.9 %add_convert_fusion = bf16[2048,128]{1,0:T(8,128)(2,1)} fusion(f32[2048,128]{1,0:T(8,128)S(1)} %get-tuple-element.4, bf16[2048,128]{1,0:T(8,128)(2,1)S(1)} %collective-permute-done.5), kind=kLoop, calls=%fused_computation.1 | loop fusion | flops 786432 | bytes 2097152 | tf_op jit(solution)/shard_map/convert_element_type | solution.py:95
  25.5 9.7 %all-to-all-start = ((bf16[32,64,128]{2,1,0:T(8,128)(2,1)}), bf16[32,64,128]{2,1,0:T(8,128)(2,1)S(1)}, u32[]{:S(2)}, u32[]{:S(2)}) async-start(bf16[32,64,128]{2,1,0:T(8,128)(2,1)} %bitcast.4), calls=%async_computation | async-start | bytes 1048576 | tf_op jit(solution)/shard_map/all_to_all | solution.py:98
  35.2 0.0 copy-start.1
  35.2 2.1 %collective-permute-start.1 = (bf16[256,128]{1,0:T(8,128)(2,1)S(1)}, bf16[256,128]{1,0:T(8,128)(2,1)S(1)}, u32[]{:S(2)}, u32[]{:S(2)}) collective-permute-start(bf16[256,128]{1,0:T(8,128)(2,1)S(1)} %get-tuple-element.7), channel_id=1, source_target_pairs={{74,0},{76,2},{78,4},{0,6},{2,8},{4,10},{6,12},{8,14},{10,64},{12,... | collective-permute-start | bytes 196616 | tf_op jit(solution)/shard_map/ppermute | solution.py:64
  37.3 0.0 collective-permute-done
  37.3 3.1 %collective-permute-start.3 = (bf16[512,128]{1,0:T(8,128)(2,1)S(1)}, bf16[512,128]{1,0:T(8,128)(2,1)S(1)}, u32[]{:S(2)}, u32[]{:S(2)}) collective-permute-start(bf16[512,128]{1,0:T(8,128)(2,1)S(1)} %pad_maximum_fusion.1), channel_id=1, source_target_pairs={{78,0},{0,2},{2,4},{4,6},{6,8},{8,10},{10,12},{12,14},{14,64},{64,... | collective-permute-start | bytes 393224 | tf_op jit(solution)/shard_map/ppermute | solution.py:64
  40.4 4.0 %collective-permute-done.1 = bf16[256,128]{1,0:T(8,128)(2,1)S(1)} collective-permute-done((bf16[256,128]{1,0:T(8,128)(2,1)S(1)}, bf16[256,128]{1,0:T(8,128)(2,1)S(1)}, u32[]{:S(2)}, u32[]{:S(2)}) %collective-permute-start.1) | collective-permute-done | bytes 65568 | tf_op jit(solution)/shard_map/ppermute | solution.py:64
  44.4 3.3 %collective-permute-start.2 = (bf16[768,128]{1,0:T(8,128)(2,1)S(1)}, bf16[768,128]{1,0:T(8,128)(2,1)S(1)}, u32[]{:S(2)}, u32[]{:S(2)}) collective-permute-start(bf16[768,128]{1,0:T(8,128)(2,1)S(1)} %pad_maximum_fusion), channel_id=1, source_target_pairs={{2,0},{4,2},{6,4},{8,6},{10,8},{12,10},{14,12},{64,14},{66,64},{68... | collective-permute-start | bytes 589832 | tf_op jit(solution)/shard_map/ppermute | solution.py:64
  47.7 6.2 %collective-permute-done.2 = bf16[768,128]{1,0:T(8,128)(2,1)S(1)} collective-permute-done((bf16[768,128]{1,0:T(8,128)(2,1)S(1)}, bf16[768,128]{1,0:T(8,128)(2,1)S(1)}, u32[]{:S(2)}, u32[]{:S(2)}) %collective-permute-start.2) | collective-permute-done | bytes 196640 | tf_op jit(solution)/shard_map/ppermute | solution.py:64
  54.0 0.0 collective-permute-done.3
  54.0 3.1 %collective-permute-start.4 = (bf16[2048,128]{1,0:T(8,128)(2,1)S(1)}, bf16[2048,128]{1,0:T(8,128)(2,1)S(1)}, u32[]{:S(2)}, u32[]{:S(2)}) collective-permute-start(bf16[2048,128]{1,0:T(8,128)(2,1)S(1)} %constant_dynamic-update-slice_fusion.own_ref), channel_id=1, source_target_pairs={{0,1},{1,0},{2,3},{3,2},{4,5},{5,4},{6,7},{7,6},{8,9},{9,8},{10,11... | collective-permute-start | bytes 1572872 | tf_op jit(solution)/shard_map/ppermute | solution.py:103
  57.1 0.0 all-to-all-done
  57.1 0.7 convert_reduce_fusion
  57.8 4.4 %all-to-all-start.1 = ((f32[16,4,128]{2,1,0:T(4,128)}), f32[16,4,128]{2,1,0:T(4,128)S(1)}, u32[]{:S(2)}, u32[]{:S(2)}) async-start(f32[16,4,128]{2,1,0:T(4,128)} %bitcast.5), calls=%async_computation.1 | async-start | bytes 65536 | tf_op jit(solution)/shard_map/all_to_all | solution.py:101
  62.2 0.1 pad_add_fusion.place_ref
  62.3 0.0 collective-permute-done.4.other_ref
  62.3 0.0 copy-done.1
  62.3 1.6 %shard_map.59 = bf16[128,128]{1,0:T(8,128)(2,1)} custom-call(s32[2]{0:T(128)S(1)} %pad_add_fusion.place_ref, bf16[128,4096]{1,0:T(8,128)(2,1)S(1)} %copy-done.1, bf16[2048,128]{1,0:T(8,128)(2,1)S(1)} %constant_dynamic-update-slice_fusion.own_ref, bf16[2048,128]{1,0:T(8,128)(2,1)S(1)} %collective-permute-done.4.other_ref), custom_call_target="tpu_custom_call" | custom-call | flops 134217728 | bytes 2097152 | tf_op jit(solution)/shard_map/pallas_call | solution.py:104
  63.9 9.8 %all-to-all-done.1 = f32[16,4,128]{2,1,0:T(4,128)S(1)} async-done(((f32[16,4,128]{2,1,0:T(4,128)}), f32[16,4,128]{2,1,0:T(4,128)S(1)}, u32[]{:S(2)}, u32[]{:S(2)}) %all-to-all-start.1) | async-done | bytes 32800 | tf_op jit(solution)/shard_map/all_to_all | solution.py:101
  73.7 0.6 reduce_sum.22
  (7 shorter events, 0.1 us)
Async XLA Ops:
  0.6 1.2 %copy-start = (bf16[128,4096]{1,0:T(8,128)(2,1)S(1)}, bf16[128,4096]{1,0:T(8,128)(2,1)}, u32[]{:S(2)}) copy-start(bf16[128,4096]{1,0:T(8,128)(2,1)} %refs_1_.1) | copy-start | bytes 3145732
  1.9 0.8 %copy-start.2 = (bf16[128,128]{1,0:T(8,128)(2,1)S(1)}, bf16[128,128]{1,0:T(8,128)(2,1)}, u32[]{:S(2)}) copy-start(bf16[128,128]{1,0:T(8,128)(2,1)} %refs_2_.1) | copy-start | bytes 98308
  2.6 16.6 %copy-start.3 = (bf16[1,256,128]{2,1,0:T(8,128)(2,1)S(1)}, bf16[1,256,128]{2,1,0:T(8,128)(2,1)}, u32[]{:S(2)}) copy-start(bf16[1,256,128]{2,1,0:T(8,128)(2,1)} %param.5) | copy-start | bytes 196612
  3.2 16.1 %copy-start.4 = (f32[1,128]{1,0:T(1,128)S(1)}, f32[1,128]{1,0:T(1,128)}, u32[]{:S(2)}) copy-start(f32[1,128]{1,0:T(1,128)} %param.6) | copy-start | bytes 1540
  3.2 21.4 %collective-permute-start.5 = (bf16[2048,128]{1,0:T(8,128)(2,1)S(1)}, bf16[2048,128]{1,0:T(8,128)(2,1)S(1)}, u32[]{:S(2)}, u32[]{:S(2)}) collective-permute-start(bf16[2048,128]{1,0:T(8,128)(2,1)S(1)} %get-tuple-element.5), channel_id=1, source_target_pairs={{0,1},{1,0},{2,3},{3,2},{4,5},{5,4},{6,7},{7,6},{8,9},{9,8},{10,11... | collective-permute-start | bytes 1572872 | tf_op jit(solution)/shard_map/ppermute | solution.py:94
  19.3 18.0 %collective-permute-start = (bf16[256,128]{1,0:T(8,128)(2,1)S(1)}, bf16[256,128]{1,0:T(8,128)(2,1)S(1)}, u32[]{:S(2)}, u32[]{:S(2)}) collective-permute-start(bf16[256,128]{1,0:T(8,128)(2,1)S(1)} %get-tuple-element.7), channel_id=1, source_target_pairs={{6,0},{8,2},{10,4},{12,6},{14,8},{64,10},{66,12},{68,14},{70,64},{... | collective-permute-start | bytes 196616 | tf_op jit(solution)/shard_map/ppermute | solution.py:64
  25.5 31.6 %all-to-all-start = ((bf16[32,64,128]{2,1,0:T(8,128)(2,1)}), bf16[32,64,128]{2,1,0:T(8,128)(2,1)S(1)}, u32[]{:S(2)}, u32[]{:S(2)}) async-start(bf16[32,64,128]{2,1,0:T(8,128)(2,1)} %bitcast.4), calls=%async_computation | async-start | bytes 1048576 | tf_op jit(solution)/shard_map/all_to_all | solution.py:98
  35.2 27.1 %copy-start.1 = (bf16[128,4096]{1,0:T(8,128)(2,1)S(1)}, bf16[128,4096]{1,0:T(8,128)(2,1)}, u32[]{:S(2)}) copy-start(bf16[128,4096]{1,0:T(8,128)(2,1)} %refs_1_.1) | copy-start | bytes 3145732
  35.2 9.2 %collective-permute-start.1 = (bf16[256,128]{1,0:T(8,128)(2,1)S(1)}, bf16[256,128]{1,0:T(8,128)(2,1)S(1)}, u32[]{:S(2)}, u32[]{:S(2)}) collective-permute-start(bf16[256,128]{1,0:T(8,128)(2,1)S(1)} %get-tuple-element.7), channel_id=1, source_target_pairs={{74,0},{76,2},{78,4},{0,6},{2,8},{4,10},{6,12},{8,14},{10,64},{12,... | collective-permute-start | bytes 196616 | tf_op jit(solution)/shard_map/ppermute | solution.py:64
  37.3 16.7 %collective-permute-start.3 = (bf16[512,128]{1,0:T(8,128)(2,1)S(1)}, bf16[512,128]{1,0:T(8,128)(2,1)S(1)}, u32[]{:S(2)}, u32[]{:S(2)}) collective-permute-start(bf16[512,128]{1,0:T(8,128)(2,1)S(1)} %pad_maximum_fusion.1), channel_id=1, source_target_pairs={{78,0},{0,2},{2,4},{4,6},{6,8},{8,10},{10,12},{12,14},{14,64},{64,... | collective-permute-start | bytes 393224 | tf_op jit(solution)/shard_map/ppermute | solution.py:64
  44.4 9.5 %collective-permute-start.2 = (bf16[768,128]{1,0:T(8,128)(2,1)S(1)}, bf16[768,128]{1,0:T(8,128)(2,1)S(1)}, u32[]{:S(2)}, u32[]{:S(2)}) collective-permute-start(bf16[768,128]{1,0:T(8,128)(2,1)S(1)} %pad_maximum_fusion), channel_id=1, source_target_pairs={{2,0},{4,2},{6,4},{8,6},{10,8},{12,10},{14,12},{64,14},{66,64},{68... | collective-permute-start | bytes 589832 | tf_op jit(solution)/shard_map/ppermute | solution.py:64
  54.0 8.3 %collective-permute-start.4 = (bf16[2048,128]{1,0:T(8,128)(2,1)S(1)}, bf16[2048,128]{1,0:T(8,128)(2,1)S(1)}, u32[]{:S(2)}, u32[]{:S(2)}) collective-permute-start(bf16[2048,128]{1,0:T(8,128)(2,1)S(1)} %constant_dynamic-update-slice_fusion.own_ref), channel_id=1, source_target_pairs={{0,1},{1,0},{2,3},{3,2},{4,5},{5,4},{6,7},{7,6},{8,9},{9,8},{10,11... | collective-permute-start | bytes 1572872 | tf_op jit(solution)/shard_map/ppermute | solution.py:103
  57.8 15.9 %all-to-all-start.1 = ((f32[16,4,128]{2,1,0:T(4,128)}), f32[16,4,128]{2,1,0:T(4,128)S(1)}, u32[]{:S(2)}, u32[]{:S(2)}) async-start(f32[16,4,128]{2,1,0:T(4,128)} %bitcast.5), calls=%async_computation.1 | async-start | bytes 65536 | tf_op jit(solution)/shard_map/all_to_all | solution.py:101

commit v8 on v5

--- a/solution.py
+++ b/solution.py
@@ -7,18 +7,29 @@
 
 Y, ZH, X, ZL, CORE = 8, 2, 4, 8, 2
 AXES = ("y", "zh", "x", "zl", "core")
+CHUNKS = 4
 FIRST, SECOND = 3, 1
 
 
-def term_kernel(scale, core_ref, act_ref, cot_ref, keep_ref, send_ref):
+def term_kernel(scale, core_ref, act_hbm, cot_hbm, keep_ref, send_ref, act_ref, cot_ref, sems):
     first = core_ref[0] == 0
     share = 4
     per = act_ref.shape[1] // (Y * ZH)
     sub = per // X
     half = sub // 2
+    wide = act_ref.shape[1] // CHUNKS
+    copies = [pltpu.make_async_copy(cot_hbm, cot_ref, sems.at[CHUNKS])]
+    for chunk in range(CHUNKS):
+        at = pl.ds(chunk * wide, wide)
+        copies.append(pltpu.make_async_copy(act_hbm.at[:, at], act_ref.at[:, at], sems.at[chunk]))
+    for copy in copies:
+        copy.start()
+    copies[0].wait()
     cot = cot_ref[...]
     low = lax.broadcasted_iota(jnp.int32, (sub // 16, 8, cot.shape[1]), 1) < share
     for outer in range(Y * ZH):
+        if outer * per % wide == 0:
+            copies[1 + outer * per // wide].wait()
         part = lax.dot_general(
             act_ref[:, outer * per : (outer + 1) * per],
             cot,
@@ -78,6 +89,7 @@
     tokens = activations.shape[0] * Y * ZH * X * ZL * CORE
     vmem = pl.BlockSpec(memory_space=pltpu.VMEM)
     smem = pl.BlockSpec(memory_space=pltpu.SMEM)
+    hbm = pl.BlockSpec(memory_space=pltpu.HBM)
     params = pltpu.CompilerParams(vmem_limit_bytes=32 * 1024 * 1024)
     core = lax.axis_index("core").reshape(1).astype(jnp.int32)
     place = jnp.concatenate([lax.axis_index("zl").reshape(1).astype(jnp.int32), core])
@@ -90,21 +102,24 @@
     keep, send = pl.pallas_call(
         lambda *refs: term_kernel(float(tokens) ** (-0.5), *refs),
         out_shape=[jax.ShapeDtypeStruct((rows, head), jnp.float32)] * 2,
-        in_specs=[smem, vmem, vmem],
+        in_specs=[smem, hbm, hbm],
         out_specs=[vmem, vmem],
-        compiler_params=params,
+        scratch_shapes=[
+            pltpu.VMEM(activations.shape, activations.dtype),
+            pltpu.VMEM(cotangent.shape, cotangent.dtype),
+            pltpu.SemaphoreType.DMA((CHUNKS + 1,)),
+        ],
+        compiler_params=pltpu.CompilerParams(vmem_limit_bytes=56 * 1024 * 1024),
         cost_estimate=pl.CostEstimate(flops=2 * 128 * width * head, bytes_accessed=3 << 20, transcendentals=0),
     )(core, activations, cotangent)
     held = jnp.concatenate([own, along_z(own, FIRST), along_z(own, -FIRST)])
-    keep, _ = lax.optimization_barrier((keep, own))
     chip = keep + lax.ppermute(send, "core", swap)
     chip = chip.astype(jnp.bfloat16)
-    ahead, back = along_z(held, SECOND), along_z(held[: 2 * own.shape[0]], -SECOND)
+    two = 2 * own.shape[0]
+    own = jnp.concatenate([held, along_z(held, SECOND), along_z(held[:two], -SECOND)])
     got = lax.all_to_all(chip, ("y", "x"), 0, 0, tiled=True)
     peers = ZH * ZL
     line = got.reshape(Y * X, peers, rows // (Y * X * peers), head).astype(jnp.float32).sum(0)
-    ahead, back, _ = lax.optimization_barrier((ahead, back, line))
-    own = jnp.concatenate([held, ahead, back])
     weight_grad = lax.all_to_all(line, ("zh", "zl"), 0, 0, tiled=True).sum(0)
 
     part = pl.pallas_call(
@@ -113,7 +128,7 @@
         in_specs=[smem, vmem, vmem],
         out_specs=vmem,
         compiler_params=params,
-        cost_estimate=pl.CostEstimate(flops=10**11, bytes_accessed=1 << 20, transcendentals=0),
+        cost_estimate=pl.CostEstimate(flops=128 * width * head, bytes_accessed=1 << 20, transcendentals=0),
     )(place, activations, own)
     other = lax.ppermute(own, "core", swap)
     values_out = pl.pallas_call(

time: 75.8 us -> 76.9 us (1.015)
  the two profiles are of different devices: /device:TPU:2 before, /device:TPU:1 now
where the time goes in v8:
time: 76.9 us; the launch traced here: 76.5 us
  starting transfers between devices  45.4 us (59%)
  waiting for transfers between devices  20.9 us (27%)
  Pallas kernels  5.73 us (7%)
  other arithmetic  3.57 us (5%)
  between operations  0.84 us (1%)
    ppermute x1, starting transfers between devices, on_device(): chip = keep + lax.ppermute(send, 'core', swap)  16.1 us
    ppermute x4, starting transfers between devices, along_z(): return lax.ppermute(value, ('zh', 'zl'), pairs)  12.4 us
    ppermute x4, waiting for transfers between devices, along_z(): return lax.ppermute(value, ('zh', 'zl'), pairs)  11.7 us
    all_to_all x1, starting transfers between devices, on_device(): got = lax.all_to_all(chip, ('y', 'x'), 0, 0, tiled=True)  9.67 us
    all_to_all x1, waiting for transfers between devices, on_device(): weight_grad = lax.all_to_all(line, ('zh', 'zl'), 0, 0, tiled=True).sum(0)  9.1 us
    all_to_all x1, starting transfers between devices, on_device(): weight_grad = lax.all_to_all(line, ('zh', 'zl'), 0, 0, tiled=True).sum(0)  4.19 us
    pallas_call x1, Pallas kernels, on_device(): pl.pallas_call(lambda *refs: term_kernel(float(tokens) ** (-0.5), *refs),...  3.45 us
    ppermute x1, starting transfers between devices, on_device(): other = lax.ppermute(own, 'core', swap)  3.09 us
  transfers between devices with their start and end apart: 8, of which 3 were waited for; matrix products, arithmetic and copies ran while one was open for 4% of the time, Pallas kernels for 3%

profile of v8, /device:TPU:1, one launch (start us, length us, event | category | flops | bytes accessed | tf_op | source)
XLA Modules:
  0.0 76.5 jit_solution(17106854757448054580)
XLA Ops:
  0.6 0.0 copy-start.1
  0.6 3.5 %shard_map.61 = (f32[2048,128]{1,0:T(8,128)}, f32[2048,128]{1,0:T(8,128)}) custom-call(s32[1]{0:T(128)} %bitcast.1.refs_0_, bf16[128,4096]{1,0:T(8,128)(2,1)} %refs_1_.1, bf16[128,128]{1,0:T(8,128)(2,1)} %refs_2_.1), custom_call_target="tpu_custom_call" | custom-call | flops 134217728 | bytes 3145728 | tf_op jit(solution)/shard_map/pallas_call | solution.py:102
  4.1 0.0 copy-start.2
  4.1 16.1 %collective-permute-start.5 = (f32[2048,128]{1,0:T(8,128)}, f32[2048,128]{1,0:T(8,128)S(1)}, u32[]{:S(2)}, u32[]{:S(2)}) collective-permute-start(f32[2048,128]{1,0:T(8,128)} %get-tuple-element.5), channel_id=1, source_target_pairs={{0,1},{1,0},{2,3},{3,2},{4,5},{5,4},{6,7},{7,6},{8,9},{9,8},{10,11... | collective-permute-start | bytes 3145736 | tf_op jit(solution)/shard_map/ppermute | solution.py:116
  20.2 0.0 copy-done.1
  20.2 0.0 copy-done.2
  20.2 5.3 %collective-permute-start = (bf16[256,128]{1,0:T(8,128)(2,1)S(1)}, bf16[256,128]{1,0:T(8,128)(2,1)S(1)}, u32[]{:S(2)}, u32[]{:S(2)}) collective-permute-start(bf16[256,128]{1,0:T(8,128)(2,1)S(1)} %get-tuple-element.7), channel_id=1, source_target_pairs={{6,0},{8,2},{10,4},{12,6},{14,8},{64,10},{66,12},{68,14},{70,64},{... | collective-permute-start | bytes 196616 | tf_op jit(solution)/shard_map/ppermute | solution.py:83
  25.5 0.0 collective-permute-done.5
  25.5 2.2 %add_convert_fusion = bf16[2048,128]{1,0:T(8,128)(2,1)} fusion(f32[2048,128]{1,0:T(8,128)} %get-tuple-element.4, f32[2048,128]{1,0:T(8,128)S(1)} %collective-permute-done.5), kind=kLoop, calls=%fused_computation.1 | loop fusion | flops 524288 | bytes 2621440 | tf_op jit(solution)/shard_map/convert_element_type | solution.py:117
  27.7 9.7 %all-to-all-start = ((bf16[32,64,128]{2,1,0:T(8,128)(2,1)}), bf16[32,64,128]{2,1,0:T(8,128)(2,1)S(1)}, u32[]{:S(2)}, u32[]{:S(2)}) async-start(bf16[32,64,128]{2,1,0:T(8,128)(2,1)} %bitcast.4), calls=%async_computation | async-start | bytes 1048576 | tf_op jit(solution)/shard_map/all_to_all | solution.py:120
  37.4 0.0 copy-start
  37.4 2.1 %collective-permute-start.1 = (bf16[256,128]{1,0:T(8,128)(2,1)S(1)}, bf16[256,128]{1,0:T(8,128)(2,1)S(1)}, u32[]{:S(2)}, u32[]{:S(2)}) collective-permute-start(bf16[256,128]{1,0:T(8,128)(2,1)S(1)} %get-tuple-element.7), channel_id=1, source_target_pairs={{74,0},{76,2},{78,4},{0,6},{2,8},{4,10},{6,12},{8,14},{10,64},{12,... | collective-permute-start | bytes 196616 | tf_op jit(solution)/shard_map/ppermute | solution.py:83
  39.4 0.0 collective-permute-done
  39.5 3.1 %collective-permute-start.3 = (bf16[512,128]{1,0:T(8,128)(2,1)S(1)}, bf16[512,128]{1,0:T(8,128)(2,1)S(1)}, u32[]{:S(2)}, u32[]{:S(2)}) collective-permute-start(bf16[512,128]{1,0:T(8,128)(2,1)S(1)} %pad_maximum_fusion.1), channel_id=1, source_target_pairs={{78,0},{0,2},{2,4},{4,6},{6,8},{8,10},{10,12},{12,14},{14,64},{64,... | collective-permute-start | bytes 393224 | tf_op jit(solution)/shard_map/ppermute | solution.py:83
  42.6 4.5 %collective-permute-done.1 = bf16[256,128]{1,0:T(8,128)(2,1)S(1)} collective-permute-done((bf16[256,128]{1,0:T(8,128)(2,1)S(1)}, bf16[256,128]{1,0:T(8,128)(2,1)S(1)}, u32[]{:S(2)}, u32[]{:S(2)}) %collective-permute-start.1) | collective-permute-done | bytes 65568 | tf_op jit(solution)/shard_map/ppermute | solution.py:83
  47.1 1.9 %collective-permute-start.2 = (bf16[768,128]{1,0:T(8,128)(2,1)S(1)}, bf16[768,128]{1,0:T(8,128)(2,1)S(1)}, u32[]{:S(2)}, u32[]{:S(2)}) collective-permute-start(bf16[768,128]{1,0:T(8,128)(2,1)S(1)} %pad_maximum_fusion), channel_id=1, source_target_pairs={{2,0},{4,2},{6,4},{8,6},{10,8},{12,10},{14,12},{64,14},{66,64},{68... | collective-permute-start | bytes 589832 | tf_op jit(solution)/shard_map/ppermute | solution.py:83
  49.1 7.2 %collective-permute-done.2 = bf16[768,128]{1,0:T(8,128)(2,1)S(1)} collective-permute-done((bf16[768,128]{1,0:T(8,128)(2,1)S(1)}, bf16[768,128]{1,0:T(8,128)(2,1)S(1)}, u32[]{:S(2)}, u32[]{:S(2)}) %collective-permute-start.2) | collective-permute-done | bytes 196640 | tf_op jit(solution)/shard_map/ppermute | solution.py:83
  56.3 0.0 collective-permute-done.3
  56.4 3.1 %collective-permute-start.4 = (bf16[2048,128]{1,0:T(8,128)(2,1)S(1)}, bf16[2048,128]{1,0:T(8,128)(2,1)S(1)}, u32[]{:S(2)}, u32[]{:S(2)}) collective-permute-start(bf16[2048,128]{1,0:T(8,128)(2,1)S(1)} %constant_dynamic-update-slice_fusion.own_ref), channel_id=1, source_target_pairs={{0,1},{1,0},{2,3},{3,2},{4,5},{5,4},{6,7},{7,6},{8,9},{9,8},{10,11... | collective-permute-start | bytes 1572872 | tf_op jit(solution)/shard_map/ppermute | solution.py:133
  59.5 0.0 all-to-all-done
  59.5 0.7 convert_reduce_fusion
  60.2 4.2 %all-to-all-start.1 = ((f32[16,4,128]{2,1,0:T(4,128)}), f32[16,4,128]{2,1,0:T(4,128)S(1)}, u32[]{:S(2)}, u32[]{:S(2)}) async-start(f32[16,4,128]{2,1,0:T(4,128)} %bitcast.5), calls=%async_computation.1 | async-start | bytes 65536 | tf_op jit(solution)/shard_map/all_to_all | solution.py:123
  64.4 0.1 pad_add_fusion.place_ref
  64.5 0.0 copy-done
  64.5 0.8 %shard_map.59.part_ref = f32[128,128]{1,0:T(8,128)S(1)} custom-call(s32[2]{0:T(128)S(1)} %pad_add_fusion.place_ref, bf16[128,4096]{1,0:T(8,128)(2,1)S(1)} %copy-done, bf16[2048,128]{1,0:T(8,128)(2,1)S(1)} %constant_dynamic-update-slice_fusion.own_ref), custom_call_target="tpu_custom_call" | custom-call | flops 67108864 | bytes 1048576 | tf_op jit(solution)/shard_map/pallas_call | solution.py:125
  65.3 0.0 collective-permute-done.4.other_ref
  65.3 1.4 %shard_map.60 = bf16[128,128]{1,0:T(8,128)(2,1)} custom-call(s32[2]{0:T(128)S(1)} %pad_add_fusion.place_ref, bf16[128,4096]{1,0:T(8,128)(2,1)S(1)} %copy-done, bf16[2048,128]{1,0:T(8,128)(2,1)S(1)} %collective-permute-done.4.other_ref, f32[128,128]{1,0:T(8,128)S(1)} %shard_map.59.part_ref), custom_call_target="tpu_custom_call" | custom-call | flops 67108864 | bytes 1048576 | tf_op jit(solution)/shard_map/pallas_call | solution.py:134
  66.8 9.1 %all-to-all-done.1 = f32[16,4,128]{2,1,0:T(4,128)S(1)} async-done(((f32[16,4,128]{2,1,0:T(4,128)}), f32[16,4,128]{2,1,0:T(4,128)S(1)}, u32[]{:S(2)}, u32[]{:S(2)}) %all-to-all-start.1) | async-done | bytes 32800 | tf_op jit(solution)/shard_map/all_to_all | solution.py:123
  75.8 0.6 reduce_sum.22
  (7 shorter events, 0.1 us)
Async XLA Ops:
  0.6 19.6 %copy-start.1 = (bf16[1,256,128]{2,1,0:T(8,128)(2,1)S(1)}, bf16[1,256,128]{2,1,0:T(8,128)(2,1)}, u32[]{:S(2)}) copy-start(bf16[1,256,128]{2,1,0:T(8,128)(2,1)} %param.5) | copy-start | bytes 196612
  4.1 16.1 %copy-start.2 = (f32[1,128]{1,0:T(1,128)S(1)}, f32[1,128]{1,0:T(1,128)}, u32[]{:S(2)}) copy-start(f32[1,128]{1,0:T(1,128)} %param.6) | copy-start | bytes 1540
  4.1 21.4 %collective-permute-start.5 = (f32[2048,128]{1,0:T(8,128)}, f32[2048,128]{1,0:T(8,128)S(1)}, u32[]{:S(2)}, u32[]{:S(2)}) collective-permute-start(f32[2048,128]{1,0:T(8,128)} %get-tuple-element.5), channel_id=1, source_target_pairs={{0,1},{1,0},{2,3},{3,2},{4,5},{5,4},{6,7},{7,6},{8,9},{9,8},{10,11... | collective-permute-start | bytes 3145736 | tf_op jit(solution)/shard_map/ppermute | solution.py:116
  20.2 19.2 %collective-permute-start = (bf16[256,128]{1,0:T(8,128)(2,1)S(1)}, bf16[256,128]{1,0:T(8,128)(2,1)S(1)}, u32[]{:S(2)}, u32[]{:S(2)}) collective-permute-start(bf16[256,128]{1,0:T(8,128)(2,1)S(1)} %get-tuple-element.7), channel_id=1, source_target_pairs={{6,0},{8,2},{10,4},{12,6},{14,8},{64,10},{66,12},{68,14},{70,64},{... | collective-permute-start | bytes 196616 | tf_op jit(solution)/shard_map/ppermute | solution.py:83
  27.7 31.8 %all-to-all-start = ((bf16[32,64,128]{2,1,0:T(8,128)(2,1)}), bf16[32,64,128]{2,1,0:T(8,128)(2,1)S(1)}, u32[]{:S(2)}, u32[]{:S(2)}) async-start(bf16[32,64,128]{2,1,0:T(8,128)(2,1)} %bitcast.4), calls=%async_computation | async-start | bytes 1048576 | tf_op jit(solution)/shard_map/all_to_all | solution.py:120
  37.4 27.1 %copy-start = (bf16[128,4096]{1,0:T(8,128)(2,1)S(1)}, bf16[128,4096]{1,0:T(8,128)(2,1)}, u32[]{:S(2)}) copy-start(bf16[128,4096]{1,0:T(8,128)(2,1)} %refs_1_.1) | copy-start | bytes 3145732
  37.4 9.7 %collective-permute-start.1 = (bf16[256,128]{1,0:T(8,128)(2,1)S(1)}, bf16[256,128]{1,0:T(8,128)(2,1)S(1)}, u32[]{:S(2)}, u32[]{:S(2)}) collective-permute-start(bf16[256,128]{1,0:T(8,128)(2,1)S(1)} %get-tuple-element.7), channel_id=1, source_target_pairs={{74,0},{76,2},{78,4},{0,6},{2,8},{4,10},{6,12},{8,14},{10,64},{12,... | collective-permute-start | bytes 196616 | tf_op jit(solution)/shard_map/ppermute | solution.py:83
  39.5 16.9 %collective-permute-start.3 = (bf16[512,128]{1,0:T(8,128)(2,1)S(1)}, bf16[512,128]{1,0:T(8,128)(2,1)S(1)}, u32[]{:S(2)}, u32[]{:S(2)}) collective-permute-start(bf16[512,128]{1,0:T(8,128)(2,1)S(1)} %pad_maximum_fusion.1), channel_id=1, source_target_pairs={{78,0},{0,2},{2,4},{4,6},{6,8},{8,10},{10,12},{12,14},{14,64},{64,... | collective-permute-start | bytes 393224 | tf_op jit(solution)/shard_map/ppermute | solution.py:83
  47.1 9.2 %collective-permute-start.2 = (bf16[768,128]{1,0:T(8,128)(2,1)S(1)}, bf16[768,128]{1,0:T(8,128)(2,1)S(1)}, u32[]{:S(2)}, u32[]{:S(2)}) collective-permute-start(bf16[768,128]{1,0:T(8,128)(2,1)S(1)} %pad_maximum_fusion), channel_id=1, source_target_pairs={{2,0},{4,2},{6,4},{8,6},{10,8},{12,10},{14,12},{64,14},{66,64},{68... | collective-permute-start | bytes 589832 | tf_op jit(solution)/shard_map/ppermute | solution.py:83
  56.4 8.9 %collective-permute-start.4 = (bf16[2048,128]{1,0:T(8,128)(2,1)S(1)}, bf16[2048,128]{1,0:T(8,128)(2,1)S(1)}, u32[]{:S(2)}, u32[]{:S(2)}) collective-permute-start(bf16[2048,128]{1,0:T(8,128)(2,1)S(1)} %constant_dynamic-update-slice_fusion.own_ref), channel_id=1, source_target_pairs={{0,1},{1,0},{2,3},{3,2},{4,5},{5,4},{6,7},{7,6},{8,9},{9,8},{10,11... | collective-permute-start | bytes 1572872 | tf_op jit(solution)/shard_map/ppermute | solution.py:133
  60.2 15.7 %all-to-all-start.1 = ((f32[16,4,128]{2,1,0:T(4,128)}), f32[16,4,128]{2,1,0:T(4,128)S(1)}, u32[]{:S(2)}, u32[]{:S(2)}) async-start(f32[16,4,128]{2,1,0:T(4,128)} %bitcast.5), calls=%async_computation.1 | async-start | bytes 65536 | tf_op jit(solution)/shard_map/all_to_all | solution.py:123

commit v9 on v5

--- a/solution.py
+++ b/solution.py
@@ -96,15 +96,13 @@
         cost_estimate=pl.CostEstimate(flops=2 * 128 * width * head, bytes_accessed=3 << 20, transcendentals=0),
     )(core, activations, cotangent)
     held = jnp.concatenate([own, along_z(own, FIRST), along_z(own, -FIRST)])
-    keep, _ = lax.optimization_barrier((keep, own))
     chip = keep + lax.ppermute(send, "core", swap)
     chip = chip.astype(jnp.bfloat16)
-    ahead, back = along_z(held, SECOND), along_z(held[: 2 * own.shape[0]], -SECOND)
+    two = 2 * own.shape[0]
+    own = jnp.concatenate([held, along_z(held, SECOND), along_z(held[:two], -SECOND)])
     got = lax.all_to_all(chip, ("y", "x"), 0, 0, tiled=True)
     peers = ZH * ZL
     line = got.reshape(Y * X, peers, rows // (Y * X * peers), head).astype(jnp.float32).sum(0)
-    ahead, back, _ = lax.optimization_barrier((ahead, back, line))
-    own = jnp.concatenate([held, ahead, back])
     weight_grad = lax.all_to_all(line, ("zh", "zl"), 0, 0, tiled=True).sum(0)
 
     part = pl.pallas_call(
@@ -113,7 +111,7 @@
         in_specs=[smem, vmem, vmem],
         out_specs=vmem,
         compiler_params=params,
-        cost_estimate=pl.CostEstimate(flops=10**11, bytes_accessed=1 << 20, transcendentals=0),
+        cost_estimate=pl.CostEstimate(flops=128 * width * head, bytes_accessed=1 << 20, transcendentals=0),
     )(place, activations, own)
     other = lax.ppermute(own, "core", swap)
     values_out = pl.pallas_call(

time: 75.8 us -> 74.8 us (0.987)
  the two profiles are of different devices: /device:TPU:2 before, /device:TPU:1 now
where the time goes in v9:
time: 74.8 us; the launch traced here: 74.2 us
  starting transfers between devices  45.4 us (61%)
  waiting for transfers between devices  20.8 us (28%)
  Pallas kernels  2.79 us (4%)
  other arithmetic  2.31 us (3%)
  local copies, waits for them, and re-layouts  2.07 us (3%)
  between operations  0.84 us (1%)
    ppermute x1, starting transfers between devices, on_device(): chip = keep + lax.ppermute(send, 'core', swap)  16.1 us
    ppermute x4, starting transfers between devices, along_z(): return lax.ppermute(value, ('zh', 'zl'), pairs)  12.4 us
    ppermute x4, waiting for transfers between devices, along_z(): return lax.ppermute(value, ('zh', 'zl'), pairs)  11.7 us
    all_to_all x1, starting transfers between devices, on_device(): got = lax.all_to_all(chip, ('y', 'x'), 0, 0, tiled=True)  9.66 us
    all_to_all x1, waiting for transfers between devices, on_device(): weight_grad = lax.all_to_all(line, ('zh', 'zl'), 0, 0, tiled=True).sum(0)  9.09 us
    all_to_all x1, starting transfers between devices, on_device(): weight_grad = lax.all_to_all(line, ('zh', 'zl'), 0, 0, tiled=True).sum(0)  4.26 us
    ppermute x1, starting transfers between devices, on_device(): other = lax.ppermute(own, 'core', swap)  3.09 us
    unnamed x13, local copies, waits for them, and re-layouts  2.05 us
  transfers between devices with their start and end apart: 8, of which 3 were waited for; matrix products, arithmetic and copies ran while one was open for 2% of the time, Pallas kernels for 3%

profile of v9, /device:TPU:1, one launch (start us, length us, event | category | flops | bytes accessed | tf_op | source)
XLA Modules:
  0.0 74.2 jit_solution(7924713344789399400)
XLA Ops:
  0.6 0.0 copy-start
  0.6 1.2 %copy-done = bf16[128,4096]{1,0:T(8,128)(2,1)S(1)} copy-done((bf16[128,4096]{1,0:T(8,128)(2,1)S(1)}, bf16[128,4096]{1,0:T(8,128)(2,1)}, u32[]{:S(2)}) %copy-start) | copy-done | bytes 1048600
  1.9 0.0 copy-start.2
  1.9 0.8 %copy-done.2 = bf16[128,128]{1,0:T(8,128)(2,1)S(1)} copy-done((bf16[128,128]{1,0:T(8,128)(2,1)S(1)}, bf16[128,128]{1,0:T(8,128)(2,1)}, u32[]{:S(2)}) %copy-start.2) | copy-done | bytes 32792
  2.6 0.5 shard_map.61
  3.1 0.0 copy-start.4
  3.2 16.1 %collective-permute-start.5 = (f32[2048,128]{1,0:T(8,128)S(1)}, f32[2048,128]{1,0:T(8,128)S(1)}, u32[]{:S(2)}, u32[]{:S(2)}) collective-permute-start(f32[2048,128]{1,0:T(8,128)S(1)} %get-tuple-element.5), channel_id=1, source_target_pairs={{0,1},{1,0},{2,3},{3,2},{4,5},{5,4},{6,7},{7,6},{8,9},{9,8},{10,11... | collective-permute-start | bytes 3145736 | tf_op jit(solution)/shard_map/ppermute | solution.py:99
  19.2 0.0 copy-done.3
  19.2 0.0 copy-done.4
  19.3 5.3 %collective-permute-start = (bf16[256,128]{1,0:T(8,128)(2,1)S(1)}, bf16[256,128]{1,0:T(8,128)(2,1)S(1)}, u32[]{:S(2)}, u32[]{:S(2)}) collective-permute-start(bf16[256,128]{1,0:T(8,128)(2,1)S(1)} %get-tuple-element.7), channel_id=1, source_target_pairs={{6,0},{8,2},{10,4},{12,6},{14,8},{64,10},{66,12},{68,14},{70,64},{... | collective-permute-start | bytes 196616 | tf_op jit(solution)/shard_map/ppermute | solution.py:72
  24.6 0.0 collective-permute-done.5
  24.6 0.9 %add_convert_fusion = bf16[2048,128]{1,0:T(8,128)(2,1)} fusion(f32[2048,128]{1,0:T(8,128)S(1)} %get-tuple-element.4, f32[2048,128]{1,0:T(8,128)S(1)} %collective-permute-done.5), kind=kLoop, calls=%fused_computation.1 | loop fusion | flops 524288 | bytes 2621440 | tf_op jit(solution)/shard_map/convert_element_type | solution.py:100
  25.5 9.7 %all-to-all-start = ((bf16[32,64,128]{2,1,0:T(8,128)(2,1)}), bf16[32,64,128]{2,1,0:T(8,128)(2,1)S(1)}, u32[]{:S(2)}, u32[]{:S(2)}) async-start(bf16[32,64,128]{2,1,0:T(8,128)(2,1)} %bitcast.4), calls=%async_computation | async-start | bytes 1048576 | tf_op jit(solution)/shard_map/all_to_all | solution.py:103
  35.1 0.0 copy-start.1
  35.1 2.1 %collective-permute-start.1 = (bf16[256,128]{1,0:T(8,128)(2,1)S(1)}, bf16[256,128]{1,0:T(8,128)(2,1)S(1)}, u32[]{:S(2)}, u32[]{:S(2)}) collective-permute-start(bf16[256,128]{1,0:T(8,128)(2,1)S(1)} %get-tuple-element.7), channel_id=1, source_target_pairs={{74,0},{76,2},{78,4},{0,6},{2,8},{4,10},{6,12},{8,14},{10,64},{12,... | collective-permute-start | bytes 196616 | tf_op jit(solution)/shard_map/ppermute | solution.py:72
  37.2 0.0 collective-permute-done
  37.2 3.1 %collective-permute-start.3 = (bf16[512,128]{1,0:T(8,128)(2,1)S(1)}, bf16[512,128]{1,0:T(8,128)(2,1)S(1)}, u32[]{:S(2)}, u32[]{:S(2)}) collective-permute-start(bf16[512,128]{1,0:T(8,128)(2,1)S(1)} %pad_maximum_fusion.1), channel_id=1, source_target_pairs={{78,0},{0,2},{2,4},{4,6},{6,8},{8,10},{10,12},{12,14},{14,64},{64,... | collective-permute-start | bytes 393224 | tf_op jit(solution)/shard_map/ppermute | solution.py:72
  40.3 4.3 %collective-permute-done.1 = bf16[256,128]{1,0:T(8,128)(2,1)S(1)} collective-permute-done((bf16[256,128]{1,0:T(8,128)(2,1)S(1)}, bf16[256,128]{1,0:T(8,128)(2,1)S(1)}, u32[]{:S(2)}, u32[]{:S(2)}) %collective-permute-start.1) | collective-permute-done | bytes 65568 | tf_op jit(solution)/shard_map/ppermute | solution.py:72
  44.7 1.9 %collective-permute-start.2 = (bf16[768,128]{1,0:T(8,128)(2,1)S(1)}, bf16[768,128]{1,0:T(8,128)(2,1)S(1)}, u32[]{:S(2)}, u32[]{:S(2)}) collective-permute-start(bf16[768,128]{1,0:T(8,128)(2,1)S(1)} %pad_maximum_fusion), channel_id=1, source_target_pairs={{2,0},{4,2},{6,4},{8,6},{10,8},{12,10},{14,12},{64,14},{66,64},{68... | collective-permute-start | bytes 589832 | tf_op jit(solution)/shard_map/ppermute | solution.py:72
  46.6 7.4 %collective-permute-done.2 = bf16[768,128]{1,0:T(8,128)(2,1)S(1)} collective-permute-done((bf16[768,128]{1,0:T(8,128)(2,1)S(1)}, bf16[768,128]{1,0:T(8,128)(2,1)S(1)}, u32[]{:S(2)}, u32[]{:S(2)}) %collective-permute-start.2) | collective-permute-done | bytes 196640 | tf_op jit(solution)/shard_map/ppermute | solution.py:72
  54.0 0.0 collective-permute-done.3
  54.1 3.1 %collective-permute-start.4 = (bf16[2048,128]{1,0:T(8,128)(2,1)S(1)}, bf16[2048,128]{1,0:T(8,128)(2,1)S(1)}, u32[]{:S(2)}, u32[]{:S(2)}) collective-permute-start(bf16[2048,128]{1,0:T(8,128)(2,1)S(1)} %constant_dynamic-update-slice_fusion.own_ref), channel_id=1, source_target_pairs={{0,1},{1,0},{2,3},{3,2},{4,5},{5,4},{6,7},{7,6},{8,9},{9,8},{10,11... | collective-permute-start | bytes 1572872 | tf_op jit(solution)/shard_map/ppermute | solution.py:116
  57.2 0.0 all-to-all-done
  57.2 0.7 convert_reduce_fusion
  57.9 4.3 %all-to-all-start.1 = ((f32[16,4,128]{2,1,0:T(4,128)}), f32[16,4,128]{2,1,0:T(4,128)S(1)}, u32[]{:S(2)}, u32[]{:S(2)}) async-start(f32[16,4,128]{2,1,0:T(4,128)} %bitcast.5), calls=%async_computation.1 | async-start | bytes 65536 | tf_op jit(solution)/shard_map/all_to_all | solution.py:106
  62.1 0.1 pad_add_fusion.place_ref
  62.2 0.0 copy-done.1
  62.2 0.8 %shard_map.59.part_ref = f32[128,128]{1,0:T(8,128)S(1)} custom-call(s32[2]{0:T(128)S(1)} %pad_add_fusion.place_ref, bf16[128,4096]{1,0:T(8,128)(2,1)S(1)} %copy-done.1, bf16[2048,128]{1,0:T(8,128)(2,1)S(1)} %constant_dynamic-update-slice_fusion.own_ref), custom_call_target="tpu_custom_call" | custom-call | flops 67108864 | bytes 1048576 | tf_op jit(solution)/shard_map/pallas_call | solution.py:108
  63.1 0.0 collective-permute-done.4.other_ref
  63.1 1.4 %shard_map.60 = bf16[128,128]{1,0:T(8,128)(2,1)} custom-call(s32[2]{0:T(128)S(1)} %pad_add_fusion.place_ref, bf16[128,4096]{1,0:T(8,128)(2,1)S(1)} %copy-done.1, bf16[2048,128]{1,0:T(8,128)(2,1)S(1)} %collective-permute-done.4.other_ref, f32[128,128]{1,0:T(8,128)S(1)} %shard_map.59.part_ref), custom_call_target="tpu_custom_call" | custom-call | flops 67108864 | bytes 1048576 | tf_op jit(solution)/shard_map/pallas_call | solution.py:117
  64.5 9.1 %all-to-all-done.1 = f32[16,4,128]{2,1,0:T(4,128)S(1)} async-done(((f32[16,4,128]{2,1,0:T(4,128)}), f32[16,4,128]{2,1,0:T(4,128)S(1)}, u32[]{:S(2)}, u32[]{:S(2)}) %all-to-all-start.1) | async-done | bytes 32800 | tf_op jit(solution)/shard_map/all_to_all | solution.py:106
  73.6 0.6 reduce_sum.22
  (8 shorter events, 0.1 us)
Async XLA Ops:
  0.6 1.2 %copy-start = (bf16[128,4096]{1,0:T(8,128)(2,1)S(1)}, bf16[128,4096]{1,0:T(8,128)(2,1)}, u32[]{:S(2)}) copy-start(bf16[128,4096]{1,0:T(8,128)(2,1)} %refs_1_.1) | copy-start | bytes 3145732
  1.9 0.8 %copy-start.2 = (bf16[128,128]{1,0:T(8,128)(2,1)S(1)}, bf16[128,128]{1,0:T(8,128)(2,1)}, u32[]{:S(2)}) copy-start(bf16[128,128]{1,0:T(8,128)(2,1)} %refs_2_.1) | copy-start | bytes 98308
  2.6 16.6 %copy-start.3 = (bf16[1,256,128]{2,1,0:T(8,128)(2,1)S(1)}, bf16[1,256,128]{2,1,0:T(8,128)(2,1)}, u32[]{:S(2)}) copy-start(bf16[1,256,128]{2,1,0:T(8,128)(2,1)} %param.5) | copy-start | bytes 196612
  3.1 16.1 %copy-start.4 = (f32[1,128]{1,0:T(1,128)S(1)}, f32[1,128]{1,0:T(1,128)}, u32[]{:S(2)}) copy-start(f32[1,128]{1,0:T(1,128)} %param.6) | copy-start | bytes 1540
  3.2 21.4 %collective-permute-start.5 = (f32[2048,128]{1,0:T(8,128)S(1)}, f32[2048,128]{1,0:T(8,128)S(1)}, u32[]{:S(2)}, u32[]{:S(2)}) collective-permute-start(f32[2048,128]{1,0:T(8,128)S(1)} %get-tuple-element.5), channel_id=1, source_target_pairs={{0,1},{1,0},{2,3},{3,2},{4,5},{5,4},{6,7},{7,6},{8,9},{9,8},{10,11... | collective-permute-start | bytes 3145736 | tf_op jit(solution)/shard_map/ppermute | solution.py:99
  19.3 17.9 %collective-permute-start = (bf16[256,128]{1,0:T(8,128)(2,1)S(1)}, bf16[256,128]{1,0:T(8,128)(2,1)S(1)}, u32[]{:S(2)}, u32[]{:S(2)}) collective-permute-start(bf16[256,128]{1,0:T(8,128)(2,1)S(1)} %get-tuple-element.7), channel_id=1, source_target_pairs={{6,0},{8,2},{10,4},{12,6},{14,8},{64,10},{66,12},{68,14},{70,64},{... | collective-permute-start | bytes 196616 | tf_op jit(solution)/shard_map/ppermute | solution.py:72
  25.5 31.7 %all-to-all-start = ((bf16[32,64,128]{2,1,0:T(8,128)(2,1)}), bf16[32,64,128]{2,1,0:T(8,128)(2,1)S(1)}, u32[]{:S(2)}, u32[]{:S(2)}) async-start(bf16[32,64,128]{2,1,0:T(8,128)(2,1)} %bitcast.4), calls=%async_computation | async-start | bytes 1048576 | tf_op jit(solution)/shard_map/all_to_all | solution.py:103
  35.1 27.1 %copy-start.1 = (bf16[128,4096]{1,0:T(8,128)(2,1)S(1)}, bf16[128,4096]{1,0:T(8,128)(2,1)}, u32[]{:S(2)}) copy-start(bf16[128,4096]{1,0:T(8,128)(2,1)} %refs_1_.1) | copy-start | bytes 3145732
  35.1 9.5 %collective-permute-start.1 = (bf16[256,128]{1,0:T(8,128)(2,1)S(1)}, bf16[256,128]{1,0:T(8,128)(2,1)S(1)}, u32[]{:S(2)}, u32[]{:S(2)}) collective-permute-start(bf16[256,128]{1,0:T(8,128)(2,1)S(1)} %get-tuple-element.7), channel_id=1, source_target_pairs={{74,0},{76,2},{78,4},{0,6},{2,8},{4,10},{6,12},{8,14},{10,64},{12,... | collective-permute-start | bytes 196616 | tf_op jit(solution)/shard_map/ppermute | solution.py:72
  37.2 16.8 %collective-permute-start.3 = (bf16[512,128]{1,0:T(8,128)(2,1)S(1)}, bf16[512,128]{1,0:T(8,128)(2,1)S(1)}, u32[]{:S(2)}, u32[]{:S(2)}) collective-permute-start(bf16[512,128]{1,0:T(8,128)(2,1)S(1)} %pad_maximum_fusion.1), channel_id=1, source_target_pairs={{78,0},{0,2},{2,4},{4,6},{6,8},{8,10},{10,12},{12,14},{14,64},{64,... | collective-permute-start | bytes 393224 | tf_op jit(solution)/shard_map/ppermute | solution.py:72
  44.7 9.4 %collective-permute-start.2 = (bf16[768,128]{1,0:T(8,128)(2,1)S(1)}, bf16[768,128]{1,0:T(8,128)(2,1)S(1)}, u32[]{:S(2)}, u32[]{:S(2)}) collective-permute-start(bf16[768,128]{1,0:T(8,128)(2,1)S(1)} %pad_maximum_fusion), channel_id=1, source_target_pairs={{2,0},{4,2},{6,4},{8,6},{10,8},{12,10},{14,12},{64,14},{66,64},{68... | collective-permute-start | bytes 589832 | tf_op jit(solution)/shard_map/ppermute | solution.py:72
  54.1 9.0 %collective-permute-start.4 = (bf16[2048,128]{1,0:T(8,128)(2,1)S(1)}, bf16[2048,128]{1,0:T(8,128)(2,1)S(1)}, u32[]{:S(2)}, u32[]{:S(2)}) collective-permute-start(bf16[2048,128]{1,0:T(8,128)(2,1)S(1)} %constant_dynamic-update-slice_fusion.own_ref), channel_id=1, source_target_pairs={{0,1},{1,0},{2,3},{3,2},{4,5},{5,4},{6,7},{7,6},{8,9},{9,8},{10,11... | collective-permute-start | bytes 1572872 | tf_op jit(solution)/shard_map/ppermute | solution.py:116
  57.9 15.7 %all-to-all-start.1 = ((f32[16,4,128]{2,1,0:T(4,128)}), f32[16,4,128]{2,1,0:T(4,128)S(1)}, u32[]{:S(2)}, u32[]{:S(2)}) async-start(f32[16,4,128]{2,1,0:T(4,128)} %bitcast.5), calls=%async_computation.1 | async-start | bytes 65536 | tf_op jit(solution)/shard_map/all_to_all | solution.py:106

commit v10 on v4

--- a/solution.py
+++ b/solution.py
@@ -31,7 +31,7 @@
             even, odd = tiles[:, 0], tiles[:, 1]
             zero = jnp.where(low, even, pltpu.roll(odd, share, 1))
             one = jnp.where(low, pltpu.roll(even, share, 1), odd)
-            at = pl.ds(((outer // ZH * X + x) * ZH + outer % ZH) * half, half)
+            at = pl.ds((x * Y * ZH + outer) * half, half)
             keep_ref[at, :] = jnp.where(first, zero, one).reshape(half, -1)
             send_ref[at, :] = jnp.where(first, one, zero).reshape(half, -1)
 
@@ -92,7 +92,7 @@
     chip = chip.astype(jnp.bfloat16)
     two = 2 * own.shape[0]
     own = jnp.concatenate([held, along_z(held, SECOND), along_z(held[:two], -SECOND)])
-    got = lax.all_to_all(chip, ("y", "x"), 0, 0, tiled=True)
+    got = lax.all_to_all(chip, ("x", "y"), 0, 0, tiled=True)
     peers = ZH * ZL
     line = got.reshape(Y * X, peers, rows // (Y * X * peers), head).astype(jnp.float32).sum(0)
     weight_grad = lax.all_to_all(line, ("zh", "zl"), 0, 0, tiled=True).sum(0)

time: 74.8 us -> 74.8 us (level)
  no operation moved by 1% of the time
where the time goes in v10:
time: 74.8 us; the launch traced here: 74.2 us
  starting transfers between devices  45.4 us (61%)
  waiting for transfers between devices  21.5 us (29%)
  other arithmetic  2.31 us (3%)
  Pallas kernels  2.1 us (3%)
  local copies, waits for them, and re-layouts  2.07 us (3%)
  between operations  0.83 us (1%)
    ppermute x1, starting transfers between devices, on_device(): chip = keep + lax.ppermute(send, 'core', swap)  16.1 us
    ppermute x4, starting transfers between devices, along_z(): return lax.ppermute(value, ('zh', 'zl'), pairs)  12.4 us
    ppermute x4, waiting for transfers between devices, along_z(): return lax.ppermute(value, ('zh', 'zl'), pairs)  11.7 us
    all_to_all x1, waiting for transfers between devices, on_device(): weight_grad = lax.all_to_all(line, ('zh', 'zl'), 0, 0, tiled=True).sum(0)  9.8 us
    all_to_all x1, starting transfers between devices, on_device(): got = lax.all_to_all(chip, ('x', 'y'), 0, 0, tiled=True)  9.66 us
    all_to_all x1, starting transfers between devices, on_device(): weight_grad = lax.all_to_all(line, ('zh', 'zl'), 0, 0, tiled=True).sum(0)  4.26 us
    ppermute x1, starting transfers between devices, on_device(): other = lax.ppermute(own, 'core', swap)  3.09 us
    unnamed x13, local copies, waits for them, and re-layouts  2.05 us
  transfers between devices with their start and end apart: 8, of which 3 were waited for; matrix products, arithmetic and copies ran while one was open for 2% of the time, Pallas kernels for 2%

profile of v10, /device:TPU:1, one launch (start us, length us, event | category | flops | bytes accessed | tf_op | source)
XLA Modules:
  0.0 74.2 jit_solution(841936794093255369)
XLA Ops:
  0.6 0.0 copy-start
  0.6 1.2 %copy-done = bf16[128,4096]{1,0:T(8,128)(2,1)S(1)} copy-done((bf16[128,4096]{1,0:T(8,128)(2,1)S(1)}, bf16[128,4096]{1,0:T(8,128)(2,1)}, u32[]{:S(2)}) %copy-start) | copy-done | bytes 1048600
  1.9 0.0 copy-start.2
  1.9 0.8 %copy-done.2 = bf16[128,128]{1,0:T(8,128)(2,1)S(1)} copy-done((bf16[128,128]{1,0:T(8,128)(2,1)S(1)}, bf16[128,128]{1,0:T(8,128)(2,1)}, u32[]{:S(2)}) %copy-start.2) | copy-done | bytes 32792
  2.6 0.0 copy-start.3
  2.6 0.5 shard_map.60
  3.1 0.0 copy-start.4
  3.2 16.1 %collective-permute-start.5 = (f32[2048,128]{1,0:T(8,128)S(1)}, f32[2048,128]{1,0:T(8,128)S(1)}, u32[]{:S(2)}, u32[]{:S(2)}) collective-permute-start(f32[2048,128]{1,0:T(8,128)S(1)} %get-tuple-element.5), channel_id=1, source_target_pairs={{0,1},{1,0},{2,3},{3,2},{4,5},{5,4},{6,7},{7,6},{8,9},{9,8},{10,11... | collective-permute-start | bytes 3145736 | tf_op jit(solution)/shard_map/ppermute | solution.py:91
  19.2 0.0 copy-done.3
  19.2 0.0 copy-done.4
  19.3 5.3 %collective-permute-start = (bf16[256,128]{1,0:T(8,128)(2,1)S(1)}, bf16[256,128]{1,0:T(8,128)(2,1)S(1)}, u32[]{:S(2)}, u32[]{:S(2)}) collective-permute-start(bf16[256,128]{1,0:T(8,128)(2,1)S(1)} %get-tuple-element.7), channel_id=1, source_target_pairs={{6,0},{8,2},{10,4},{12,6},{14,8},{64,10},{66,12},{68,14},{70,64},{... | collective-permute-start | bytes 196616 | tf_op jit(solution)/shard_map/ppermute | solution.py:64
  24.6 0.0 collective-permute-done.5
  24.6 0.9 %add_convert_fusion = bf16[2048,128]{1,0:T(8,128)(2,1)} fusion(f32[2048,128]{1,0:T(8,128)S(1)} %get-tuple-element.4, f32[2048,128]{1,0:T(8,128)S(1)} %collective-permute-done.5), kind=kLoop, calls=%fused_computation.1 | loop fusion | flops 524288 | bytes 2621440 | tf_op jit(solution)/shard_map/convert_element_type | solution.py:92
  25.5 9.7 %all-to-all-start = ((bf16[32,64,128]{2,1,0:T(8,128)(2,1)}), bf16[32,64,128]{2,1,0:T(8,128)(2,1)S(1)}, u32[]{:S(2)}, u32[]{:S(2)}) async-start(bf16[32,64,128]{2,1,0:T(8,128)(2,1)} %bitcast.4), calls=%async_computation | async-start | bytes 1048576 | tf_op jit(solution)/shard_map/all_to_all | solution.py:95
  35.1 0.0 copy-start.1
  35.1 2.1 %collective-permute-start.1 = (bf16[256,128]{1,0:T(8,128)(2,1)S(1)}, bf16[256,128]{1,0:T(8,128)(2,1)S(1)}, u32[]{:S(2)}, u32[]{:S(2)}) collective-permute-start(bf16[256,128]{1,0:T(8,128)(2,1)S(1)} %get-tuple-element.7), channel_id=1, source_target_pairs={{74,0},{76,2},{78,4},{0,6},{2,8},{4,10},{6,12},{8,14},{10,64},{12,... | collective-permute-start | bytes 196616 | tf_op jit(solution)/shard_map/ppermute | solution.py:64
  37.2 0.0 collective-permute-done
  37.2 3.1 %collective-permute-start.3 = (bf16[512,128]{1,0:T(8,128)(2,1)S(1)}, bf16[512,128]{1,0:T(8,128)(2,1)S(1)}, u32[]{:S(2)}, u32[]{:S(2)}) collective-permute-start(bf16[512,128]{1,0:T(8,128)(2,1)S(1)} %pad_maximum_fusion.1), channel_id=1, source_target_pairs={{78,0},{0,2},{2,4},{4,6},{6,8},{8,10},{10,12},{12,14},{14,64},{64,... | collective-permute-start | bytes 393224 | tf_op jit(solution)/shard_map/ppermute | solution.py:64
  40.3 4.3 %collective-permute-done.1 = bf16[256,128]{1,0:T(8,128)(2,1)S(1)} collective-permute-done((bf16[256,128]{1,0:T(8,128)(2,1)S(1)}, bf16[256,128]{1,0:T(8,128)(2,1)S(1)}, u32[]{:S(2)}, u32[]{:S(2)}) %collective-permute-start.1) | collective-permute-done | bytes 65568 | tf_op jit(solution)/shard_map/ppermute | solution.py:64
  44.7 1.9 %collective-permute-start.2 = (bf16[768,128]{1,0:T(8,128)(2,1)S(1)}, bf16[768,128]{1,0:T(8,128)(2,1)S(1)}, u32[]{:S(2)}, u32[]{:S(2)}) collective-permute-start(bf16[768,128]{1,0:T(8,128)(2,1)S(1)} %pad_maximum_fusion), channel_id=1, source_target_pairs={{2,0},{4,2},{6,4},{8,6},{10,8},{12,10},{14,12},{64,14},{66,64},{68... | collective-permute-start | bytes 589832 | tf_op jit(solution)/shard_map/ppermute | solution.py:64
  46.6 7.4 %collective-permute-done.2 = bf16[768,128]{1,0:T(8,128)(2,1)S(1)} collective-permute-done((bf16[768,128]{1,0:T(8,128)(2,1)S(1)}, bf16[768,128]{1,0:T(8,128)(2,1)S(1)}, u32[]{:S(2)}, u32[]{:S(2)}) %collective-permute-start.2) | collective-permute-done | bytes 196640 | tf_op jit(solution)/shard_map/ppermute | solution.py:64
  54.0 0.0 collective-permute-done.3
  54.1 3.1 %collective-permute-start.4 = (bf16[2048,128]{1,0:T(8,128)(2,1)S(1)}, bf16[2048,128]{1,0:T(8,128)(2,1)S(1)}, u32[]{:S(2)}, u32[]{:S(2)}) collective-permute-start(bf16[2048,128]{1,0:T(8,128)(2,1)S(1)} %constant_dynamic-update-slice_fusion.own_ref), channel_id=1, source_target_pairs={{0,1},{1,0},{2,3},{3,2},{4,5},{5,4},{6,7},{7,6},{8,9},{9,8},{10,11... | collective-permute-start | bytes 1572872 | tf_op jit(solution)/shard_map/ppermute | solution.py:100
  57.2 0.0 all-to-all-done
  57.2 0.7 convert_reduce_fusion
  57.9 4.3 %all-to-all-start.1 = ((f32[16,4,128]{2,1,0:T(4,128)}), f32[16,4,128]{2,1,0:T(4,128)S(1)}, u32[]{:S(2)}, u32[]{:S(2)}) async-start(f32[16,4,128]{2,1,0:T(4,128)} %bitcast.5), calls=%async_computation.1 | async-start | bytes 65536 | tf_op jit(solution)/shard_map/all_to_all | solution.py:98
  62.1 0.1 pad_add_fusion.place_ref
  62.2 0.0 collective-permute-done.4.other_ref
  62.2 0.0 copy-done.1
  62.2 1.6 %shard_map.59 = bf16[128,128]{1,0:T(8,128)(2,1)} custom-call(s32[2]{0:T(128)S(1)} %pad_add_fusion.place_ref, bf16[128,4096]{1,0:T(8,128)(2,1)S(1)} %copy-done.1, bf16[2048,128]{1,0:T(8,128)(2,1)S(1)} %constant_dynamic-update-slice_fusion.own_ref, bf16[2048,128]{1,0:T(8,128)(2,1)S(1)} %collective-permute-done.4.other_ref), custom_call_target="tpu_custom_call" | custom-call | flops 134217728 | bytes 2097152 | tf_op jit(solution)/shard_map/pallas_call | solution.py:101
  63.8 9.8 %all-to-all-done.1 = f32[16,4,128]{2,1,0:T(4,128)S(1)} async-done(((f32[16,4,128]{2,1,0:T(4,128)}), f32[16,4,128]{2,1,0:T(4,128)S(1)}, u32[]{:S(2)}, u32[]{:S(2)}) %all-to-all-start.1) | async-done | bytes 32800 | tf_op jit(solution)/shard_map/all_to_all | solution.py:98
  73.6 0.6 reduce_sum.22
  (7 shorter events, 0.1 us)
Async XLA Ops:
  0.6 1.2 %copy-start = (bf16[128,4096]{1,0:T(8,128)(2,1)S(1)}, bf16[128,4096]{1,0:T(8,128)(2,1)}, u32[]{:S(2)}) copy-start(bf16[128,4096]{1,0:T(8,128)(2,1)} %refs_1_.1) | copy-start | bytes 3145732
  1.9 0.8 %copy-start.2 = (bf16[128,128]{1,0:T(8,128)(2,1)S(1)}, bf16[128,128]{1,0:T(8,128)(2,1)}, u32[]{:S(2)}) copy-start(bf16[128,128]{1,0:T(8,128)(2,1)} %refs_2_.1) | copy-start | bytes 98308
  2.6 16.6 %copy-start.3 = (bf16[1,256,128]{2,1,0:T(8,128)(2,1)S(1)}, bf16[1,256,128]{2,1,0:T(8,128)(2,1)}, u32[]{:S(2)}) copy-start(bf16[1,256,128]{2,1,0:T(8,128)(2,1)} %param.5) | copy-start | bytes 196612
  3.1 16.1 %copy-start.4 = (f32[1,128]{1,0:T(1,128)S(1)}, f32[1,128]{1,0:T(1,128)}, u32[]{:S(2)}) copy-start(f32[1,128]{1,0:T(1,128)} %param.6) | copy-start | bytes 1540
  3.2 21.4 %collective-permute-start.5 = (f32[2048,128]{1,0:T(8,128)S(1)}, f32[2048,128]{1,0:T(8,128)S(1)}, u32[]{:S(2)}, u32[]{:S(2)}) collective-permute-start(f32[2048,128]{1,0:T(8,128)S(1)} %get-tuple-element.5), channel_id=1, source_target_pairs={{0,1},{1,0},{2,3},{3,2},{4,5},{5,4},{6,7},{7,6},{8,9},{9,8},{10,11... | collective-permute-start | bytes 3145736 | tf_op jit(solution)/shard_map/ppermute | solution.py:91
  19.3 17.9 %collective-permute-start = (bf16[256,128]{1,0:T(8,128)(2,1)S(1)}, bf16[256,128]{1,0:T(8,128)(2,1)S(1)}, u32[]{:S(2)}, u32[]{:S(2)}) collective-permute-start(bf16[256,128]{1,0:T(8,128)(2,1)S(1)} %get-tuple-element.7), channel_id=1, source_target_pairs={{6,0},{8,2},{10,4},{12,6},{14,8},{64,10},{66,12},{68,14},{70,64},{... | collective-permute-start | bytes 196616 | tf_op jit(solution)/shard_map/ppermute | solution.py:64
  25.5 31.7 %all-to-all-start = ((bf16[32,64,128]{2,1,0:T(8,128)(2,1)}), bf16[32,64,128]{2,1,0:T(8,128)(2,1)S(1)}, u32[]{:S(2)}, u32[]{:S(2)}) async-start(bf16[32,64,128]{2,1,0:T(8,128)(2,1)} %bitcast.4), calls=%async_computation | async-start | bytes 1048576 | tf_op jit(solution)/shard_map/all_to_all | solution.py:95
  35.1 27.1 %copy-start.1 = (bf16[128,4096]{1,0:T(8,128)(2,1)S(1)}, bf16[128,4096]{1,0:T(8,128)(2,1)}, u32[]{:S(2)}) copy-start(bf16[128,4096]{1,0:T(8,128)(2,1)} %refs_1_.1) | copy-start | bytes 3145732
  35.1 9.5 %collective-permute-start.1 = (bf16[256,128]{1,0:T(8,128)(2,1)S(1)}, bf16[256,128]{1,0:T(8,128)(2,1)S(1)}, u32[]{:S(2)}, u32[]{:S(2)}) collective-permute-start(bf16[256,128]{1,0:T(8,128)(2,1)S(1)} %get-tuple-element.7), channel_id=1, source_target_pairs={{74,0},{76,2},{78,4},{0,6},{2,8},{4,10},{6,12},{8,14},{10,64},{12,... | collective-permute-start | bytes 196616 | tf_op jit(solution)/shard_map/ppermute | solution.py:64
  37.2 16.8 %collective-permute-start.3 = (bf16[512,128]{1,0:T(8,128)(2,1)S(1)}, bf16[512,128]{1,0:T(8,128)(2,1)S(1)}, u32[]{:S(2)}, u32[]{:S(2)}) collective-permute-start(bf16[512,128]{1,0:T(8,128)(2,1)S(1)} %pad_maximum_fusion.1), channel_id=1, source_target_pairs={{78,0},{0,2},{2,4},{4,6},{6,8},{8,10},{10,12},{12,14},{14,64},{64,... | collective-permute-start | bytes 393224 | tf_op jit(solution)/shard_map/ppermute | solution.py:64
  44.7 9.4 %collective-permute-start.2 = (bf16[768,128]{1,0:T(8,128)(2,1)S(1)}, bf16[768,128]{1,0:T(8,128)(2,1)S(1)}, u32[]{:S(2)}, u32[]{:S(2)}) collective-permute-start(bf16[768,128]{1,0:T(8,128)(2,1)S(1)} %pad_maximum_fusion), channel_id=1, source_target_pairs={{2,0},{4,2},{6,4},{8,6},{10,8},{12,10},{14,12},{64,14},{66,64},{68... | collective-permute-start | bytes 589832 | tf_op jit(solution)/shard_map/ppermute | solution.py:64
  54.1 8.1 %collective-permute-start.4 = (bf16[2048,128]{1,0:T(8,128)(2,1)S(1)}, bf16[2048,128]{1,0:T(8,128)(2,1)S(1)}, u32[]{:S(2)}, u32[]{:S(2)}) collective-permute-start(bf16[2048,128]{1,0:T(8,128)(2,1)S(1)} %constant_dynamic-update-slice_fusion.own_ref), channel_id=1, source_target_pairs={{0,1},{1,0},{2,3},{3,2},{4,5},{5,4},{6,7},{7,6},{8,9},{9,8},{10,11... | collective-permute-start | bytes 1572872 | tf_op jit(solution)/shard_map/ppermute | solution.py:100
  57.9 15.7 %all-to-all-start.1 = ((f32[16,4,128]{2,1,0:T(4,128)}), f32[16,4,128]{2,1,0:T(4,128)S(1)}, u32[]{:S(2)}, u32[]{:S(2)}) async-start(f32[16,4,128]{2,1,0:T(4,128)} %bitcast.5), calls=%async_computation.1 | async-start | bytes 65536 | tf_op jit(solution)/shard_map/all_to_all | solution.py:98

commit v11 on v9

--- a/solution.py
+++ b/solution.py
@@ -33,7 +33,7 @@
             one = jnp.where(low, pltpu.roll(even, share, 1), odd)
             at = pl.ds(((outer // ZH * X + x) * ZH + outer % ZH) * half, half)
             keep_ref[at, :] = jnp.where(first, zero, one).reshape(half, -1)
-            send_ref[at, :] = jnp.where(first, one, zero).reshape(half, -1)
+            send_ref[at, :] = jnp.where(first, one, zero).reshape(half, -1).astype(send_ref.dtype)
 
 
 def gather_order():
@@ -89,14 +89,17 @@
     rows = width // CORE
     keep, send = pl.pallas_call(
         lambda *refs: term_kernel(float(tokens) ** (-0.5), *refs),
-        out_shape=[jax.ShapeDtypeStruct((rows, head), jnp.float32)] * 2,
+        out_shape=[
+            jax.ShapeDtypeStruct((rows, head), jnp.float32),
+            jax.ShapeDtypeStruct((rows, head), jnp.bfloat16),
+        ],
         in_specs=[smem, vmem, vmem],
         out_specs=[vmem, vmem],
         compiler_params=params,
         cost_estimate=pl.CostEstimate(flops=2 * 128 * width * head, bytes_accessed=3 << 20, transcendentals=0),
     )(core, activations, cotangent)
     held = jnp.concatenate([own, along_z(own, FIRST), along_z(own, -FIRST)])
-    chip = keep + lax.ppermute(send, "core", swap)
+    chip = keep + lax.ppermute(send, "core", swap).astype(jnp.float32)
     chip = chip.astype(jnp.bfloat16)
     two = 2 * own.shape[0]
     own = jnp.concatenate([held, along_z(held, SECOND), along_z(held[:two], -SECOND)])

time: 74.8 us -> 74.8 us (level)
  starting transfers between devices: 45.4 us -> 46.9 us
  waiting for transfers between devices: 20.8 us -> 19.3 us
    ppermute x4, waiting for transfers between devices: 11.7 us -> 10.2 us  [along_z(): return lax.ppermute(value, ('zh', 'zl'), pairs)]
    ppermute x4, starting transfers between devices: 12.4 us -> 13.7 us  [along_z(): return lax.ppermute(value, ('zh', 'zl'), pairs)]
where the time goes in v11:
time: 74.8 us; the launch traced here: 74.3 us
  starting transfers between devices  46.9 us (63%)
  waiting for transfers between devices  19.3 us (26%)
  Pallas kernels  2.81 us (4%)
  other arithmetic  2.34 us (3%)
  local copies, waits for them, and re-layouts  2.07 us (3%)
  between operations  0.84 us (1%)
    ppermute x1, starting transfers between devices, on_device(): chip = keep + lax.ppermute(send, 'core', swap).astype(jnp.float32)  16.1 us
    ppermute x4, starting transfers between devices, along_z(): return lax.ppermute(value, ('zh', 'zl'), pairs)  13.7 us
    ppermute x4, waiting for transfers between devices, along_z(): return lax.ppermute(value, ('zh', 'zl'), pairs)  10.2 us
    all_to_all x1, starting transfers between devices, on_device(): got = lax.all_to_all(chip, ('y', 'x'), 0, 0, tiled=True)  9.66 us
    all_to_all x1, waiting for transfers between devices, on_device(): weight_grad = lax.all_to_all(line, ('zh', 'zl'), 0, 0, tiled=True).sum(0)  9.1 us
    all_to_all x1, starting transfers between devices, on_device(): weight_grad = lax.all_to_all(line, ('zh', 'zl'), 0, 0, tiled=True).sum(0)  4.37 us
    ppermute x1, starting transfers between devices, on_device(): other = lax.ppermute(own, 'core', swap)  3.1 us
    unnamed x13, local copies, waits for them, and re-layouts  2.05 us
  transfers between devices with their start and end apart: 8, of which 3 were waited for; matrix products, arithmetic and copies ran while one was open for 2% of the time, Pallas kernels for 3%

profile of v11, /device:TPU:1, one launch (start us, length us, event | category | flops | bytes accessed | tf_op | source)
XLA Modules:
  0.0 74.3 jit_solution(14413587147546873471)
XLA Ops:
  0.6 0.0 copy-start
  0.6 1.2 %copy-done = bf16[128,4096]{1,0:T(8,128)(2,1)S(1)} copy-done((bf16[128,4096]{1,0:T(8,128)(2,1)S(1)}, bf16[128,4096]{1,0:T(8,128)(2,1)}, u32[]{:S(2)}) %copy-start) | copy-done | bytes 1048600
  1.9 0.0 copy-start.2
  1.9 0.8 %copy-done.2 = bf16[128,128]{1,0:T(8,128)(2,1)S(1)} copy-done((bf16[128,128]{1,0:T(8,128)(2,1)S(1)}, bf16[128,128]{1,0:T(8,128)(2,1)}, u32[]{:S(2)}) %copy-start.2) | copy-done | bytes 32792
  2.6 0.5 shard_map.61
  3.2 0.0 copy-start.4
  3.2 16.1 %collective-permute-start.5 = (bf16[2048,128]{1,0:T(8,128)(2,1)S(1)}, bf16[2048,128]{1,0:T(8,128)(2,1)S(1)}, u32[]{:S(2)}, u32[]{:S(2)}) collective-permute-start(bf16[2048,128]{1,0:T(8,128)(2,1)S(1)} %get-tuple-element.5), channel_id=1, source_target_pairs={{0,1},{1,0},{2,3},{3,2},{4,5},{5,4},{6,7},{7,6},{8,9},{9,8},{10,11... | collective-permute-start | bytes 1572872 | tf_op jit(solution)/shard_map/ppermute | solution.py:102
  19.2 0.0 copy-done.3
  19.3 0.0 copy-done.4
  19.3 5.3 %collective-permute-start = (bf16[256,128]{1,0:T(8,128)(2,1)S(1)}, bf16[256,128]{1,0:T(8,128)(2,1)S(1)}, u32[]{:S(2)}, u32[]{:S(2)}) collective-permute-start(bf16[256,128]{1,0:T(8,128)(2,1)S(1)} %get-tuple-element.7), channel_id=1, source_target_pairs={{6,0},{8,2},{10,4},{12,6},{14,8},{64,10},{66,12},{68,14},{70,64},{... | collective-permute-start | bytes 196616 | tf_op jit(solution)/shard_map/ppermute | solution.py:72
  24.6 0.0 collective-permute-done.5
  24.6 0.9 %add_convert_fusion = bf16[2048,128]{1,0:T(8,128)(2,1)} fusion(f32[2048,128]{1,0:T(8,128)S(1)} %get-tuple-element.4, bf16[2048,128]{1,0:T(8,128)(2,1)S(1)} %collective-permute-done.5), kind=kLoop, calls=%fused_computation.1 | loop fusion | flops 786432 | bytes 2097152 | tf_op jit(solution)/shard_map/convert_element_type | solution.py:103
  25.5 9.7 %all-to-all-start = ((bf16[32,64,128]{2,1,0:T(8,128)(2,1)}), bf16[32,64,128]{2,1,0:T(8,128)(2,1)S(1)}, u32[]{:S(2)}, u32[]{:S(2)}) async-start(bf16[32,64,128]{2,1,0:T(8,128)(2,1)} %bitcast.4), calls=%async_computation | async-start | bytes 1048576 | tf_op jit(solution)/shard_map/all_to_all | solution.py:106
  35.2 0.0 copy-start.1
  35.2 2.1 %collective-permute-start.1 = (bf16[256,128]{1,0:T(8,128)(2,1)S(1)}, bf16[256,128]{1,0:T(8,128)(2,1)S(1)}, u32[]{:S(2)}, u32[]{:S(2)}) collective-permute-start(bf16[256,128]{1,0:T(8,128)(2,1)S(1)} %get-tuple-element.7), channel_id=1, source_target_pairs={{74,0},{76,2},{78,4},{0,6},{2,8},{4,10},{6,12},{8,14},{10,64},{12,... | collective-permute-start | bytes 196616 | tf_op jit(solution)/shard_map/ppermute | solution.py:72
  37.3 0.0 collective-permute-done
  37.3 3.1 %collective-permute-start.3 = (bf16[512,128]{1,0:T(8,128)(2,1)S(1)}, bf16[512,128]{1,0:T(8,128)(2,1)S(1)}, u32[]{:S(2)}, u32[]{:S(2)}) collective-permute-start(bf16[512,128]{1,0:T(8,128)(2,1)S(1)} %pad_maximum_fusion.1), channel_id=1, source_target_pairs={{78,0},{0,2},{2,4},{4,6},{6,8},{8,10},{10,12},{12,14},{14,64},{64,... | collective-permute-start | bytes 393224 | tf_op jit(solution)/shard_map/ppermute | solution.py:72
  40.4 4.0 %collective-permute-done.1 = bf16[256,128]{1,0:T(8,128)(2,1)S(1)} collective-permute-done((bf16[256,128]{1,0:T(8,128)(2,1)S(1)}, bf16[256,128]{1,0:T(8,128)(2,1)S(1)}, u32[]{:S(2)}, u32[]{:S(2)}) %collective-permute-start.1) | collective-permute-done | bytes 65568 | tf_op jit(solution)/shard_map/ppermute | solution.py:72
  44.4 3.3 %collective-permute-start.2 = (bf16[768,128]{1,0:T(8,128)(2,1)S(1)}, bf16[768,128]{1,0:T(8,128)(2,1)S(1)}, u32[]{:S(2)}, u32[]{:S(2)}) collective-permute-start(bf16[768,128]{1,0:T(8,128)(2,1)S(1)} %pad_maximum_fusion), channel_id=1, source_target_pairs={{2,0},{4,2},{6,4},{8,6},{10,8},{12,10},{14,12},{64,14},{66,64},{68... | collective-permute-start | bytes 589832 | tf_op jit(solution)/shard_map/ppermute | solution.py:72
  47.7 6.2 %collective-permute-done.2 = bf16[768,128]{1,0:T(8,128)(2,1)S(1)} collective-permute-done((bf16[768,128]{1,0:T(8,128)(2,1)S(1)}, bf16[768,128]{1,0:T(8,128)(2,1)S(1)}, u32[]{:S(2)}, u32[]{:S(2)}) %collective-permute-start.2) | collective-permute-done | bytes 196640 | tf_op jit(solution)/shard_map/ppermute | solution.py:72
  54.0 0.0 collective-permute-done.3
  54.0 3.1 %collective-permute-start.4 = (bf16[2048,128]{1,0:T(8,128)(2,1)S(1)}, bf16[2048,128]{1,0:T(8,128)(2,1)S(1)}, u32[]{:S(2)}, u32[]{:S(2)}) collective-permute-start(bf16[2048,128]{1,0:T(8,128)(2,1)S(1)} %constant_dynamic-update-slice_fusion.own_ref), channel_id=1, source_target_pairs={{0,1},{1,0},{2,3},{3,2},{4,5},{5,4},{6,7},{7,6},{8,9},{9,8},{10,11... | collective-permute-start | bytes 1572872 | tf_op jit(solution)/shard_map/ppermute | solution.py:119
  57.1 0.0 all-to-all-done
  57.1 0.7 convert_reduce_fusion
  57.8 4.4 %all-to-all-start.1 = ((f32[16,4,128]{2,1,0:T(4,128)}), f32[16,4,128]{2,1,0:T(4,128)S(1)}, u32[]{:S(2)}, u32[]{:S(2)}) async-start(f32[16,4,128]{2,1,0:T(4,128)} %bitcast.5), calls=%async_computation.1 | async-start | bytes 65536 | tf_op jit(solution)/shard_map/all_to_all | solution.py:109
  62.2 0.1 pad_add_fusion.place_ref
  62.3 0.0 copy-done.1
  62.3 0.8 %shard_map.59.part_ref = f32[128,128]{1,0:T(8,128)S(1)} custom-call(s32[2]{0:T(128)S(1)} %pad_add_fusion.place_ref, bf16[128,4096]{1,0:T(8,128)(2,1)S(1)} %copy-done.1, bf16[2048,128]{1,0:T(8,128)(2,1)S(1)} %constant_dynamic-update-slice_fusion.own_ref), custom_call_target="tpu_custom_call" | custom-call | flops 67108864 | bytes 1048576 | tf_op jit(solution)/shard_map/pallas_call | solution.py:111
  63.1 0.0 collective-permute-done.4.other_ref
  63.1 1.4 %shard_map.60 = bf16[128,128]{1,0:T(8,128)(2,1)} custom-call(s32[2]{0:T(128)S(1)} %pad_add_fusion.place_ref, bf16[128,4096]{1,0:T(8,128)(2,1)S(1)} %copy-done.1, bf16[2048,128]{1,0:T(8,128)(2,1)S(1)} %collective-permute-done.4.other_ref, f32[128,128]{1,0:T(8,128)S(1)} %shard_map.59.part_ref), custom_call_target="tpu_custom_call" | custom-call | flops 67108864 | bytes 1048576 | tf_op jit(solution)/shard_map/pallas_call | solution.py:120
  64.6 9.1 %all-to-all-done.1 = f32[16,4,128]{2,1,0:T(4,128)S(1)} async-done(((f32[16,4,128]{2,1,0:T(4,128)}), f32[16,4,128]{2,1,0:T(4,128)S(1)}, u32[]{:S(2)}, u32[]{:S(2)}) %all-to-all-start.1) | async-done | bytes 32800 | tf_op jit(solution)/shard_map/all_to_all | solution.py:109
  73.7 0.6 reduce_sum.22
  (8 shorter events, 0.1 us)
Async XLA Ops:
  0.6 1.2 %copy-start = (bf16[128,4096]{1,0:T(8,128)(2,1)S(1)}, bf16[128,4096]{1,0:T(8,128)(2,1)}, u32[]{:S(2)}) copy-start(bf16[128,4096]{1,0:T(8,128)(2,1)} %refs_1_.1) | copy-start | bytes 3145732
  1.9 0.8 %copy-start.2 = (bf16[128,128]{1,0:T(8,128)(2,1)S(1)}, bf16[128,128]{1,0:T(8,128)(2,1)}, u32[]{:S(2)}) copy-start(bf16[128,128]{1,0:T(8,128)(2,1)} %refs_2_.1) | copy-start | bytes 98308
  2.6 16.6 %copy-start.3 = (bf16[1,256,128]{2,1,0:T(8,128)(2,1)S(1)}, bf16[1,256,128]{2,1,0:T(8,128)(2,1)}, u32[]{:S(2)}) copy-start(bf16[1,256,128]{2,1,0:T(8,128)(2,1)} %param.5) | copy-start | bytes 196612
  3.2 16.1 %copy-start.4 = (f32[1,128]{1,0:T(1,128)S(1)}, f32[1,128]{1,0:T(1,128)}, u32[]{:S(2)}) copy-start(f32[1,128]{1,0:T(1,128)} %param.6) | copy-start | bytes 1540
  3.2 21.4 %collective-permute-start.5 = (bf16[2048,128]{1,0:T(8,128)(2,1)S(1)}, bf16[2048,128]{1,0:T(8,128)(2,1)S(1)}, u32[]{:S(2)}, u32[]{:S(2)}) collective-permute-start(bf16[2048,128]{1,0:T(8,128)(2,1)S(1)} %get-tuple-element.5), channel_id=1, source_target_pairs={{0,1},{1,0},{2,3},{3,2},{4,5},{5,4},{6,7},{7,6},{8,9},{9,8},{10,11... | collective-permute-start | bytes 1572872 | tf_op jit(solution)/shard_map/ppermute | solution.py:102
  19.3 18.0 %collective-permute-start = (bf16[256,128]{1,0:T(8,128)(2,1)S(1)}, bf16[256,128]{1,0:T(8,128)(2,1)S(1)}, u32[]{:S(2)}, u32[]{:S(2)}) collective-permute-start(bf16[256,128]{1,0:T(8,128)(2,1)S(1)} %get-tuple-element.7), channel_id=1, source_target_pairs={{6,0},{8,2},{10,4},{12,6},{14,8},{64,10},{66,12},{68,14},{70,64},{... | collective-permute-start | bytes 196616 | tf_op jit(solution)/shard_map/ppermute | solution.py:72
  25.5 31.6 %all-to-all-start = ((bf16[32,64,128]{2,1,0:T(8,128)(2,1)}), bf16[32,64,128]{2,1,0:T(8,128)(2,1)S(1)}, u32[]{:S(2)}, u32[]{:S(2)}) async-start(bf16[32,64,128]{2,1,0:T(8,128)(2,1)} %bitcast.4), calls=%async_computation | async-start | bytes 1048576 | tf_op jit(solution)/shard_map/all_to_all | solution.py:106
  35.2 27.1 %copy-start.1 = (bf16[128,4096]{1,0:T(8,128)(2,1)S(1)}, bf16[128,4096]{1,0:T(8,128)(2,1)}, u32[]{:S(2)}) copy-start(bf16[128,4096]{1,0:T(8,128)(2,1)} %refs_1_.1) | copy-start | bytes 3145732
  35.2 9.2 %collective-permute-start.1 = (bf16[256,128]{1,0:T(8,128)(2,1)S(1)}, bf16[256,128]{1,0:T(8,128)(2,1)S(1)}, u32[]{:S(2)}, u32[]{:S(2)}) collective-permute-start(bf16[256,128]{1,0:T(8,128)(2,1)S(1)} %get-tuple-element.7), channel_id=1, source_target_pairs={{74,0},{76,2},{78,4},{0,6},{2,8},{4,10},{6,12},{8,14},{10,64},{12,... | collective-permute-start | bytes 196616 | tf_op jit(solution)/shard_map/ppermute | solution.py:72
  37.3 16.7 %collective-permute-start.3 = (bf16[512,128]{1,0:T(8,128)(2,1)S(1)}, bf16[512,128]{1,0:T(8,128)(2,1)S(1)}, u32[]{:S(2)}, u32[]{:S(2)}) collective-permute-start(bf16[512,128]{1,0:T(8,128)(2,1)S(1)} %pad_maximum_fusion.1), channel_id=1, source_target_pairs={{78,0},{0,2},{2,4},{4,6},{6,8},{8,10},{10,12},{12,14},{14,64},{64,... | collective-permute-start | bytes 393224 | tf_op jit(solution)/shard_map/ppermute | solution.py:72
  44.4 9.5 %collective-permute-start.2 = (bf16[768,128]{1,0:T(8,128)(2,1)S(1)}, bf16[768,128]{1,0:T(8,128)(2,1)S(1)}, u32[]{:S(2)}, u32[]{:S(2)}) collective-permute-start(bf16[768,128]{1,0:T(8,128)(2,1)S(1)} %pad_maximum_fusion), channel_id=1, source_target_pairs={{2,0},{4,2},{6,4},{8,6},{10,8},{12,10},{14,12},{64,14},{66,64},{68... | collective-permute-start | bytes 589832 | tf_op jit(solution)/shard_map/ppermute | solution.py:72
  54.0 9.1 %collective-permute-start.4 = (bf16[2048,128]{1,0:T(8,128)(2,1)S(1)}, bf16[2048,128]{1,0:T(8,128)(2,1)S(1)}, u32[]{:S(2)}, u32[]{:S(2)}) collective-permute-start(bf16[2048,128]{1,0:T(8,128)(2,1)S(1)} %constant_dynamic-update-slice_fusion.own_ref), channel_id=1, source_target_pairs={{0,1},{1,0},{2,3},{3,2},{4,5},{5,4},{6,7},{7,6},{8,9},{9,8},{10,11... | collective-permute-start | bytes 1572872 | tf_op jit(solution)/shard_map/ppermute | solution.py:119
  57.8 15.9 %all-to-all-start.1 = ((f32[16,4,128]{2,1,0:T(4,128)}), f32[16,4,128]{2,1,0:T(4,128)S(1)}, u32[]{:S(2)}, u32[]{:S(2)}) async-start(f32[16,4,128]{2,1,0:T(4,128)} %bitcast.5), calls=%async_computation.1 | async-start | bytes 65536 | tf_op jit(solution)/shard_map/all_to_all | solution.py:109

commit v12 on v11

--- a/solution.py
+++ b/solution.py
@@ -86,6 +86,7 @@
     stored = (codes.astype(jnp.float32) * scales[:, None, :]).astype(jnp.bfloat16)
     own = stored.reshape(-1, head)
 
+    cotangent, _ = lax.optimization_barrier((cotangent, stored))
     rows = width // CORE
     keep, send = pl.pallas_call(
         lambda *refs: term_kernel(float(tokens) ** (-0.5), *refs),

time: 74.8 us -> 75.5 us (level)
  other arithmetic: 2.34 us -> 3.21 us
    unnamed x1, other arithmetic: 0.02 us -> 0.87 us
    unnamed x13 -> x11, local copies, waits for them, and re-layouts: 2.05 us -> 1.93 us
where the time goes in v12:
time: 75.5 us; the launch traced here: 75 us
  starting transfers between devices  47 us (62%)
  waiting for transfers between devices  19.2 us (25%)
  other arithmetic  3.21 us (4%)
  Pallas kernels  2.8 us (4%)
  local copies, waits for them, and re-layouts  1.95 us (3%)
  between operations  0.83 us (1%)
    ppermute x1, starting transfers between devices, on_device(): chip = keep + lax.ppermute(send, 'core', swap).astype(jnp.float32)  16.1 us
    ppermute x4, starting transfers between devices, along_z(): return lax.ppermute(value, ('zh', 'zl'), pairs)  13.8 us
    ppermute x4, waiting for transfers between devices, along_z(): return lax.ppermute(value, ('zh', 'zl'), pairs)  10.1 us
    all_to_all x1, starting transfers between devices, on_device(): got = lax.all_to_all(chip, ('y', 'x'), 0, 0, tiled=True)  9.68 us
    all_to_all x1, waiting for transfers between devices, on_device(): weight_grad = lax.all_to_all(line, ('zh', 'zl'), 0, 0, tiled=True).sum(0)  9.1 us
    all_to_all x1, starting transfers between devices, on_device(): weight_grad = lax.all_to_all(line, ('zh', 'zl'), 0, 0, tiled=True).sum(0)  4.38 us
    ppermute x1, starting transfers between devices, on_device(): other = lax.ppermute(own, 'core', swap)  3.1 us
    unnamed x11, local copies, waits for them, and re-layouts  1.93 us
  transfers between devices with their start and end apart: 8, of which 3 were waited for; matrix products, arithmetic and copies ran while one was open for 2% of the time, Pallas kernels for 3%

profile of v12, /device:TPU:1, one launch (start us, length us, event | category | flops | bytes accessed | tf_op | source)
XLA Modules:
  0.0 75.0 jit_solution(3593910648253961113)
XLA Ops:
  0.6 0.0 copy-start.3
  0.6 0.6 copy-done.3
  1.3 0.0 copy-start.2
  1.3 0.9 %constant_dynamic-update-slice_fusion.4 = (bf16[2048,128]{1,0:T(8,128)(2,1)S(1)}, bf16[1,256,128]{2,1,0:T(8,128)(2,1)S(1)}) fusion(f32[128]{0:T(128)S(1)} %bitcast.11, bf16[1,256,128]{2,1,0:T(8,128)(2,1)} %param.5), kind=kLoop, calls=%fused_computation.9 | loop fusion | flops 98303 | bytes 197120
  2.2 0.0 copy-done.2
  2.2 0.0 copy-start
  2.2 1.2 %copy-done = bf16[128,4096]{1,0:T(8,128)(2,1)S(1)} copy-done((bf16[128,4096]{1,0:T(8,128)(2,1)S(1)}, bf16[128,4096]{1,0:T(8,128)(2,1)}, u32[]{:S(2)}) %copy-start) | copy-done | bytes 1048600
  3.4 0.5 shard_map.61
  3.9 16.1 %collective-permute-start.5 = (bf16[2048,128]{1,0:T(8,128)(2,1)S(1)}, bf16[2048,128]{1,0:T(8,128)(2,1)S(1)}, u32[]{:S(2)}, u32[]{:S(2)}) collective-permute-start(bf16[2048,128]{1,0:T(8,128)(2,1)S(1)} %get-tuple-element.7), channel_id=1, source_target_pairs={{0,1},{1,0},{2,3},{3,2},{4,5},{5,4},{6,7},{7,6},{8,9},{9,8},{10,11... | collective-permute-start | bytes 1572872 | tf_op jit(solution)/shard_map/ppermute | solution.py:103
  20.0 5.3 %collective-permute-start = (bf16[256,128]{1,0:T(8,128)(2,1)S(1)}, bf16[256,128]{1,0:T(8,128)(2,1)S(1)}, u32[]{:S(2)}, u32[]{:S(2)}) collective-permute-start(bf16[256,128]{1,0:T(8,128)(2,1)S(1)} %bitcast.7), channel_id=1, source_target_pairs={{6,0},{8,2},{10,4},{12,6},{14,8},{64,10},{66,12},{68,14},{70,64},{... | collective-permute-start | bytes 196616 | tf_op jit(solution)/shard_map/ppermute | solution.py:72
  25.3 0.0 collective-permute-done.5
  25.3 0.9 %add_convert_fusion = bf16[2048,128]{1,0:T(8,128)(2,1)} fusion(f32[2048,128]{1,0:T(8,128)S(1)} %get-tuple-element.6, bf16[2048,128]{1,0:T(8,128)(2,1)S(1)} %collective-permute-done.5), kind=kLoop, calls=%fused_computation.1 | loop fusion | flops 786432 | bytes 2097152 | tf_op jit(solution)/shard_map/convert_element_type | solution.py:104
  26.2 9.7 %all-to-all-start = ((bf16[32,64,128]{2,1,0:T(8,128)(2,1)}), bf16[32,64,128]{2,1,0:T(8,128)(2,1)S(1)}, u32[]{:S(2)}, u32[]{:S(2)}) async-start(bf16[32,64,128]{2,1,0:T(8,128)(2,1)} %bitcast.4), calls=%async_computation | async-start | bytes 1048576 | tf_op jit(solution)/shard_map/all_to_all | solution.py:107
  35.9 0.0 copy-start.1
  35.9 2.1 %collective-permute-start.1 = (bf16[256,128]{1,0:T(8,128)(2,1)S(1)}, bf16[256,128]{1,0:T(8,128)(2,1)S(1)}, u32[]{:S(2)}, u32[]{:S(2)}) collective-permute-start(bf16[256,128]{1,0:T(8,128)(2,1)S(1)} %bitcast.8), channel_id=1, source_target_pairs={{74,0},{76,2},{78,4},{0,6},{2,8},{4,10},{6,12},{8,14},{10,64},{12,... | collective-permute-start | bytes 196616 | tf_op jit(solution)/shard_map/ppermute | solution.py:72
  38.0 0.0 collective-permute-done
  38.0 3.1 %collective-permute-start.3 = (bf16[512,128]{1,0:T(8,128)(2,1)S(1)}, bf16[512,128]{1,0:T(8,128)(2,1)S(1)}, u32[]{:S(2)}, u32[]{:S(2)}) collective-permute-start(bf16[512,128]{1,0:T(8,128)(2,1)S(1)} %pad_maximum_fusion.1), channel_id=1, source_target_pairs={{78,0},{0,2},{2,4},{4,6},{6,8},{8,10},{10,12},{12,14},{14,64},{64,... | collective-permute-start | bytes 393224 | tf_op jit(solution)/shard_map/ppermute | solution.py:72
  41.1 3.9 %collective-permute-done.1 = bf16[256,128]{1,0:T(8,128)(2,1)S(1)} collective-permute-done((bf16[256,128]{1,0:T(8,128)(2,1)S(1)}, bf16[256,128]{1,0:T(8,128)(2,1)S(1)}, u32[]{:S(2)}, u32[]{:S(2)}) %collective-permute-start.1) | collective-permute-done | bytes 65568 | tf_op jit(solution)/shard_map/ppermute | solution.py:72
  45.1 3.3 %collective-permute-start.2 = (bf16[768,128]{1,0:T(8,128)(2,1)S(1)}, bf16[768,128]{1,0:T(8,128)(2,1)S(1)}, u32[]{:S(2)}, u32[]{:S(2)}) collective-permute-start(bf16[768,128]{1,0:T(8,128)(2,1)S(1)} %pad_maximum_fusion), channel_id=1, source_target_pairs={{2,0},{4,2},{6,4},{8,6},{10,8},{12,10},{14,12},{64,14},{66,64},{68... | collective-permute-start | bytes 589832 | tf_op jit(solution)/shard_map/ppermute | solution.py:72
  48.5 6.2 %collective-permute-done.2 = bf16[768,128]{1,0:T(8,128)(2,1)S(1)} collective-permute-done((bf16[768,128]{1,0:T(8,128)(2,1)S(1)}, bf16[768,128]{1,0:T(8,128)(2,1)S(1)}, u32[]{:S(2)}, u32[]{:S(2)}) %collective-permute-start.2) | collective-permute-done | bytes 196640 | tf_op jit(solution)/shard_map/ppermute | solution.py:72
  54.7 0.0 collective-permute-done.3
  54.7 3.1 %collective-permute-start.4 = (bf16[2048,128]{1,0:T(8,128)(2,1)S(1)}, bf16[2048,128]{1,0:T(8,128)(2,1)S(1)}, u32[]{:S(2)}, u32[]{:S(2)}) collective-permute-start(bf16[2048,128]{1,0:T(8,128)(2,1)S(1)} %constant_dynamic-update-slice_fusion.own_ref), channel_id=1, source_target_pairs={{0,1},{1,0},{2,3},{3,2},{4,5},{5,4},{6,7},{7,6},{8,9},{9,8},{10,11... | collective-permute-start | bytes 1572872 | tf_op jit(solution)/shard_map/ppermute | solution.py:120
  57.8 0.0 all-to-all-done
  57.9 0.7 convert_reduce_fusion
  58.6 4.4 %all-to-all-start.1 = ((f32[16,4,128]{2,1,0:T(4,128)}), f32[16,4,128]{2,1,0:T(4,128)S(1)}, u32[]{:S(2)}, u32[]{:S(2)}) async-start(f32[16,4,128]{2,1,0:T(4,128)} %bitcast.5), calls=%async_computation.1 | async-start | bytes 65536 | tf_op jit(solution)/shard_map/all_to_all | solution.py:110
  62.9 0.1 pad_add_fusion.place_ref
  63.0 0.0 copy-done.1
  63.0 0.8 %shard_map.59.part_ref = f32[128,128]{1,0:T(8,128)S(1)} custom-call(s32[2]{0:T(128)S(1)} %pad_add_fusion.place_ref, bf16[128,4096]{1,0:T(8,128)(2,1)S(1)} %copy-done.1, bf16[2048,128]{1,0:T(8,128)(2,1)S(1)} %constant_dynamic-update-slice_fusion.own_ref), custom_call_target="tpu_custom_call" | custom-call | flops 67108864 | bytes 1048576 | tf_op jit(solution)/shard_map/pallas_call | solution.py:112
  63.9 0.0 collective-permute-done.4.other_ref
  63.9 1.4 %shard_map.60 = bf16[128,128]{1,0:T(8,128)(2,1)} custom-call(s32[2]{0:T(128)S(1)} %pad_add_fusion.place_ref, bf16[128,4096]{1,0:T(8,128)(2,1)S(1)} %copy-done.1, bf16[2048,128]{1,0:T(8,128)(2,1)S(1)} %collective-permute-done.4.other_ref, f32[128,128]{1,0:T(8,128)S(1)} %shard_map.59.part_ref), custom_call_target="tpu_custom_call" | custom-call | flops 67108864 | bytes 1048576 | tf_op jit(solution)/shard_map/pallas_call | solution.py:121
  65.3 9.1 %all-to-all-done.1 = f32[16,4,128]{2,1,0:T(4,128)S(1)} async-done(((f32[16,4,128]{2,1,0:T(4,128)}), f32[16,4,128]{2,1,0:T(4,128)S(1)}, u32[]{:S(2)}, u32[]{:S(2)}) %all-to-all-start.1) | async-done | bytes 32800 | tf_op jit(solution)/shard_map/all_to_all | solution.py:110
  74.4 0.6 reduce_sum.22
  (6 shorter events, 0.1 us)
Async XLA Ops:
  0.6 0.7 copy-start.3
  1.3 0.9 %copy-start.2 = (bf16[128,128]{1,0:T(8,128)(2,1)S(1)}, bf16[128,128]{1,0:T(8,128)(2,1)}, u32[]{:S(2)}) copy-start(bf16[128,128]{1,0:T(8,128)(2,1)} %refs_2_) | copy-start | bytes 98308
  2.2 1.2 %copy-start = (bf16[128,4096]{1,0:T(8,128)(2,1)S(1)}, bf16[128,4096]{1,0:T(8,128)(2,1)}, u32[]{:S(2)}) copy-start(bf16[128,4096]{1,0:T(8,128)(2,1)} %refs_1_.1) | copy-start | bytes 3145732
  3.9 21.4 %collective-permute-start.5 = (bf16[2048,128]{1,0:T(8,128)(2,1)S(1)}, bf16[2048,128]{1,0:T(8,128)(2,1)S(1)}, u32[]{:S(2)}, u32[]{:S(2)}) collective-permute-start(bf16[2048,128]{1,0:T(8,128)(2,1)S(1)} %get-tuple-element.7), channel_id=1, source_target_pairs={{0,1},{1,0},{2,3},{3,2},{4,5},{5,4},{6,7},{7,6},{8,9},{9,8},{10,11... | collective-permute-start | bytes 1572872 | tf_op jit(solution)/shard_map/ppermute | solution.py:103
  20.0 18.0 %collective-permute-start = (bf16[256,128]{1,0:T(8,128)(2,1)S(1)}, bf16[256,128]{1,0:T(8,128)(2,1)S(1)}, u32[]{:S(2)}, u32[]{:S(2)}) collective-permute-start(bf16[256,128]{1,0:T(8,128)(2,1)S(1)} %bitcast.7), channel_id=1, source_target_pairs={{6,0},{8,2},{10,4},{12,6},{14,8},{64,10},{66,12},{68,14},{70,64},{... | collective-permute-start | bytes 196616 | tf_op jit(solution)/shard_map/ppermute | solution.py:72
  26.2 31.6 %all-to-all-start = ((bf16[32,64,128]{2,1,0:T(8,128)(2,1)}), bf16[32,64,128]{2,1,0:T(8,128)(2,1)S(1)}, u32[]{:S(2)}, u32[]{:S(2)}) async-start(bf16[32,64,128]{2,1,0:T(8,128)(2,1)} %bitcast.4), calls=%async_computation | async-start | bytes 1048576 | tf_op jit(solution)/shard_map/all_to_all | solution.py:107
  35.9 27.1 %copy-start.1 = (bf16[128,4096]{1,0:T(8,128)(2,1)S(1)}, bf16[128,4096]{1,0:T(8,128)(2,1)}, u32[]{:S(2)}) copy-start(bf16[128,4096]{1,0:T(8,128)(2,1)} %refs_1_.1) | copy-start | bytes 3145732
  35.9 9.1 %collective-permute-start.1 = (bf16[256,128]{1,0:T(8,128)(2,1)S(1)}, bf16[256,128]{1,0:T(8,128)(2,1)S(1)}, u32[]{:S(2)}, u32[]{:S(2)}) collective-permute-start(bf16[256,128]{1,0:T(8,128)(2,1)S(1)} %bitcast.8), channel_id=1, source_target_pairs={{74,0},{76,2},{78,4},{0,6},{2,8},{4,10},{6,12},{8,14},{10,64},{12,... | collective-permute-start | bytes 196616 | tf_op jit(solution)/shard_map/ppermute | solution.py:72
  38.0 16.7 %collective-permute-start.3 = (bf16[512,128]{1,0:T(8,128)(2,1)S(1)}, bf16[512,128]{1,0:T(8,128)(2,1)S(1)}, u32[]{:S(2)}, u32[]{:S(2)}) collective-permute-start(bf16[512,128]{1,0:T(8,128)(2,1)S(1)} %pad_maximum_fusion.1), channel_id=1, source_target_pairs={{78,0},{0,2},{2,4},{4,6},{6,8},{8,10},{10,12},{12,14},{14,64},{64,... | collective-permute-start | bytes 393224 | tf_op jit(solution)/shard_map/ppermute | solution.py:72
  45.1 9.6 %collective-permute-start.2 = (bf16[768,128]{1,0:T(8,128)(2,1)S(1)}, bf16[768,128]{1,0:T(8,128)(2,1)S(1)}, u32[]{:S(2)}, u32[]{:S(2)}) collective-permute-start(bf16[768,128]{1,0:T(8,128)(2,1)S(1)} %pad_maximum_fusion), channel_id=1, source_target_pairs={{2,0},{4,2},{6,4},{8,6},{10,8},{12,10},{14,12},{64,14},{66,64},{68... | collective-permute-start | bytes 589832 | tf_op jit(solution)/shard_map/ppermute | solution.py:72
  54.7 9.1 %collective-permute-start.4 = (bf16[2048,128]{1,0:T(8,128)(2,1)S(1)}, bf16[2048,128]{1,0:T(8,128)(2,1)S(1)}, u32[]{:S(2)}, u32[]{:S(2)}) collective-permute-start(bf16[2048,128]{1,0:T(8,128)(2,1)S(1)} %constant_dynamic-update-slice_fusion.own_ref), channel_id=1, source_target_pairs={{0,1},{1,0},{2,3},{3,2},{4,5},{5,4},{6,7},{7,6},{8,9},{9,8},{10,11... | collective-permute-start | bytes 1572872 | tf_op jit(solution)/shard_map/ppermute | solution.py:120
  58.6 15.9 %all-to-all-start.1 = ((f32[16,4,128]{2,1,0:T(4,128)}), f32[16,4,128]{2,1,0:T(4,128)S(1)}, u32[]{:S(2)}, u32[]{:S(2)}) async-start(f32[16,4,128]{2,1,0:T(4,128)} %bitcast.5), calls=%async_computation.1 | async-start | bytes 65536 | tf_op jit(solution)/shard_map/all_to_all | solution.py:110
